TPU v7x, 256 devices: a whole 4x4x8 slice. The times are simulated.
256 devices in a mesh: fsdp: 64 (over y, z, core), tp: 4 (over x).
Axes of the slice: x: 4, y: 4, z: 8, core: 2. Of those that a mesh axis runs over, the one named last changes fastest.
Arguments:
- grad_q_up: bfloat16 [1536, 24576], P('tp', 'fsdp'), may hold values from -1 to 1
- grad_kv_down: bfloat16 [576, 7168], P('tp', 'fsdp'), may hold values from -1 to 1
- grad_kv_up: bfloat16 [512, 32768], P('tp', 'fsdp'), may hold values from -1 to 1
Outputs:
- step_q_up: bfloat16 [1536, 24576], P('tp', 'fsdp')
- step_kv_down: bfloat16 [576, 7168], P('tp', 'fsdp')
- step_kv_up: bfloat16 [512, 32768], P('tp', 'fsdp')
All inputs are finite; a program needn't handle non-finite values.
Results may differ from a plain program's by a relative error of at most 0.012.
The roundings to bfloat16 on the way count: a program that leaves them out, or rounds other values in their place, can miss the bound.
Values may be sent and summed in bfloat16 or wider, within the bound.
No kernel may reach another device: no remote copies, remote signals or barrier semaphores. Data moves between devices by JAX's collectives and lax.ppermute only.
A program may use at most 64 MiB of HBM per device.

v0:
```python
import math

import jax
import jax.numpy as jnp
from jax import lax
from jax.sharding import PartitionSpec as P

coef_a = 3.4445
coef_b = -4.775
coef_c = 2.0315


def combine(iterate, first, second, factor):
    mixed = coef_a * iterate.astype(jnp.float32) + coef_b * first + coef_c * second
    return (factor * mixed).astype(jnp.bfloat16)


def shared_gram(partial_value):
    share = lax.psum_scatter(partial_value, "fsdp", scatter_dimension=1, tiled=True).astype(
        jnp.bfloat16
    )
    return lax.all_gather(share, "fsdp", axis=1, tiled=True)


def panels(iterate):
    factor = math.sqrt(iterate.shape[1] * lax.axis_size("fsdp"))
    rows_all = lax.all_gather(iterate, "tp", axis=0, tiled=True)
    partial_value = lax.dot_general(
        iterate, rows_all, (((1,), (1,)), ((), ())), preferred_element_type=jnp.float32
    )
    gram_b = shared_gram(partial_value)
    first = jnp.dot(gram_b, rows_all, preferred_element_type=jnp.float32)
    second = jnp.dot(
        gram_b,
        lax.all_gather(first.astype(jnp.bfloat16), "tp", axis=0, tiled=True),
        preferred_element_type=jnp.float32,
    )
    return combine(iterate, first, second, factor)


def shards(grad_q_up, grad_kv_down, grad_kv_up):
    step_q_up = panels(grad_q_up)
    step_kv_down = panels(grad_kv_down)
    step_kv_up = panels(grad_kv_up)
    return (step_q_up, step_kv_down, step_kv_up)


def solution(mesh):
    placed = (P("tp", "fsdp"), P("tp", "fsdp"), P("tp", "fsdp"))
    return jax.shard_map(
        shards,
        mesh=mesh,
        in_specs=placed,
        out_specs=(P("tp", "fsdp"), P("tp", "fsdp"), P("tp", "fsdp")),
        check_vma=False,
    )
```

profile of v0, /device:TPU:1, one launch (start us, length us, event | category | flops | bytes accessed | tf_op | source)
XLA Modules:
  0.0 653.6 jit_solution(12189652725706866114)
XLA Ops:
  7.2 0.0 all-gather.5.cloned.1.call-start
  7.2 0.7 all-gather.5.cloned.1.call-update
  7.9 0.0 reduce-scatter.4.cloned.1.call-start
  7.9 31.7 %all-gather.5.cloned.1.call-done = bf16[1536,384]{1,0:T(8,128)(2,1)} async-done(((bf16[384,384]{1,0:T(8,128)(2,1)}), bf16[1536,384]{1,0:T(8,128)(2,1)}) %all-gather.5.cloned.1.call-update) | async-done | bytes 1179664 | tf_op jit(solution)/shard_map/all_gather | solution.py:27
  39.6 3.7 fusion.13
  43.3 0.0 reduce-scatter.4.cloned.1.call-update
  43.3 0.0 all-gather.7.cloned.1.call-start
  43.4 134.9 %reduce-scatter.4.cloned.1.call-done = f32[384,24]{0,1:T(8,128)} async-done(((f32[384,1536]{0,1:T(8,128)}), f32[384,24]{0,1:T(8,128)}) %reduce-scatter.4.cloned.1.call-update) | async-done | bytes 36880
  178.3 1.4 convert_element_type.37
  179.7 0.0 all-gather.7.cloned.1.call-update
  179.7 0.0 all-gather.9.cloned.1.call-start
  179.8 9.4 %all_gather.30 = bf16[576,112]{1,0:T(8,128)(2,1)S(1)} all-gather(bf16[144,112]{1,0:T(8,128)(2,1)S(1)} %copy-done.3), channel_id=1, replica_groups=mesh['fsdp'=64,'tp'=4] {'tp'}, dimensions={0}, use_global_device_ids=true | all-gather | bytes 161280 | tf_op jit(solution)/shard_map/all_gather | solution.py:27
  189.2 9.9 %all_gather.33 = bf16[512,512]{1,0:T(8,128)(2,1)S(1)} all-gather(bf16[128,512]{1,0:T(8,128)(2,1)S(1)} %copy-done.1), channel_id=1, replica_groups=mesh['fsdp'=64,'tp'=4] {'tp'}, dimensions={0}, use_global_device_ids=true | all-gather | bytes 655360 | tf_op jit(solution)/shard_map/all_gather | solution.py:27
  199.1 0.3 fusion.15
  199.4 0.0 copy-start.5
  199.4 63.2 %all-gather.7.cloned.1.call-done = bf16[384,1536]{0,1:T(8,128)(2,1)} async-done(((bf16[384,24]{0,1:T(8,128)(2,1)}), bf16[384,1536]{0,1:T(8,128)(2,1)}) %all-gather.7.cloned.1.call-update) | async-done | bytes 1179664 | tf_op jit(solution)/shard_map/all_gather | solution.py:22
  262.6 2.8 fusion.10
  265.4 0.0 all-gather.9.cloned.1.call-update
  265.4 0.2 fusion.14
  265.7 0.6 dynamic-slice
  266.9 252.1 %all-reduce.5 = (bf16[144,576]{0,1:T(8,128)(2,1)S(1)}, bf16[128,512]{0,1:T(8,128)(2,1)S(1)}) all-reduce(f32[144,576]{0,1:T(8,128)S(1)} %fusion.14, f32[128,512]{0,1:T(8,128)S(1)} %fusion.15), channel_id=3, replica_groups=mesh['fsdp'=64,'tp'=4] {'fsdp'}, use_global_device_ids=true, to_apply=%region_1.0.clone | all-reduce | flops 148480 | bytes 890880
  519.1 52.6 %all-gather = bf16[64,9,144]{2,1,0:T(8,128)(2,1)S(1)} all-gather(bf16[1,9,144]{2,1,0:T(8,128)(2,1)S(1)} %fusion.9), channel_id=1, replica_groups=mesh['fsdp'=64,'tp'=4] {'fsdp'}, dimensions={0}, use_global_device_ids=true | all-gather | bytes 168480 | tf_op jit(solution)/shard_map/all_gather | solution.py:22
  571.7 0.2 reshape.7
  572.5 49.5 %all_gather.34 = bf16[128,512]{0,1:T(8,128)(2,1)S(1)} all-gather(bf16[128,8]{0,1:T(8,128)(2,1)S(1)} %dynamic-slice_convert_fusion.1), channel_id=1, replica_groups=mesh['fsdp'=64,'tp'=4] {'fsdp'}, dimensions={1}, use_global_device_ids=true | all-gather | bytes 133120 | tf_op jit(solution)/shard_map/all_gather | solution.py:22
  622.0 0.3 fusion.11
  622.3 9.8 %all_gather.32 = bf16[576,112]{1,0:T(8,128)(2,1)S(1)} all-gather(bf16[144,112]{1,0:T(8,128)(2,1)S(1)} %get-tuple-element.7), channel_id=1, replica_groups=mesh['fsdp'=64,'tp'=4] {'tp'}, dimensions={0}, use_global_device_ids=true | all-gather | bytes 161280 | tf_op jit(solution)/shard_map/all_gather | solution.py:35
  632.1 0.3 fusion.12
  632.4 0.0 copy-start
  632.4 10.0 %all_gather.35 = bf16[512,512]{1,0:T(8,128)(2,1)S(1)} all-gather(bf16[128,512]{1,0:T(8,128)(2,1)S(1)} %get-tuple-element.9), channel_id=1, replica_groups=mesh['fsdp'=64,'tp'=4] {'tp'}, dimensions={0}, use_global_device_ids=true | all-gather | bytes 655360 | tf_op jit(solution)/shard_map/all_gather | solution.py:35
  642.4 0.9 fusion.8
  643.3 0.9 fusion.5
  644.3 2.8 fusion.2
  (13 shorter events, 0.0 us)
Async XLA Ops:
  7.2 32.4 %all-gather.5.cloned.1.call-start = ((), (), s32[]{:S(2)}) async-start(), calls=%async_computation.1 | async-start | bytes 1474560 | tf_op jit(solution)/shard_map/all_gather | solution.py:27
  7.9 170.4 %reduce-scatter.4.cloned.1.call-start = ((), (), s32[]{:S(2)}) async-start(), calls=%async_computation.4 | async-start | bytes 2396160
  43.3 136.5 %copy-start.3 = (bf16[144,112]{1,0:T(8,128)(2,1)S(1)}, bf16[144,112]{1,0:T(8,128)(2,1)}, u32[]{:S(2)}) copy-start(bf16[144,112]{1,0:T(8,128)(2,1)} %param.4) | copy-start | bytes 96772
  43.3 145.9 %copy-start.1 = (bf16[128,512]{1,0:T(8,128)(2,1)S(1)}, bf16[128,512]{1,0:T(8,128)(2,1)}, u32[]{:S(2)}) copy-start(bf16[128,512]{1,0:T(8,128)(2,1)} %param.5) | copy-start | bytes 393220
  43.3 219.3 %copy-start.2 = (bf16[1536,384]{1,0:T(8,128)(2,1)S(1)}, bf16[1536,384]{1,0:T(8,128)(2,1)}, u32[]{:S(2)}) copy-start(bf16[1536,384]{1,0:T(8,128)(2,1)} %all-gather.5.cloned.1.call-done) | copy-start | bytes 3538948
  43.3 219.3 %all-gather.7.cloned.1.call-start = ((), (), s32[]{:S(2)}) async-start(), calls=%async_computation.2 | async-start | bytes 1198080 | tf_op jit(solution)/shard_map/all_gather | solution.py:22
  179.7 464.5 %all-gather.9.cloned.1.call-start = ((), (), s32[]{:S(2)}) async-start(), calls=%async_computation.3 | async-start | bytes 1474560 | tf_op jit(solution)/shard_map/all_gather | solution.py:35
  199.4 66.3 %copy-start.5 = (u32[256]{0:T(256)S(1)}, u32[256]{0:T(256)}, u32[]{:S(2)}) copy-start(u32[256]{0:T(256)} %constant.3) | copy-start | bytes 3076
  632.4 11.9 %copy-start = (bf16[384,384]{1,0:T(8,128)(2,1)S(1)}, bf16[384,384]{1,0:T(8,128)(2,1)}, u32[]{:S(2)}) copy-start(bf16[384,384]{1,0:T(8,128)(2,1)} %param.3) | copy-start | bytes 884740
  632.4 11.9 %copy-start.4 = (bf16[384,1536]{0,1:T(8,128)(2,1)S(1)}, bf16[384,1536]{0,1:T(8,128)(2,1)}, u32[]{:S(2)}) copy-start(bf16[384,1536]{0,1:T(8,128)(2,1)} %all-gather.7.cloned.1.call-done) | copy-start | bytes 3538948
Sparse Core Ops, SparseCore 0:
  9.8 29.7 all-gather.4
  43.7 134.5 reduce-scatter.3
  181.9 80.6 all-gather.6
  265.6 23.2 all-gather.8
where the time goes:
time: 658 us; the launch traced here: 654 us
  blocking collectives  393 us (60%)
  waiting for transfers between devices  231 us (35%)
  between operations  15.2 us (2%)
  matrix products  12.2 us (2%)
    unnamed x1, blocking collectives  252 us
    unnamed x5, waiting for transfers between devices  136 us
    all_gather x2, blocking collectives, shared_gram(): return lax.all_gather(share, 'fsdp', axis=1, tiled=True)  102 us
    all_gather x1, waiting for transfers between devices, shared_gram(): return lax.all_gather(share, 'fsdp', axis=1, tiled=True)  63.2 us
    all_gather x1, waiting for transfers between devices, panels(): rows_all = lax.all_gather(iterate, 'tp', axis=0, tiled=True)  31.7 us
    all_gather x2, blocking collectives, panels(): lax.all_gather(first.astype(jnp.bfloat16), 'tp', axis=0, tiled=True)  19.8 us
    all_gather x2, blocking collectives, panels(): rows_all = lax.all_gather(iterate, 'tp', axis=0, tiled=True)  19.3 us
  transfers between devices with their start and end apart: 4, of which 3 were waited for; matrix products, arithmetic and copies ran while one was open for 1% of the time, Pallas kernels for 0%

commit v1 on v0

v1 whole, which is shorter than its diff:
```python
import functools
import math

import jax
import jax.numpy as jnp
from jax import lax
from jax.experimental import pallas as pl
from jax.experimental.pallas import tpu as pltpu
from jax.sharding import Mesh, PartitionSpec as P

coef_a = 3.4445
coef_b = -4.775
coef_c = 2.0315

bf16 = jnp.bfloat16
f32 = jnp.float32

QR, QC = 384, 384
DR, DC = 144, 112
UR, UC = 128, 512
NX, NY, NZ = 4, 4, 8
Q0, U0, D0 = 0, 1152, 1664
XROWS = 1808
GQ, GU, GD = 0, 4608, 5120
GEND = 5840
GROWS = 6144
HALF = GROWS // 2
PIECE = HALF // NY
SHARD = PIECE // NZ


def vmem(n):
    return [pl.BlockSpec(memory_space=pltpu.VMEM)] * n


def call(kernel, outs, scratch=(), flops=0):
    def run(*args):
        outs_t = tuple(jax.ShapeDtypeStruct(s, d) for s, d in outs)
        moved = sum(a.size * a.dtype.itemsize for a in args) + sum(
            s.size * s.dtype.itemsize for s in outs_t
        )
        return pl.pallas_call(
            kernel,
            out_shape=outs_t,
            in_specs=vmem(len(args)),
            out_specs=tuple(vmem(len(outs))),
            scratch_shapes=list(scratch),
            cost_estimate=pl.CostEstimate(flops=flops, bytes_accessed=moved, transcendentals=0),
            compiler_params=pltpu.CompilerParams(vmem_limit_bytes=40 << 20),
        )(*args)

    return run


def dot_t(a, b):
    return lax.dot_general(a, b, (((1,), (1,)), ((), ())), preferred_element_type=f32)


def dot(a, b):
    return jnp.dot(a, b, preferred_element_type=f32)


def q_of(p):
    return jnp.concatenate([p[Q0 + QR * k : Q0 + QR * (k + 1), :] for k in range(QC // 128)], axis=1)


def u_of(p):
    return jnp.concatenate([p[U0 + UR * k : U0 + UR * (k + 1), :] for k in range(UC // 128)], axis=1)


def d_of(p):
    return p[D0 : D0 + DR, :]


def pack_kernel(q, d, u, o):
    for k in range(QC // 128):
        o[Q0 + QR * k : Q0 + QR * (k + 1), :] = q[:, 128 * k : 128 * (k + 1)]
    for k in range(UC // 128):
        o[U0 + UR * k : U0 + UR * (k + 1), :] = u[:, 128 * k : 128 * (k + 1)]
    o[D0 : D0 + DR, :] = jnp.zeros((DR, 128), bf16)
    o[D0 : D0 + DR, 0:DC] = d[...]


def gram_kernel(p0, p1, p2, p3, keep, send):
    core = lax.axis_index("c")

    def put(low, high, row, value):
        ref = low if row < HALF else high
        at = row % HALF
        ref[at : at + value.shape[0], :] = value.astype(bf16)

    def emit(low, high):
        own = q_of(p0)
        for i, p in enumerate((p0, p1, p2, p3)):
            g = dot_t(own, q_of(p))
            for k in range(3):
                put(low, high, GQ + (3 * i + k) * QR, g[:, 128 * k : 128 * (k + 1)])
        own = u_of(p0)
        for i, p in enumerate((p0, p1, p2, p3)):
            put(low, high, GU + i * UR, dot_t(own, u_of(p)))
        everyone = jnp.concatenate([d_of(p) for p in (p0, p1, p2, p3)], axis=0)
        g = dot_t(d_of(p0), everyone)
        for k in range(4):
            put(low, high, GD + k * DR, g[:, 128 * k : 128 * (k + 1)])
        high[GD + 4 * DR - HALF : GROWS - HALF, :] = jnp.zeros((GROWS - GD - 4 * DR, 128), bf16)
        high[GD + 4 * DR - HALF : GEND - HALF, 0:64] = g[:, 512:576].astype(bf16)

    @pl.when(core == 0)
    def _():
        emit(keep, send)

    @pl.when(core == 1)
    def _():
        emit(send, keep)


def core_sum_kernel(keep, got, *outs):
    y = lax.axis_index("y")
    for i, o in enumerate(outs):
        at = pl.multiple_of(lax.rem(y + i, NY) * PIECE, PIECE)
        rows = pl.ds(at, PIECE)
        o[...] = (keep[rows, :].astype(f32) + got[rows, :].astype(f32)).astype(bf16)


def y_sum_kernel(a, b, c, d, o):
    o[...] = (
        (a[...].astype(f32) + b[...].astype(f32)) + (c[...].astype(f32) + d[...].astype(f32))
    ).astype(bf16)


def z_sum_kernel(a, o):
    total = a[0:SHARD, :].astype(f32)
    for i in range(1, NZ):
        total = total + a[SHARD * i : SHARD * (i + 1), :].astype(f32)
    total = total.astype(bf16)
    for i in range(NZ):
        o[SHARD * i : SHARD * (i + 1), :] = total


def products(gram, blocks):
    acc = None
    for i, p in enumerate(blocks):
        lhs = jnp.concatenate(
            [gram[GQ + (3 * i + k) * QR : GQ + (3 * i + k + 1) * QR, :] for k in range(3)], axis=1
        )
        term = dot(lhs, q_of(p))
        acc = term if acc is None else acc + term
    out_q = acc
    acc = None
    for i, p in enumerate(blocks):
        term = dot(gram[GU + i * UR : GU + (i + 1) * UR, :], u_of(p))
        acc = term if acc is None else acc + term
    out_u = acc
    lhs = jnp.concatenate(
        [gram[GD + k * DR : GD + (k + 1) * DR, :] for k in range(4)]
        + [gram[GD + 4 * DR : GD + 5 * DR, 0:64]],
        axis=1,
    )
    out_d = dot(lhs, jnp.concatenate([d_of(p) for p in blocks], axis=0))
    return out_q, out_d, out_u


def first_kernel(*refs):
    mine, other = refs[0:4], refs[4:8]
    blocks = refs[8:12]
    gram, first_b, acc = refs[12:15]
    y, core = lax.axis_index("y"), lax.axis_index("c")
    for group, which in ((mine, core), (other, 1 - core)):
        for i, piece in enumerate(group):
            at = which * HALF + lax.rem(y + NY - i, NY) * PIECE
            gram[pl.ds(pl.multiple_of(at, PIECE), PIECE), :] = piece[...]
    out_q, out_d, out_u = products(gram, blocks)

    def put(row, value):
        rows = slice(row, row + value.shape[0])
        first_b[rows, :] = value.astype(bf16)
        acc[rows, :] = coef_a * blocks[0][rows, :].astype(f32) + coef_b * value

    for k in range(QC // 128):
        put(Q0 + QR * k, out_q[:, 128 * k : 128 * (k + 1)])
    for k in range(UC // 128):
        put(U0 + UR * k, out_u[:, 128 * k : 128 * (k + 1)])
    put(D0, out_d)


def second_kernel(factors, gram, acc, f0, f1, f2, f3, step_q, step_d, step_u):
    out_q, out_d, out_u = products(gram, (f0, f1, f2, f3))
    fq, fd, fu = factors
    for k in range(QC // 128):
        lanes = slice(128 * k, 128 * (k + 1))
        step_q[:, lanes] = (
            fq * (acc[Q0 + QR * k : Q0 + QR * (k + 1), :] + coef_c * out_q[:, lanes])
        ).astype(bf16)
    for k in range(UC // 128):
        lanes = slice(128 * k, 128 * (k + 1))
        step_u[:, lanes] = (
            fu * (acc[U0 + UR * k : U0 + UR * (k + 1), :] + coef_c * out_u[:, lanes])
        ).astype(bf16)
    whole = (fd * (acc[D0 : D0 + DR, :] + coef_c * out_d)).astype(bf16)
    step_d[...] = whole[:, 0:DC]


def shift(value, axis, size, by):
    return lax.ppermute(value, axis, [(i, (i + by) % size) for i in range(size)])


def from_others(value, axis, size):
    return [value] + [shift(value, axis, size, i) for i in range(1, size)]


def shards(grad_q_up, grad_kv_down, grad_kv_up):
    columns = 64
    factors = tuple(math.sqrt(g.shape[1] * columns) for g in (grad_q_up, grad_kv_down, grad_kv_up))
    flops = 2 * 4 * (QR * QR * QC + UR * UR * UC + DR * DR * 128)
    (packed,) = call(pack_kernel, [((XROWS, 128), bf16)])(grad_q_up, grad_kv_down, grad_kv_up)
    blocks = from_others(packed, "x", NX)
    half = ((HALF, 128), bf16)
    piece = ((PIECE, 128), bf16)
    keep, send = call(gram_kernel, [half, half], flops=flops)(*blocks)
    got = shift(send, "c", 2, 1)
    pieces = call(core_sum_kernel, [piece] * NY)(keep, got)
    pieces = [pieces[0]] + [shift(pieces[i], "y", NY, i) for i in range(1, NY)]
    (total,) = call(y_sum_kernel, [piece])(*pieces)
    total = lax.all_to_all(total, "z", 0, 0, tiled=True)
    (total,) = call(z_sum_kernel, [piece])(total)
    total = lax.all_to_all(total, "z", 0, 0, tiled=True)
    mine = from_others(total, "y", NY)
    other = [shift(m, "c", 2, 1) for m in mine]
    gram, first_b, acc = call(
        first_kernel,
        [((GROWS, 128), bf16), ((XROWS, 128), bf16), ((XROWS, 128), f32)],
        flops=flops,
    )(*mine, *other, *blocks)
    firsts = from_others(first_b, "x", NX)
    return tuple(
        call(
            functools.partial(second_kernel, factors),
            [((QR, QC), bf16), ((DR, DC), bf16), ((UR, UC), bf16)],
            flops=flops,
        )(gram, acc, *firsts)
    )


def solution(mesh):
    fine = Mesh(mesh.devices.reshape(NY, NZ, 2, NX), ("y", "z", "c", "x"))
    placed = P("x", ("y", "z", "c"))
    return jax.shard_map(
        shards,
        mesh=fine,
        in_specs=(placed, placed, placed),
        out_specs=(placed, placed, placed),
        check_vma=False,
    )
```

time: 658 us -> 120 us (0.18)
  blocking collectives: 393 us -> 27.6 us
  waiting for transfers between devices: 231 us -> 57.3 us
  starting transfers between devices: 0.16 us -> 27 us
  between operations: 15.2 us -> 0.68 us
  matrix products: 12.2 us -> 0 us
    unnamed x1 -> x0, blocking collectives: 252 us -> none
    all_gather x6 -> x0, blocking collectives: 141 us -> none  [the longest x2 102 us: shared_gram(): return lax.all_gather(share, 'fsdp', axis=1, tiled=True)]
    unnamed x5 -> x0, waiting for transfers between devices: 136 us -> none
    all_gather x3 -> x0, waiting for transfers between devices: 94.9 us -> none  [the longest x1 63.2 us: shared_gram(): return lax.all_gather(share, 'fsdp', axis=1, tiled=True)]
    ppermute x0 -> x17, waiting for transfers between devices: none -> 57.3 us  [shift(): lax.ppermute(value, axis, [(i, (i + by) % size) for i in range(size)])]
    all_to_all x0 -> x2, blocking collectives: none -> 27.6 us  [shards(): total = lax.all_to_all(total, 'z', 0, 0, tiled=True)]
    ppermute x0 -> x17, starting transfers between devices: none -> 27 us  [shift(): lax.ppermute(value, axis, [(i, (i + by) % size) for i in range(size)])]
    dot_general x9 -> x0, matrix products: 12.2 us -> none  [the longest x3 4.62 us: panels(): jnp.dot(gram_b, lax.all_gather(first.astype(jnp.bfloat16), 'tp', axis=0,...]
  transfers between devices with their start and end apart: 4 -> 17, of which waited for: 3 -> 11; matrix products, arithmetic and copies ran while one was open for 1% -> 0% of each run, Pallas kernels for 0% -> 0%
where the time goes in v1:
time: 120 us
  waiting for transfers between devices  57.3 us (48%)
  blocking collectives  27.6 us (23%)
  starting transfers between devices  27 us (22%)
  Pallas kernels  4.47 us (4%)
  local copies, waits for them, and re-layouts  2.63 us (2%)
    ppermute x17, waiting for transfers between devices, shift(): lax.ppermute(value, axis, [(i, (i + by) % size) for i in range(size)])  57.3 us
    all_to_all x2, blocking collectives, shards(): total = lax.all_to_all(total, 'z', 0, 0, tiled=True)  27.6 us
    ppermute x17, starting transfers between devices, shift(): lax.ppermute(value, axis, [(i, (i + by) % size) for i in range(size)])  27 us
    pallas_call x7, Pallas kernels, run(): pl.pallas_call(kernel, out_shape=outs_t, in_specs=vmem(len(args)), out_sp...  4.47 us
    unnamed x6, local copies, waits for them, and re-layouts  2.63 us
  transfers between devices with their start and end apart: 17, of which 11 were waited for; matrix products, arithmetic and copies ran while one was open for 0% of the time, Pallas kernels for 0%

profile of v1, /device:TPU:1, one launch (start us, length us, event | category | flops | bytes accessed | tf_op | source)
XLA Modules:
  0.0 119.7 jit_solution(3069462390017930656)
XLA Ops:
  0.6 1.0 copy-done
  1.6 0.9 copy-done.1
  2.5 0.8 copy-done.2
  3.4 3.4 %collective-permute-start.2 = (bf16[1808,128]{1,0:T(8,128)(2,1)S(1)}, bf16[1808,128]{1,0:T(8,128)(2,1)S(1)}, u32[]{:S(2)}, u32[]{:S(2)}) collective-permute-start(bf16[1808,128]{1,0:T(8,128)(2,1)S(1)} %shard_map.58.p0.refs_8_), channel_id=1, source_target_pairs={{0,3},{1,0},{2,1},{3,2},{4,7},{5,4},{6,5},{7,6},{8,11},{9,8},{10,9... | collective-permute-start | bytes 1388552 | tf_op jit(solution)/shard_map/ppermute | solution.py:204
  7.3 0.6 collective-permute-start
  7.9 11.2 %collective-permute-done.2.p3.refs_11_ = bf16[1808,128]{1,0:T(8,128)(2,1)S(1)} collective-permute-done((bf16[1808,128]{1,0:T(8,128)(2,1)S(1)}, bf16[1808,128]{1,0:T(8,128)(2,1)S(1)}, u32[]{:S(2)}, u32[]{:S(2)}) %collective-permute-start.2) | collective-permute-done | bytes 462880 | tf_op jit(solution)/shard_map/ppermute | solution.py:204
  19.4 11.2 %collective-permute-done.p1.refs_9_ = bf16[1808,128]{1,0:T(8,128)(2,1)S(1)} collective-permute-done((bf16[1808,128]{1,0:T(8,128)(2,1)S(1)}, bf16[1808,128]{1,0:T(8,128)(2,1)S(1)}, u32[]{:S(2)}, u32[]{:S(2)}) %collective-permute-start) | collective-permute-done | bytes 462880 | tf_op jit(solution)/shard_map/ppermute | solution.py:204
  30.7 1.1 shard_map.59
  31.8 0.6 collective-permute-start.3
  32.4 1.9 %collective-permute-done.3.got = bf16[3072,128]{1,0:T(8,128)(2,1)S(1)} collective-permute-done((bf16[3072,128]{1,0:T(8,128)(2,1)S(1)}, bf16[3072,128]{1,0:T(8,128)(2,1)S(1)}, u32[]{:S(2)}, u32[]{:S(2)}) %collective-permute-start.3) | collective-permute-done | bytes 786464 | tf_op jit(solution)/shard_map/ppermute | solution.py:204
  34.5 1.4 %collective-permute-start.4 = (bf16[768,128]{1,0:T(8,128)(2,1)S(1)}, bf16[768,128]{1,0:T(8,128)(2,1)S(1)}, u32[]{:S(2)}, u32[]{:S(2)}) collective-permute-start(bf16[768,128]{1,0:T(8,128)(2,1)S(1)} %get-tuple-element.15), channel_id=1, source_target_pairs={{0,64},{64,128},{128,192},{192,0},{1,65},{65,129},{129,193},{193,1... | collective-permute-start | bytes 589832 | tf_op jit(solution)/shard_map/ppermute | solution.py:204
  35.9 2.6 %collective-permute-start.5 = (bf16[768,128]{1,0:T(8,128)(2,1)S(1)}, bf16[768,128]{1,0:T(8,128)(2,1)S(1)}, u32[]{:S(2)}, u32[]{:S(2)}) collective-permute-start(bf16[768,128]{1,0:T(8,128)(2,1)S(1)} %get-tuple-element.16), channel_id=1, source_target_pairs={{0,128},{64,192},{128,0},{192,64},{1,129},{65,193},{129,1},{193,65... | collective-permute-start | bytes 589832 | tf_op jit(solution)/shard_map/ppermute | solution.py:204
  38.5 1.1 collective-permute-start.6
  39.6 2.5 %collective-permute-done.4.b = bf16[768,128]{1,0:T(8,128)(2,1)S(1)} collective-permute-done((bf16[768,128]{1,0:T(8,128)(2,1)S(1)}, bf16[768,128]{1,0:T(8,128)(2,1)S(1)}, u32[]{:S(2)}, u32[]{:S(2)}) %collective-permute-start.4) | collective-permute-done | bytes 196640 | tf_op jit(solution)/shard_map/ppermute | solution.py:204
  42.0 5.3 %collective-permute-done.5.c = bf16[768,128]{1,0:T(8,128)(2,1)S(1)} collective-permute-done((bf16[768,128]{1,0:T(8,128)(2,1)S(1)}, bf16[768,128]{1,0:T(8,128)(2,1)S(1)}, u32[]{:S(2)}, u32[]{:S(2)}) %collective-permute-start.5) | collective-permute-done | bytes 196640 | tf_op jit(solution)/shard_map/ppermute | solution.py:204
  47.5 16.5 %all_to_all.22 = bf16[8,96,128]{2,1,0:T(8,128)(2,1)S(1)} all-to-all(bf16[8,96,128]{2,1,0:T(8,128)(2,1)S(1)} %bitcast.6), channel_id=1, replica_groups=mesh['y'=4,'z'=8,'c'=2,'x'=4] {'z'}, dimensions={0} | all-to-all | bytes 393216 | tf_op jit(solution)/shard_map/all_to_all | solution.py:224
  63.9 11.1 %all_to_all.23 = bf16[8,96,128]{2,1,0:T(8,128)(2,1)S(1)} all-to-all(bf16[8,96,128]{2,1,0:T(8,128)(2,1)S(1)} %bitcast.5), channel_id=1, replica_groups=mesh['y'=4,'z'=8,'c'=2,'x'=4] {'z'}, dimensions={0} | all-to-all | bytes 393216 | tf_op jit(solution)/shard_map/all_to_all | solution.py:226
  75.1 3.5 %collective-permute-start.9 = (bf16[768,128]{1,0:T(8,128)(2,1)S(1)}, bf16[768,128]{1,0:T(8,128)(2,1)S(1)}, u32[]{:S(2)}, u32[]{:S(2)}) collective-permute-start(bf16[768,128]{1,0:T(8,128)(2,1)S(1)} %bitcast.7), channel_id=1, source_target_pairs={{0,192},{64,0},{128,64},{192,128},{1,193},{65,1},{129,65},{193,129... | collective-permute-start | bytes 589832 | tf_op jit(solution)/shard_map/ppermute | solution.py:204
  78.6 0.6 collective-permute-start.7
  79.1 3.8 %collective-permute-start.10 = (bf16[768,128]{1,0:T(8,128)(2,1)S(1)}, bf16[768,128]{1,0:T(8,128)(2,1)S(1)}, u32[]{:S(2)}, u32[]{:S(2)}) collective-permute-start(bf16[768,128]{1,0:T(8,128)(2,1)S(1)} %bitcast.10), channel_id=1, source_target_pairs={{0,4},{4,0},{1,5},{5,1},{2,6},{6,2},{3,7},{7,3},{8,12},{12,8},{9,1... | collective-permute-start | bytes 589832 | tf_op jit(solution)/shard_map/ppermute | solution.py:204
  82.9 0.9 collective-permute-done.9.refs_3_
  83.8 4.1 %collective-permute-start.13 = (bf16[768,128]{1,0:T(8,128)(2,1)S(1)}, bf16[768,128]{1,0:T(8,128)(2,1)S(1)}, u32[]{:S(2)}, u32[]{:S(2)}) collective-permute-start(bf16[768,128]{1,0:T(8,128)(2,1)S(1)} %collective-permute-done.9.refs_3_), channel_id=1, source_target_pairs={{0,4},{4,0},{1,5},{5,1},{2,6},{6,2},{3,7},{7,3},{8,12},{12,8},{9,1... | collective-permute-start | bytes 589832 | tf_op jit(solution)/shard_map/ppermute | solution.py:204
  87.9 1.7 %collective-permute-start.12 = (bf16[768,128]{1,0:T(8,128)(2,1)S(1)}, bf16[768,128]{1,0:T(8,128)(2,1)S(1)}, u32[]{:S(2)}, u32[]{:S(2)}) collective-permute-start(bf16[768,128]{1,0:T(8,128)(2,1)S(1)} %collective-permute-done.8.refs_2_), channel_id=1, source_target_pairs={{0,4},{4,0},{1,5},{5,1},{2,6},{6,2},{3,7},{7,3},{8,12},{12,8},{9,1... | collective-permute-start | bytes 589832 | tf_op jit(solution)/shard_map/ppermute | solution.py:204
  89.6 1.7 %collective-permute-start.11 = (bf16[768,128]{1,0:T(8,128)(2,1)S(1)}, bf16[768,128]{1,0:T(8,128)(2,1)S(1)}, u32[]{:S(2)}, u32[]{:S(2)}) collective-permute-start(bf16[768,128]{1,0:T(8,128)(2,1)S(1)} %collective-permute-done.7.refs_1_), channel_id=1, source_target_pairs={{0,4},{4,0},{1,5},{5,1},{2,6},{6,2},{3,7},{7,3},{8,12},{12,8},{9,1... | collective-permute-start | bytes 589832 | tf_op jit(solution)/shard_map/ppermute | solution.py:204
  91.3 1.1 collective-permute-done.11.refs_5_
  92.4 1.2 shard_map.63
  94.0 0.5 collective-permute-start.15
  94.5 0.6 collective-permute-start.14
  95.1 10.4 %collective-permute-done.16.f3 = bf16[1808,128]{1,0:T(8,128)(2,1)S(1)} collective-permute-done((bf16[1808,128]{1,0:T(8,128)(2,1)S(1)}, bf16[1808,128]{1,0:T(8,128)(2,1)S(1)}, u32[]{:S(2)}, u32[]{:S(2)}) %collective-permute-start.16) | collective-permute-done | bytes 462880 | tf_op jit(solution)/shard_map/ppermute | solution.py:204
  105.5 1.5 %collective-permute-done.15.f2 = bf16[1808,128]{1,0:T(8,128)(2,1)S(1)} collective-permute-done((bf16[1808,128]{1,0:T(8,128)(2,1)S(1)}, bf16[1808,128]{1,0:T(8,128)(2,1)S(1)}, u32[]{:S(2)}, u32[]{:S(2)}) %collective-permute-start.15) | collective-permute-done | bytes 462880 | tf_op jit(solution)/shard_map/ppermute | solution.py:204
  107.0 10.9 %collective-permute-done.14.f1 = bf16[1808,128]{1,0:T(8,128)(2,1)S(1)} collective-permute-done((bf16[1808,128]{1,0:T(8,128)(2,1)S(1)}, bf16[1808,128]{1,0:T(8,128)(2,1)S(1)}, u32[]{:S(2)}, u32[]{:S(2)}) %collective-permute-start.14) | collective-permute-done | bytes 462880 | tf_op jit(solution)/shard_map/ppermute | solution.py:204
  117.9 1.8 %shard_map.64 = (bf16[384,384]{1,0:T(8,128)(2,1)}, bf16[144,112]{1,0:T(8,128)(2,1)}, bf16[128,512]{1,0:T(8,128)(2,1)}) custom-call(bf16[6144,128]{1,0:T(8,128)(2,1)S(1)} %get-tuple-element.18.gram, f32[1808,128]{1,0:T(8,128)S(1)} %get-tuple-element.19.acc, bf16[1808,128]{1,0:T(8,128)(2,1)S(1)} %get-tuple-element.20.f0, ...), custom_call_target="tpu_custom_call" | custom-call | flops 541327360 | bytes 4808192 | tf_op jit(solution)/shard_map/pallas_call | solution.py:42
  (17 shorter events, 1.7 us)
Async XLA Ops:
  0.6 1.0 copy-start
  1.6 0.9 copy-start.1
  2.5 0.8 copy-start.2
  3.4 15.7 %collective-permute-start.2 = (bf16[1808,128]{1,0:T(8,128)(2,1)S(1)}, bf16[1808,128]{1,0:T(8,128)(2,1)S(1)}, u32[]{:S(2)}, u32[]{:S(2)}) collective-permute-start(bf16[1808,128]{1,0:T(8,128)(2,1)S(1)} %shard_map.58.p0.refs_8_), channel_id=1, source_target_pairs={{0,3},{1,0},{2,1},{3,2},{4,7},{5,4},{6,5},{7,6},{8,11},{9,8},{10,9... | collective-permute-start | bytes 1388552 | tf_op jit(solution)/shard_map/ppermute | solution.py:204
  6.7 12.7 %collective-permute-start.1 = (bf16[1808,128]{1,0:T(8,128)(2,1)S(1)}, bf16[1808,128]{1,0:T(8,128)(2,1)S(1)}, u32[]{:S(2)}, u32[]{:S(2)}) collective-permute-start(bf16[1808,128]{1,0:T(8,128)(2,1)S(1)} %shard_map.58.p0.refs_8_), channel_id=1, source_target_pairs={{0,2},{1,3},{2,0},{3,1},{4,6},{5,7},{6,4},{7,5},{8,10},{9,11},{10,... | collective-permute-start | bytes 1388552 | tf_op jit(solution)/shard_map/ppermute | solution.py:204
  7.3 23.4 %collective-permute-start = (bf16[1808,128]{1,0:T(8,128)(2,1)S(1)}, bf16[1808,128]{1,0:T(8,128)(2,1)S(1)}, u32[]{:S(2)}, u32[]{:S(2)}) collective-permute-start(bf16[1808,128]{1,0:T(8,128)(2,1)S(1)} %shard_map.58.p0.refs_8_), channel_id=1, source_target_pairs={{0,1},{1,2},{2,3},{3,0},{4,5},{5,6},{6,7},{7,4},{8,9},{9,10},{10,1... | collective-permute-start | bytes 1388552 | tf_op jit(solution)/shard_map/ppermute | solution.py:204
  31.8 2.5 %collective-permute-start.3 = (bf16[3072,128]{1,0:T(8,128)(2,1)S(1)}, bf16[3072,128]{1,0:T(8,128)(2,1)S(1)}, u32[]{:S(2)}, u32[]{:S(2)}) collective-permute-start(bf16[3072,128]{1,0:T(8,128)(2,1)S(1)} %get-tuple-element.13), channel_id=1, source_target_pairs={{0,4},{4,0},{1,5},{5,1},{2,6},{6,2},{3,7},{7,3},{8,12},{12,8},{9,1... | collective-permute-start | bytes 2359304 | tf_op jit(solution)/shard_map/ppermute | solution.py:204
  34.5 7.5 %collective-permute-start.4 = (bf16[768,128]{1,0:T(8,128)(2,1)S(1)}, bf16[768,128]{1,0:T(8,128)(2,1)S(1)}, u32[]{:S(2)}, u32[]{:S(2)}) collective-permute-start(bf16[768,128]{1,0:T(8,128)(2,1)S(1)} %get-tuple-element.15), channel_id=1, source_target_pairs={{0,64},{64,128},{128,192},{192,0},{1,65},{65,129},{129,193},{193,1... | collective-permute-start | bytes 589832 | tf_op jit(solution)/shard_map/ppermute | solution.py:204
  35.9 11.5 %collective-permute-start.5 = (bf16[768,128]{1,0:T(8,128)(2,1)S(1)}, bf16[768,128]{1,0:T(8,128)(2,1)S(1)}, u32[]{:S(2)}, u32[]{:S(2)}) collective-permute-start(bf16[768,128]{1,0:T(8,128)(2,1)S(1)} %get-tuple-element.16), channel_id=1, source_target_pairs={{0,128},{64,192},{128,0},{192,64},{1,129},{65,193},{129,1},{193,65... | collective-permute-start | bytes 589832 | tf_op jit(solution)/shard_map/ppermute | solution.py:204
  38.5 8.9 %collective-permute-start.6 = (bf16[768,128]{1,0:T(8,128)(2,1)S(1)}, bf16[768,128]{1,0:T(8,128)(2,1)S(1)}, u32[]{:S(2)}, u32[]{:S(2)}) collective-permute-start(bf16[768,128]{1,0:T(8,128)(2,1)S(1)} %get-tuple-element.17), channel_id=1, source_target_pairs={{0,192},{64,0},{128,64},{192,128},{1,193},{65,1},{129,65},{193,129... | collective-permute-start | bytes 589832 | tf_op jit(solution)/shard_map/ppermute | solution.py:204
  75.1 8.8 %collective-permute-start.9 = (bf16[768,128]{1,0:T(8,128)(2,1)S(1)}, bf16[768,128]{1,0:T(8,128)(2,1)S(1)}, u32[]{:S(2)}, u32[]{:S(2)}) collective-permute-start(bf16[768,128]{1,0:T(8,128)(2,1)S(1)} %bitcast.7), channel_id=1, source_target_pairs={{0,192},{64,0},{128,64},{192,128},{1,193},{65,1},{129,65},{193,129... | collective-permute-start | bytes 589832 | tf_op jit(solution)/shard_map/ppermute | solution.py:204
  78.6 9.3 %collective-permute-start.8 = (bf16[768,128]{1,0:T(8,128)(2,1)S(1)}, bf16[768,128]{1,0:T(8,128)(2,1)S(1)}, u32[]{:S(2)}, u32[]{:S(2)}) collective-permute-start(bf16[768,128]{1,0:T(8,128)(2,1)S(1)} %bitcast.8), channel_id=1, source_target_pairs={{0,128},{64,192},{128,0},{192,64},{1,129},{65,193},{129,1},{193,65... | collective-permute-start | bytes 589832 | tf_op jit(solution)/shard_map/ppermute | solution.py:204
  78.6 11.1 %collective-permute-start.7 = (bf16[768,128]{1,0:T(8,128)(2,1)S(1)}, bf16[768,128]{1,0:T(8,128)(2,1)S(1)}, u32[]{:S(2)}, u32[]{:S(2)}) collective-permute-start(bf16[768,128]{1,0:T(8,128)(2,1)S(1)} %bitcast.9), channel_id=1, source_target_pairs={{0,64},{64,128},{128,192},{192,0},{1,65},{65,129},{129,193},{193,1... | collective-permute-start | bytes 589832 | tf_op jit(solution)/shard_map/ppermute | solution.py:204
  79.1 12.2 %collective-permute-start.10 = (bf16[768,128]{1,0:T(8,128)(2,1)S(1)}, bf16[768,128]{1,0:T(8,128)(2,1)S(1)}, u32[]{:S(2)}, u32[]{:S(2)}) collective-permute-start(bf16[768,128]{1,0:T(8,128)(2,1)S(1)} %bitcast.10), channel_id=1, source_target_pairs={{0,4},{4,0},{1,5},{5,1},{2,6},{6,2},{3,7},{7,3},{8,12},{12,8},{9,1... | collective-permute-start | bytes 589832 | tf_op jit(solution)/shard_map/ppermute | solution.py:204
  83.8 7.5 %collective-permute-start.13 = (bf16[768,128]{1,0:T(8,128)(2,1)S(1)}, bf16[768,128]{1,0:T(8,128)(2,1)S(1)}, u32[]{:S(2)}, u32[]{:S(2)}) collective-permute-start(bf16[768,128]{1,0:T(8,128)(2,1)S(1)} %collective-permute-done.9.refs_3_), channel_id=1, source_target_pairs={{0,4},{4,0},{1,5},{5,1},{2,6},{6,2},{3,7},{7,3},{8,12},{12,8},{9,1... | collective-permute-start | bytes 589832 | tf_op jit(solution)/shard_map/ppermute | solution.py:204
  87.9 3.4 %collective-permute-start.12 = (bf16[768,128]{1,0:T(8,128)(2,1)S(1)}, bf16[768,128]{1,0:T(8,128)(2,1)S(1)}, u32[]{:S(2)}, u32[]{:S(2)}) collective-permute-start(bf16[768,128]{1,0:T(8,128)(2,1)S(1)} %collective-permute-done.8.refs_2_), channel_id=1, source_target_pairs={{0,4},{4,0},{1,5},{5,1},{2,6},{6,2},{3,7},{7,3},{8,12},{12,8},{9,1... | collective-permute-start | bytes 589832 | tf_op jit(solution)/shard_map/ppermute | solution.py:204
  89.6 2.8 %collective-permute-start.11 = (bf16[768,128]{1,0:T(8,128)(2,1)S(1)}, bf16[768,128]{1,0:T(8,128)(2,1)S(1)}, u32[]{:S(2)}, u32[]{:S(2)}) collective-permute-start(bf16[768,128]{1,0:T(8,128)(2,1)S(1)} %collective-permute-done.7.refs_1_), channel_id=1, source_target_pairs={{0,4},{4,0},{1,5},{5,1},{2,6},{6,2},{3,7},{7,3},{8,12},{12,8},{9,1... | collective-permute-start | bytes 589832 | tf_op jit(solution)/shard_map/ppermute | solution.py:204
  93.6 11.9 %collective-permute-start.16 = (bf16[1808,128]{1,0:T(8,128)(2,1)S(1)}, bf16[1808,128]{1,0:T(8,128)(2,1)S(1)}, u32[]{:S(2)}, u32[]{:S(2)}) collective-permute-start(bf16[1808,128]{1,0:T(8,128)(2,1)S(1)} %get-tuple-element.20.f0), channel_id=1, source_target_pairs={{0,3},{1,0},{2,1},{3,2},{4,7},{5,4},{6,5},{7,6},{8,11},{9,8},{10,9... | collective-permute-start | bytes 1388552 | tf_op jit(solution)/shard_map/ppermute | solution.py:204
  94.0 13.0 %collective-permute-start.15 = (bf16[1808,128]{1,0:T(8,128)(2,1)S(1)}, bf16[1808,128]{1,0:T(8,128)(2,1)S(1)}, u32[]{:S(2)}, u32[]{:S(2)}) collective-permute-start(bf16[1808,128]{1,0:T(8,128)(2,1)S(1)} %get-tuple-element.20.f0), channel_id=1, source_target_pairs={{0,2},{1,3},{2,0},{3,1},{4,6},{5,7},{6,4},{7,5},{8,10},{9,11},{10,... | collective-permute-start | bytes 1388552 | tf_op jit(solution)/shard_map/ppermute | solution.py:204
  94.5 23.4 %collective-permute-start.14 = (bf16[1808,128]{1,0:T(8,128)(2,1)S(1)}, bf16[1808,128]{1,0:T(8,128)(2,1)S(1)}, u32[]{:S(2)}, u32[]{:S(2)}) collective-permute-start(bf16[1808,128]{1,0:T(8,128)(2,1)S(1)} %get-tuple-element.20.f0), channel_id=1, source_target_pairs={{0,1},{1,2},{2,3},{3,0},{4,5},{5,6},{6,7},{7,4},{8,9},{9,10},{10,1... | collective-permute-start | bytes 1388552 | tf_op jit(solution)/shard_map/ppermute | solution.py:204

commit v2 on v0

v2 whole, which is shorter than its diff:
```python
import functools
import math

import jax
import jax.numpy as jnp
from jax import lax
from jax.experimental import pallas as pl
from jax.experimental.pallas import tpu as pltpu
from jax.sharding import Mesh, PartitionSpec as P

coef_a = 3.4445
coef_b = -4.775
coef_c = 2.0315

bf16 = jnp.bfloat16
f32 = jnp.float32

QR, QC = 384, 384
DR, DC = 144, 112
UR, UC = 128, 512
QH = QR // 2
NX, NY, NZ = 4, 4, 8
NP = 2 * NY

X1 = 2 * QR + DR
XROWS = X1 + QR + UR * (UC // 128)
F1 = 3 * QH + 4 * UR
FCUT = 3 * QH + 3 * UR

A1, A2, B1, B2 = 272, 288, 96, 112
PA, PB = A1 + A2, B1 + B2
G1, G2 = A1 + B1, A2 + B2
PIECE = PA + PB
SHARD = PIECE // NZ
A_AT = 0
B1_AT, B2_AT = A1 * NP, A2 * NP


def vmem(n):
    return [pl.BlockSpec(memory_space=pltpu.VMEM)] * n


def call(kernel, outs, flops=0, scratch=(), hbm=(), after=(), limit=40):
    def run(*args):
        n = len(args)
        args = (*args, *after)
        outs_t = tuple(jax.ShapeDtypeStruct(s, d) for s, d in outs)
        moved = sum(a.size * a.dtype.itemsize for a in args) + sum(
            s.size * s.dtype.itemsize for s in outs_t
        )
        return pl.pallas_call(
            skip(kernel, n, len(after)),
            out_shape=outs_t,
            in_specs=[
                pl.BlockSpec(memory_space=pl.ANY if i in hbm or i >= n else pltpu.VMEM)
                for i in range(len(args))
            ],
            out_specs=tuple(vmem(len(outs))),
            scratch_shapes=list(scratch),
            cost_estimate=pl.CostEstimate(flops=flops, bytes_accessed=moved, transcendentals=0),
            compiler_params=pltpu.CompilerParams(vmem_limit_bytes=limit << 20),
        )(*args)

    return run


def skip(kernel, n, extra):
    return lambda *refs: kernel(*refs[:n], *refs[n + extra :])


def dot_t(a, b):
    return lax.dot_general(a, b, (((1,), (1,)), ((), ())), preferred_element_type=f32)


def dot(a, b):
    return jnp.dot(a, b, preferred_element_type=f32)


def lanes(parts):
    return jnp.concatenate(parts, axis=1)


def rows(parts):
    return jnp.concatenate(parts, axis=0)


def rows_of(block, lo, n):
    cut, parts = block
    if lo < cut:
        return parts[0][lo : lo + n, :]
    return parts[1][lo - cut : lo - cut + n, :]


def x_q(p):
    return lanes([rows_of(p, at, QR) for at in (0, QR, X1)])


def x_d(p):
    return rows_of(p, 2 * QR, DR)


def x_u(p):
    return lanes([rows_of(p, X1 + QR + UR * k, UR) for k in range(4)])


def f_q(p):
    return rows([lanes([rows_of(p, at + QH * k, QH) for k in range(3)]) for at in (0, F1)])


def f_d(p):
    return rows_of(p, F1 + 3 * QH, DR)


def f_u(p):
    return lanes([rows_of(p, 3 * QH + UR * k, UR) for k in range(4)])


def blocks_of(refs, cut):
    out = [(XROWS, (r,)) for r in refs[0:3]]
    return out + ([(cut, tuple(refs[3:5]))] if len(refs) == 5 else [])


def padded(parts, to):
    return rows(parts + [jnp.zeros((to - sum(p.shape[0] for p in parts), 128), bf16)])


def pack_kernel(q, d, u, o, held, sems):
    moves = [(d, held)]
    for k in range(2):
        moves.append((q.at[:, 128 * k : 128 * (k + 1)], o.at[QR * k : QR * (k + 1), :]))
    moves.append((q.at[:, 256:384], o.at[X1 : X1 + QR, :]))
    for k in range(4):
        at = slice(X1 + QR + UR * k, X1 + QR + UR * (k + 1))
        moves.append((u.at[:, 128 * k : 128 * (k + 1)], o.at[at, :]))
    copies = [pltpu.make_async_copy(a, b, sems.at[i]) for i, (a, b) in enumerate(moves)]
    for copy in copies:
        copy.start()
    copies[0].wait()
    o[2 * QR : X1, :] = jnp.zeros((DR, 128), bf16)
    o[2 * QR : X1, 0:DC] = held[...]
    for copy in copies[1:]:
        copy.wait()


def gram_kernel(*refs):
    every = blocks_of(refs[0:5], X1)
    own = every[0]
    keep, send = refs[5:7]
    core = lax.axis_index("c")

    def emit(low, high):
        def put(size, base, at, value):
            value = value.astype(bf16)
            done, n = 0, value.shape[0]
            while done < n:
                piece, off = divmod(at + done, size)
                m = min(n - done, size - off)
                ref = low if piece < NY else high
                to = (piece % NY) * PIECE + base + off
                ref[to : to + m, :] = value[done : done + m, :]
                done += m

        for blocks, upper, lower, base1, base2 in (
            (every[0:3], A1, A2, 0, G1),
            (every[3:4], B1, B2, A1, G1 + A2),
        ):
            count = len(blocks)
            mine = x_q(own)
            for i, p in enumerate(blocks):
                g = dot_t(mine, x_q(p))
                for k in range(3):
                    at = (3 * i + k) * QH
                    put(upper, base1, at, g[0:QH, 128 * k : 128 * (k + 1)])
                    put(lower, base2, at, g[QH:QR, 128 * k : 128 * (k + 1)])
            at = 3 * count * QH
            mine = x_u(own)
            for i, p in enumerate(blocks):
                put(upper, base1, at + UR * i, dot_t(mine, x_u(p)))
            end = at + UR * count
            if upper * NP > end:
                put(upper, base1, end, jnp.zeros((upper * NP - end, 128), f32))
            g = dot_t(x_d(own), padded([x_d(p) for p in blocks], 128 * (count + 1)))
            for k in range(count + 1):
                put(lower, base2, at + DR * k, g[:, 128 * k : 128 * (k + 1)])
            end = at + DR * (count + 1)
            if lower * NP > end:
                put(lower, base2, end, jnp.zeros((lower * NP - end, 128), f32))

    @pl.when(core == 0)
    def _():
        emit(keep, send)

    @pl.when(core == 1)
    def _():
        emit(send, keep)


def core_sum_kernel(keep, got, *outs):
    y = lax.axis_index("y")
    n = outs[0].shape[0]
    for i, o in enumerate(outs):
        at = pl.ds(pl.multiple_of(lax.rem(y + i, NY) * n, 16), n)
        o[...] = (keep[at, :].astype(f32) + got[at, :].astype(f32)).astype(bf16)


def y_sum_kernel(a, b, c, d, o):
    o[...] = (
        (a[...].astype(f32) + b[...].astype(f32)) + (c[...].astype(f32) + d[...].astype(f32))
    ).astype(bf16)


def z_sum_kernel(a, o):
    total = a[0:SHARD, :].astype(f32)
    for i in range(1, NZ):
        total = total + a[SHARD * i : SHARD * (i + 1), :].astype(f32)
    total = total.astype(bf16)
    for i in range(NZ):
        o[SHARD * i : SHARD * (i + 1), :] = total


def q_product(gram, b_at, q):
    out = None
    for i in range(4):
        base = b_at if i == 3 else 3 * i * QH
        lhs = lanes([gram[base + QH * k : base + QH * (k + 1), :] for k in range(3)])
        term = dot(lhs, q[i])
        out = term if out is None else out + term
    return out


def u_product(gram, blocks, u_of):
    out = None
    for i, p in enumerate(blocks):
        at = (B1_AT + 3 * QH) if i == 3 else 9 * QH + UR * i
        term = dot(gram[at : at + UR, :], u_of(p))
        out = term if out is None else out + term
    return out


def d_product(gram, blocks, d_of):
    lhs_a = lanes([gram[9 * QH + DR * k : 9 * QH + DR * (k + 1), :] for k in range(4)])
    at = B2_AT + 3 * QH
    lhs_b = lanes([gram[at + DR * k : at + DR * (k + 1), :] for k in range(2)])
    rhs_a = padded([d_of(p) for p in blocks[0:3]], 512)
    return dot(lhs_a, rhs_a) + dot(lhs_b, padded([d_of(blocks[3])], 256))


def unpack_gram(gram1, gram2, mine, other):
    y, core = lax.axis_index("y"), lax.axis_index("c")
    for group, which in ((mine, core), (other, 1 - core)):
        for i, piece in enumerate(group):
            p = which * NY + lax.rem(y + NY - i, NY)
            for gram, base, size, at in (
                (gram1, 0, A1, 0),
                (gram1, B1_AT, B1, A1),
                (gram2, 0, A2, G1),
                (gram2, B2_AT, B2, G1 + A2),
            ):
                to = pl.multiple_of(base + p * size, 16)
                gram[pl.ds(to, size), :] = piece[at : at + size, :]


def first_kernel(*refs):
    blocks = blocks_of(refs[8:13], X1)
    gram1, gram2, first_b, acc = refs[13:17]
    unpack_gram(gram1, gram2, refs[0:4], refs[4:8])

    def put(at, x, value):
        to = slice(at, at + value.shape[0])
        first_b[to, :] = value.astype(bf16)
        acc[to, :] = coef_a * x.astype(f32) + coef_b * value

    q = [x_q(p) for p in blocks]
    for h, (gram, b_at, base) in enumerate(((gram1, B1_AT, 0), (gram2, B2_AT, F1))):
        out = q_product(gram, b_at, q)
        for k in range(3):
            at = slice(128 * k, 128 * (k + 1))
            put(base + QH * k, q[0][QH * h : QH * (h + 1), at], out[:, at])
    out = u_product(gram1, blocks, x_u)
    x = x_u(blocks[0])
    for k in range(4):
        at = slice(128 * k, 128 * (k + 1))
        put(3 * QH + UR * k, x[:, at], out[:, at])
    put(F1 + 3 * QH, x_d(blocks[0]), d_product(gram2, blocks, x_d))


def second_kernel(factors, gram1, gram2, acc, *refs):
    blocks = blocks_of(refs[0:5], FCUT)
    step_q, step_d, step_u = refs[5:8]
    fq, fd, fu = factors
    q = [f_q(p) for p in blocks]
    for h, (gram, b_at, base) in enumerate(((gram1, B1_AT, 0), (gram2, B2_AT, F1))):
        out = q_product(gram, b_at, q)
        for k in range(3):
            at = slice(128 * k, 128 * (k + 1))
            rest = acc[base + QH * k : base + QH * (k + 1), :]
            step_q[QH * h : QH * (h + 1), at] = (fq * (rest + coef_c * out[:, at])).astype(bf16)
    out = u_product(gram1, blocks, f_u)
    for k in range(4):
        at = slice(128 * k, 128 * (k + 1))
        base = 3 * QH + UR * k
        step_u[:, at] = (fu * (acc[base : base + UR, :] + coef_c * out[:, at])).astype(bf16)
    out = d_product(gram2, blocks, f_d)
    base = F1 + 3 * QH
    step_d[...] = (fd * (acc[base : base + DR, :] + coef_c * out)).astype(bf16)[:, 0:DC]


def shift(value, axis, size, by):
    return lax.ppermute(value, axis, [(i, (i + by) % size) for i in range(size)])


def ring(own, cut):
    left, right = shift(own, "x", NX, 1), shift(own, "x", NX, -1)
    return [own, left, right, shift(left[0:cut], "x", NX, 1), shift(right[cut:], "x", NX, -1)]


def sum_y(keep, send, n):
    got = shift(send, "c", 2, 1)
    pieces = call(core_sum_kernel, [((n, 128), bf16)] * NY)(keep, got)
    return [pieces[0]] + [shift(pieces[i], "y", NY, i) for i in range(1, NY)]


def gather_y(part):
    mine = [part] + [shift(part, "y", NY, i) for i in range(1, NY)]
    return mine + [shift(m, "c", 2, 1) for m in mine]


def shards(grad_q_up, grad_kv_down, grad_kv_up):
    columns = NP * NZ
    factors = tuple(math.sqrt(g.shape[1] * columns) for g in (grad_q_up, grad_kv_down, grad_kv_up))
    flops = 2 * 4 * (QR * QR * QC + UR * UR * UC + DR * DR * 128)
    (packed,) = call(
        pack_kernel,
        [((XROWS, 128), bf16)],
        scratch=[pltpu.VMEM((DR, DC), bf16), pltpu.SemaphoreType.DMA((8,))],
        hbm=(0, 1, 2),
        limit=60,
    )(grad_q_up, grad_kv_down, grad_kv_up)
    x = ring(packed, X1)
    keep, send = call(gram_kernel, [((NY * PIECE, 128), bf16)] * 2, flops)(*x)
    (total,) = call(y_sum_kernel, [((PIECE, 128), bf16)])(*sum_y(keep, send, PIECE))
    total = lax.all_to_all(total, "z", 0, 0, tiled=True)
    (total,) = call(z_sum_kernel, [((PIECE, 128), bf16)])(total)
    total = lax.all_to_all(total, "z", 0, 0, tiled=True)
    gram1, gram2, first_b, acc = call(
        first_kernel,
        [
            ((NP * G1, 128), bf16),
            ((NP * G2, 128), bf16),
            ((XROWS, 128), bf16),
            ((XROWS, 128), f32),
        ],
        flops,
    )(*gather_y(total), *x)
    return tuple(
        call(
            functools.partial(second_kernel, factors),
            [((QR, QC), bf16), ((DR, DC), bf16), ((UR, UC), bf16)],
            flops,
        )(gram1, gram2, acc, *ring(first_b, FCUT))
    )


def solution(mesh):
    fine = Mesh(mesh.devices.reshape(NY, NZ, 2, NX), ("y", "z", "c", "x"))
    placed = P("x", ("y", "z", "c"))
    return jax.shard_map(
        shards,
        mesh=fine,
        in_specs=(placed, placed, placed),
        out_specs=(placed, placed, placed),
        check_vma=False,
    )
```

time: 658 us -> 111 us (0.17)
  blocking collectives: 393 us -> 27.6 us
  waiting for transfers between devices: 231 us -> 38.2 us
  starting transfers between devices: 0.16 us -> 37.8 us
  between operations: 15.2 us -> 0.73 us
  matrix products: 12.2 us -> 0 us
    unnamed x1 -> x0, blocking collectives: 252 us -> none
    all_gather x6 -> x0, blocking collectives: 141 us -> none  [the longest x2 102 us: shared_gram(): return lax.all_gather(share, 'fsdp', axis=1, tiled=True)]
    unnamed x5 -> x0, waiting for transfers between devices: 136 us -> none
    all_gather x3 -> x0, waiting for transfers between devices: 94.9 us -> none  [the longest x1 63.2 us: shared_gram(): return lax.all_gather(share, 'fsdp', axis=1, tiled=True)]
    ppermute x0 -> x19, waiting for transfers between devices: none -> 38.2 us  [shift(): lax.ppermute(value, axis, [(i, (i + by) % size) for i in range(size)])]
    ppermute x0 -> x19, starting transfers between devices: none -> 37.8 us  [shift(): lax.ppermute(value, axis, [(i, (i + by) % size) for i in range(size)])]
    all_to_all x0 -> x2, blocking collectives: none -> 27.6 us  [shards(): total = lax.all_to_all(total, 'z', 0, 0, tiled=True)]
    dot_general x9 -> x0, matrix products: 12.2 us -> none  [the longest x3 4.62 us: panels(): jnp.dot(gram_b, lax.all_gather(first.astype(jnp.bfloat16), 'tp', axis=0,...]
  transfers between devices with their start and end apart: 4 -> 19, of which waited for: 3 -> 10; matrix products, arithmetic and copies ran while one was open for 1% -> 0% of each run, Pallas kernels for 0% -> 0%
where the time goes in v2:
time: 111 us
  waiting for transfers between devices  38.2 us (34%)
  starting transfers between devices  37.8 us (34%)
  blocking collectives  27.6 us (25%)
  Pallas kernels  6.25 us (6%)
    ppermute x19, waiting for transfers between devices, shift(): lax.ppermute(value, axis, [(i, (i + by) % size) for i in range(size)])  38.2 us
    ppermute x19, starting transfers between devices, shift(): lax.ppermute(value, axis, [(i, (i + by) % size) for i in range(size)])  37.8 us
    all_to_all x2, blocking collectives, shards(): total = lax.all_to_all(total, 'z', 0, 0, tiled=True)  27.6 us
    pallas_call x7, Pallas kernels, run(): pl.pallas_call(skip(kernel, n, len(after)), out_shape=outs_t, in_specs=[p...  6.25 us
  transfers between devices with their start and end apart: 19, of which 10 were waited for; matrix products, arithmetic and copies ran while one was open for 0% of the time, Pallas kernels for 0%

profile of v2, /device:TPU:1, one launch (start us, length us, event | category | flops | bytes accessed | tf_op | source)
XLA Modules:
  0.0 110.7 jit_solution(14855925997914368638)
XLA Ops:
  0.6 1.9 %shard_map.58.refs_0_.refs_8_ = bf16[1808,128]{1,0:T(8,128)(2,1)} custom-call(bf16[384,384]{1,0:T(8,128)(2,1)} %refs_0_.1, bf16[144,112]{1,0:T(8,128)(2,1)} %refs_1_.1, bf16[128,512]{1,0:T(8,128)(2,1)} %refs_2_.1), custom_call_target="tpu_custom_call" | custom-call | bytes 921088 | tf_op jit(solution)/shard_map/pallas_call | solution.py:51
  2.5 2.1 %collective-permute-start = (bf16[1808,128]{1,0:T(8,128)(2,1)}, bf16[1808,128]{1,0:T(8,128)(2,1)S(1)}, u32[]{:S(2)}, u32[]{:S(2)}) collective-permute-start(bf16[1808,128]{1,0:T(8,128)(2,1)} %shard_map.58.refs_0_.refs_8_), channel_id=1, source_target_pairs={{0,1},{1,2},{2,3},{3,0},{4,5},{5,6},{6,7},{7,4},{8,9},{9,10},{10,1... | collective-permute-start | bytes 1388552 | tf_op jit(solution)/shard_map/ppermute | solution.py:309
  4.6 1.4 %collective-permute-start.1 = (bf16[1808,128]{1,0:T(8,128)(2,1)}, bf16[1808,128]{1,0:T(8,128)(2,1)S(1)}, u32[]{:S(2)}, u32[]{:S(2)}) collective-permute-start(bf16[1808,128]{1,0:T(8,128)(2,1)} %shard_map.58.refs_0_.refs_8_), channel_id=1, source_target_pairs={{0,3},{1,0},{2,1},{3,2},{4,7},{5,4},{6,5},{7,6},{8,11},{9,8},{10,9... | collective-permute-start | bytes 1388552 | tf_op jit(solution)/shard_map/ppermute | solution.py:309
  6.0 8.2 %collective-permute-done.refs_1_.refs_9_ = bf16[1808,128]{1,0:T(8,128)(2,1)S(1)} collective-permute-done((bf16[1808,128]{1,0:T(8,128)(2,1)}, bf16[1808,128]{1,0:T(8,128)(2,1)S(1)}, u32[]{:S(2)}, u32[]{:S(2)}) %collective-permute-start) | collective-permute-done | bytes 462880 | tf_op jit(solution)/shard_map/ppermute | solution.py:309
  14.2 2.0 %collective-permute-start.2 = (bf16[912,128]{1,0:T(8,128)(2,1)S(1)}, bf16[912,128]{1,0:T(8,128)(2,1)S(1)}, u32[]{:S(2)}, u32[]{:S(2)}) collective-permute-start(bf16[912,128]{1,0:T(8,128)(2,1)S(1)} %slice.16), channel_id=1, source_target_pairs={{0,1},{1,2},{2,3},{3,0},{4,5},{5,6},{6,7},{7,4},{8,9},{9,10},{10,1... | collective-permute-start | bytes 700424 | tf_op jit(solution)/shard_map/ppermute | solution.py:309
  16.1 1.7 %collective-permute-start.3 = (bf16[896,128]{1,0:T(8,128)(2,1)S(1)}, bf16[896,128]{1,0:T(8,128)(2,1)S(1)}, u32[]{:S(2)}, u32[]{:S(2)}) collective-permute-start(bf16[896,128]{1,0:T(8,128)(2,1)S(1)} %slice.17), channel_id=1, source_target_pairs={{0,3},{1,0},{2,1},{3,2},{4,7},{5,4},{6,5},{7,6},{8,11},{9,8},{10,9... | collective-permute-start | bytes 688136 | tf_op jit(solution)/shard_map/ppermute | solution.py:309
  17.8 3.3 %collective-permute-done.3.refs_4_.refs_12_ = bf16[896,128]{1,0:T(8,128)(2,1)S(1)} collective-permute-done((bf16[896,128]{1,0:T(8,128)(2,1)S(1)}, bf16[896,128]{1,0:T(8,128)(2,1)S(1)}, u32[]{:S(2)}, u32[]{:S(2)}) %collective-permute-start.3) | collective-permute-done | bytes 229408 | tf_op jit(solution)/shard_map/ppermute | solution.py:309
  21.1 1.1 %shard_map.59 = (bf16[3072,128]{1,0:T(8,128)(2,1)S(1)}, bf16[3072,128]{1,0:T(8,128)(2,1)S(1)}) custom-call(bf16[1808,128]{1,0:T(8,128)(2,1)S(1)} %copy-done, bf16[1808,128]{1,0:T(8,128)(2,1)S(1)} %collective-permute-done.refs_1_.refs_9_, bf16[1808,128]{1,0:T(8,128)(2,1)S(1)} %collective-permute-done.1.refs_2_.refs_10_, ...), custom_call_target="tpu_custom_call" | custom-call | flops 541327360 | bytes 3424256 | tf_op jit(solution)/shard_map/pallas_call | solution.py:51
  22.3 4.0 %collective-permute-start.4 = (bf16[3072,128]{1,0:T(8,128)(2,1)S(1)}, bf16[3072,128]{1,0:T(8,128)(2,1)S(1)}, u32[]{:S(2)}, u32[]{:S(2)}) collective-permute-start(bf16[3072,128]{1,0:T(8,128)(2,1)S(1)} %get-tuple-element.14), channel_id=1, source_target_pairs={{0,4},{4,0},{1,5},{5,1},{2,6},{6,2},{3,7},{7,3},{8,12},{12,8},{9,1... | collective-permute-start | bytes 2359304 | tf_op jit(solution)/shard_map/ppermute | solution.py:309
  26.3 1.9 %collective-permute-done.4.refs_1_ = bf16[3072,128]{1,0:T(8,128)(2,1)S(1)} collective-permute-done((bf16[3072,128]{1,0:T(8,128)(2,1)S(1)}, bf16[3072,128]{1,0:T(8,128)(2,1)S(1)}, u32[]{:S(2)}, u32[]{:S(2)}) %collective-permute-start.4) | collective-permute-done | bytes 786464 | tf_op jit(solution)/shard_map/ppermute | solution.py:309
  28.4 2.1 %collective-permute-start.5 = (bf16[768,128]{1,0:T(8,128)(2,1)S(1)}, bf16[768,128]{1,0:T(8,128)(2,1)S(1)}, u32[]{:S(2)}, u32[]{:S(2)}) collective-permute-start(bf16[768,128]{1,0:T(8,128)(2,1)S(1)} %get-tuple-element.16), channel_id=1, source_target_pairs={{0,64},{64,128},{128,192},{192,0},{1,65},{65,129},{129,193},{193,1... | collective-permute-start | bytes 589832 | tf_op jit(solution)/shard_map/ppermute | solution.py:309
  30.4 2.6 %collective-permute-start.6 = (bf16[768,128]{1,0:T(8,128)(2,1)S(1)}, bf16[768,128]{1,0:T(8,128)(2,1)S(1)}, u32[]{:S(2)}, u32[]{:S(2)}) collective-permute-start(bf16[768,128]{1,0:T(8,128)(2,1)S(1)} %get-tuple-element.17), channel_id=1, source_target_pairs={{0,128},{64,192},{128,0},{192,64},{1,129},{65,193},{129,1},{193,65... | collective-permute-start | bytes 589832 | tf_op jit(solution)/shard_map/ppermute | solution.py:309
  33.1 1.1 collective-permute-start.7
  34.1 2.7 %collective-permute-done.5.refs_1_ = bf16[768,128]{1,0:T(8,128)(2,1)S(1)} collective-permute-done((bf16[768,128]{1,0:T(8,128)(2,1)S(1)}, bf16[768,128]{1,0:T(8,128)(2,1)S(1)}, u32[]{:S(2)}, u32[]{:S(2)}) %collective-permute-start.5) | collective-permute-done | bytes 196640 | tf_op jit(solution)/shard_map/ppermute | solution.py:309
  36.8 5.1 %collective-permute-done.6.refs_2_ = bf16[768,128]{1,0:T(8,128)(2,1)S(1)} collective-permute-done((bf16[768,128]{1,0:T(8,128)(2,1)S(1)}, bf16[768,128]{1,0:T(8,128)(2,1)S(1)}, u32[]{:S(2)}, u32[]{:S(2)}) %collective-permute-start.6) | collective-permute-done | bytes 196640 | tf_op jit(solution)/shard_map/ppermute | solution.py:309
  42.0 16.4 %all_to_all.22 = bf16[8,96,128]{2,1,0:T(8,128)(2,1)S(1)} all-to-all(bf16[8,96,128]{2,1,0:T(8,128)(2,1)S(1)} %bitcast.6), channel_id=1, replica_groups=mesh['y'=4,'z'=8,'c'=2,'x'=4] {'z'}, dimensions={0} | all-to-all | bytes 393216 | tf_op jit(solution)/shard_map/all_to_all | solution.py:342
  58.5 11.1 %all_to_all.23 = bf16[8,96,128]{2,1,0:T(8,128)(2,1)S(1)} all-to-all(bf16[8,96,128]{2,1,0:T(8,128)(2,1)S(1)} %bitcast.5), channel_id=1, replica_groups=mesh['y'=4,'z'=8,'c'=2,'x'=4] {'z'}, dimensions={0} | all-to-all | bytes 393216 | tf_op jit(solution)/shard_map/all_to_all | solution.py:344
  69.6 3.5 %collective-permute-start.10 = (bf16[768,128]{1,0:T(8,128)(2,1)S(1)}, bf16[768,128]{1,0:T(8,128)(2,1)S(1)}, u32[]{:S(2)}, u32[]{:S(2)}) collective-permute-start(bf16[768,128]{1,0:T(8,128)(2,1)S(1)} %bitcast.7), channel_id=1, source_target_pairs={{0,192},{64,0},{128,64},{192,128},{1,193},{65,1},{129,65},{193,129... | collective-permute-start | bytes 589832 | tf_op jit(solution)/shard_map/ppermute | solution.py:309
  73.1 0.6 collective-permute-start.8
  73.7 3.8 %collective-permute-start.11 = (bf16[768,128]{1,0:T(8,128)(2,1)S(1)}, bf16[768,128]{1,0:T(8,128)(2,1)S(1)}, u32[]{:S(2)}, u32[]{:S(2)}) collective-permute-start(bf16[768,128]{1,0:T(8,128)(2,1)S(1)} %bitcast.10), channel_id=1, source_target_pairs={{0,4},{4,0},{1,5},{5,1},{2,6},{6,2},{3,7},{7,3},{8,12},{12,8},{9,1... | collective-permute-start | bytes 589832 | tf_op jit(solution)/shard_map/ppermute | solution.py:309
  77.5 0.9 collective-permute-done.10.refs_3_
  78.4 4.1 %collective-permute-start.14 = (bf16[768,128]{1,0:T(8,128)(2,1)S(1)}, bf16[768,128]{1,0:T(8,128)(2,1)S(1)}, u32[]{:S(2)}, u32[]{:S(2)}) collective-permute-start(bf16[768,128]{1,0:T(8,128)(2,1)S(1)} %collective-permute-done.10.refs_3_), channel_id=1, source_target_pairs={{0,4},{4,0},{1,5},{5,1},{2,6},{6,2},{3,7},{7,3},{8,12},{12,8},{9,1... | collective-permute-start | bytes 589832 | tf_op jit(solution)/shard_map/ppermute | solution.py:309
  82.5 1.7 %collective-permute-start.13 = (bf16[768,128]{1,0:T(8,128)(2,1)S(1)}, bf16[768,128]{1,0:T(8,128)(2,1)S(1)}, u32[]{:S(2)}, u32[]{:S(2)}) collective-permute-start(bf16[768,128]{1,0:T(8,128)(2,1)S(1)} %collective-permute-done.9.refs_2_), channel_id=1, source_target_pairs={{0,4},{4,0},{1,5},{5,1},{2,6},{6,2},{3,7},{7,3},{8,12},{12,8},{9,1... | collective-permute-start | bytes 589832 | tf_op jit(solution)/shard_map/ppermute | solution.py:309
  84.2 1.7 %collective-permute-start.12 = (bf16[768,128]{1,0:T(8,128)(2,1)S(1)}, bf16[768,128]{1,0:T(8,128)(2,1)S(1)}, u32[]{:S(2)}, u32[]{:S(2)}) collective-permute-start(bf16[768,128]{1,0:T(8,128)(2,1)S(1)} %collective-permute-done.8.refs_1_), channel_id=1, source_target_pairs={{0,4},{4,0},{1,5},{5,1},{2,6},{6,2},{3,7},{7,3},{8,12},{12,8},{9,1... | collective-permute-start | bytes 589832 | tf_op jit(solution)/shard_map/ppermute | solution.py:309
  85.9 1.1 collective-permute-done.12.refs_5_
  87.0 1.2 %shard_map.63 = (bf16[2944,128]{1,0:T(8,128)(2,1)S(1)}, bf16[3200,128]{1,0:T(8,128)(2,1)S(1)}, bf16[1808,128]{1,0:T(8,128)(2,1)S(1)}, f32[1808,128]{1,0:T(8,128)S(1)}) custom-call(bf16[768,128]{1,0:T(8,128)(2,1)S(1)} %bitcast.11, bf16[768,128]{1,0:T(8,128)(2,1)S(1)} %collective-permute-done.8.refs_1_, bf16[768,128]{1,0:T(8,128)(2,1)S(1)} %collective-permute-done.9.refs_2_, ...), custom_call_target="tpu_custom_call" | custom-call | flops 541327360 | bytes 6385664 | tf_op jit(solution)/shard_map/pallas_call | solution.py:51
  88.2 2.8 %collective-permute-start.16 = (bf16[1808,128]{1,0:T(8,128)(2,1)S(1)}, bf16[1808,128]{1,0:T(8,128)(2,1)S(1)}, u32[]{:S(2)}, u32[]{:S(2)}) collective-permute-start(bf16[1808,128]{1,0:T(8,128)(2,1)S(1)} %get-tuple-element.22.refs_3_), channel_id=1, source_target_pairs={{0,3},{1,0},{2,1},{3,2},{4,7},{5,4},{6,5},{7,6},{8,11},{9,8},{10,9... | collective-permute-start | bytes 1388552 | tf_op jit(solution)/shard_map/ppermute | solution.py:309
  91.0 10.3 %collective-permute-done.15.refs_4_ = bf16[1808,128]{1,0:T(8,128)(2,1)S(1)} collective-permute-done((bf16[1808,128]{1,0:T(8,128)(2,1)S(1)}, bf16[1808,128]{1,0:T(8,128)(2,1)S(1)}, u32[]{:S(2)}, u32[]{:S(2)}) %collective-permute-start.15) | collective-permute-done | bytes 462880 | tf_op jit(solution)/shard_map/ppermute | solution.py:309
  101.4 2.7 %collective-permute-start.18 = (bf16[848,128]{1,0:T(8,128)(2,1)S(1)}, bf16[848,128]{1,0:T(8,128)(2,1)S(1)}, u32[]{:S(2)}, u32[]{:S(2)}) collective-permute-start(bf16[848,128]{1,0:T(8,128)(2,1)S(1)} %slice.19), channel_id=1, source_target_pairs={{0,3},{1,0},{2,1},{3,2},{4,7},{5,4},{6,5},{7,6},{8,11},{9,8},{10,9... | collective-permute-start | bytes 651272 | tf_op jit(solution)/shard_map/ppermute | solution.py:309
  104.2 3.2 %collective-permute-done.18.refs_7_ = bf16[848,128]{1,0:T(8,128)(2,1)S(1)} collective-permute-done((bf16[848,128]{1,0:T(8,128)(2,1)S(1)}, bf16[848,128]{1,0:T(8,128)(2,1)S(1)}, u32[]{:S(2)}, u32[]{:S(2)}) %collective-permute-start.18) | collective-permute-done | bytes 217120 | tf_op jit(solution)/shard_map/ppermute | solution.py:309
  107.4 1.5 %collective-permute-done.17.refs_6_ = bf16[960,128]{1,0:T(8,128)(2,1)S(1)} collective-permute-done((bf16[960,128]{1,0:T(8,128)(2,1)S(1)}, bf16[960,128]{1,0:T(8,128)(2,1)S(1)}, u32[]{:S(2)}, u32[]{:S(2)}) %collective-permute-start.17) | collective-permute-done | bytes 245792 | tf_op jit(solution)/shard_map/ppermute | solution.py:309
  108.9 1.8 %shard_map.64 = (bf16[384,384]{1,0:T(8,128)(2,1)}, bf16[144,112]{1,0:T(8,128)(2,1)}, bf16[128,512]{1,0:T(8,128)(2,1)}) custom-call(bf16[2944,128]{1,0:T(8,128)(2,1)S(1)} %get-tuple-element.19.refs_0_, bf16[3200,128]{1,0:T(8,128)(2,1)S(1)} %get-tuple-element.20.refs_1_, f32[1808,128]{1,0:T(8,128)S(1)} %get-tuple-element.21.refs_2_, ...), custom_call_target="tpu_custom_call" | custom-call | flops 541327360 | bytes 4808192 | tf_op jit(solution)/shard_map/pallas_call | solution.py:51
  (21 shorter events, 0.6 us)
Async XLA Ops:
  2.5 18.6 %copy-start = (bf16[1808,128]{1,0:T(8,128)(2,1)S(1)}, bf16[1808,128]{1,0:T(8,128)(2,1)}, u32[]{:S(2)}) copy-start(bf16[1808,128]{1,0:T(8,128)(2,1)} %shard_map.58.refs_0_.refs_8_) | copy-start | bytes 1388548
  2.5 11.6 %collective-permute-start = (bf16[1808,128]{1,0:T(8,128)(2,1)}, bf16[1808,128]{1,0:T(8,128)(2,1)S(1)}, u32[]{:S(2)}, u32[]{:S(2)}) collective-permute-start(bf16[1808,128]{1,0:T(8,128)(2,1)} %shard_map.58.refs_0_.refs_8_), channel_id=1, source_target_pairs={{0,1},{1,2},{2,3},{3,0},{4,5},{5,6},{6,7},{7,4},{8,9},{9,10},{10,1... | collective-permute-start | bytes 1388552 | tf_op jit(solution)/shard_map/ppermute | solution.py:309
  4.6 11.5 %collective-permute-start.1 = (bf16[1808,128]{1,0:T(8,128)(2,1)}, bf16[1808,128]{1,0:T(8,128)(2,1)S(1)}, u32[]{:S(2)}, u32[]{:S(2)}) collective-permute-start(bf16[1808,128]{1,0:T(8,128)(2,1)} %shard_map.58.refs_0_.refs_8_), channel_id=1, source_target_pairs={{0,3},{1,0},{2,1},{3,2},{4,7},{5,4},{6,5},{7,6},{8,11},{9,8},{10,9... | collective-permute-start | bytes 1388552 | tf_op jit(solution)/shard_map/ppermute | solution.py:309
  14.2 7.0 %collective-permute-start.2 = (bf16[912,128]{1,0:T(8,128)(2,1)S(1)}, bf16[912,128]{1,0:T(8,128)(2,1)S(1)}, u32[]{:S(2)}, u32[]{:S(2)}) collective-permute-start(bf16[912,128]{1,0:T(8,128)(2,1)S(1)} %slice.16), channel_id=1, source_target_pairs={{0,1},{1,2},{2,3},{3,0},{4,5},{5,6},{6,7},{7,4},{8,9},{9,10},{10,1... | collective-permute-start | bytes 700424 | tf_op jit(solution)/shard_map/ppermute | solution.py:309
  16.1 5.0 %collective-permute-start.3 = (bf16[896,128]{1,0:T(8,128)(2,1)S(1)}, bf16[896,128]{1,0:T(8,128)(2,1)S(1)}, u32[]{:S(2)}, u32[]{:S(2)}) collective-permute-start(bf16[896,128]{1,0:T(8,128)(2,1)S(1)} %slice.17), channel_id=1, source_target_pairs={{0,3},{1,0},{2,1},{3,2},{4,7},{5,4},{6,5},{7,6},{8,11},{9,8},{10,9... | collective-permute-start | bytes 688136 | tf_op jit(solution)/shard_map/ppermute | solution.py:309
  22.3 5.9 %collective-permute-start.4 = (bf16[3072,128]{1,0:T(8,128)(2,1)S(1)}, bf16[3072,128]{1,0:T(8,128)(2,1)S(1)}, u32[]{:S(2)}, u32[]{:S(2)}) collective-permute-start(bf16[3072,128]{1,0:T(8,128)(2,1)S(1)} %get-tuple-element.14), channel_id=1, source_target_pairs={{0,4},{4,0},{1,5},{5,1},{2,6},{6,2},{3,7},{7,3},{8,12},{12,8},{9,1... | collective-permute-start | bytes 2359304 | tf_op jit(solution)/shard_map/ppermute | solution.py:309
  28.4 8.5 %collective-permute-start.5 = (bf16[768,128]{1,0:T(8,128)(2,1)S(1)}, bf16[768,128]{1,0:T(8,128)(2,1)S(1)}, u32[]{:S(2)}, u32[]{:S(2)}) collective-permute-start(bf16[768,128]{1,0:T(8,128)(2,1)S(1)} %get-tuple-element.16), channel_id=1, source_target_pairs={{0,64},{64,128},{128,192},{192,0},{1,65},{65,129},{129,193},{193,1... | collective-permute-start | bytes 589832 | tf_op jit(solution)/shard_map/ppermute | solution.py:309
  30.4 11.5 %collective-permute-start.6 = (bf16[768,128]{1,0:T(8,128)(2,1)S(1)}, bf16[768,128]{1,0:T(8,128)(2,1)S(1)}, u32[]{:S(2)}, u32[]{:S(2)}) collective-permute-start(bf16[768,128]{1,0:T(8,128)(2,1)S(1)} %get-tuple-element.17), channel_id=1, source_target_pairs={{0,128},{64,192},{128,0},{192,64},{1,129},{65,193},{129,1},{193,65... | collective-permute-start | bytes 589832 | tf_op jit(solution)/shard_map/ppermute | solution.py:309
  33.1 8.9 %collective-permute-start.7 = (bf16[768,128]{1,0:T(8,128)(2,1)S(1)}, bf16[768,128]{1,0:T(8,128)(2,1)S(1)}, u32[]{:S(2)}, u32[]{:S(2)}) collective-permute-start(bf16[768,128]{1,0:T(8,128)(2,1)S(1)} %get-tuple-element.18), channel_id=1, source_target_pairs={{0,192},{64,0},{128,64},{192,128},{1,193},{65,1},{129,65},{193,129... | collective-permute-start | bytes 589832 | tf_op jit(solution)/shard_map/ppermute | solution.py:309
  69.6 8.8 %collective-permute-start.10 = (bf16[768,128]{1,0:T(8,128)(2,1)S(1)}, bf16[768,128]{1,0:T(8,128)(2,1)S(1)}, u32[]{:S(2)}, u32[]{:S(2)}) collective-permute-start(bf16[768,128]{1,0:T(8,128)(2,1)S(1)} %bitcast.7), channel_id=1, source_target_pairs={{0,192},{64,0},{128,64},{192,128},{1,193},{65,1},{129,65},{193,129... | collective-permute-start | bytes 589832 | tf_op jit(solution)/shard_map/ppermute | solution.py:309
  73.1 9.3 %collective-permute-start.9 = (bf16[768,128]{1,0:T(8,128)(2,1)S(1)}, bf16[768,128]{1,0:T(8,128)(2,1)S(1)}, u32[]{:S(2)}, u32[]{:S(2)}) collective-permute-start(bf16[768,128]{1,0:T(8,128)(2,1)S(1)} %bitcast.8), channel_id=1, source_target_pairs={{0,128},{64,192},{128,0},{192,64},{1,129},{65,193},{129,1},{193,65... | collective-permute-start | bytes 589832 | tf_op jit(solution)/shard_map/ppermute | solution.py:309
  73.1 11.1 %collective-permute-start.8 = (bf16[768,128]{1,0:T(8,128)(2,1)S(1)}, bf16[768,128]{1,0:T(8,128)(2,1)S(1)}, u32[]{:S(2)}, u32[]{:S(2)}) collective-permute-start(bf16[768,128]{1,0:T(8,128)(2,1)S(1)} %bitcast.9), channel_id=1, source_target_pairs={{0,64},{64,128},{128,192},{192,0},{1,65},{65,129},{129,193},{193,1... | collective-permute-start | bytes 589832 | tf_op jit(solution)/shard_map/ppermute | solution.py:309
  73.7 12.2 %collective-permute-start.11 = (bf16[768,128]{1,0:T(8,128)(2,1)S(1)}, bf16[768,128]{1,0:T(8,128)(2,1)S(1)}, u32[]{:S(2)}, u32[]{:S(2)}) collective-permute-start(bf16[768,128]{1,0:T(8,128)(2,1)S(1)} %bitcast.10), channel_id=1, source_target_pairs={{0,4},{4,0},{1,5},{5,1},{2,6},{6,2},{3,7},{7,3},{8,12},{12,8},{9,1... | collective-permute-start | bytes 589832 | tf_op jit(solution)/shard_map/ppermute | solution.py:309
  78.4 7.5 %collective-permute-start.14 = (bf16[768,128]{1,0:T(8,128)(2,1)S(1)}, bf16[768,128]{1,0:T(8,128)(2,1)S(1)}, u32[]{:S(2)}, u32[]{:S(2)}) collective-permute-start(bf16[768,128]{1,0:T(8,128)(2,1)S(1)} %collective-permute-done.10.refs_3_), channel_id=1, source_target_pairs={{0,4},{4,0},{1,5},{5,1},{2,6},{6,2},{3,7},{7,3},{8,12},{12,8},{9,1... | collective-permute-start | bytes 589832 | tf_op jit(solution)/shard_map/ppermute | solution.py:309
  82.5 3.4 %collective-permute-start.13 = (bf16[768,128]{1,0:T(8,128)(2,1)S(1)}, bf16[768,128]{1,0:T(8,128)(2,1)S(1)}, u32[]{:S(2)}, u32[]{:S(2)}) collective-permute-start(bf16[768,128]{1,0:T(8,128)(2,1)S(1)} %collective-permute-done.9.refs_2_), channel_id=1, source_target_pairs={{0,4},{4,0},{1,5},{5,1},{2,6},{6,2},{3,7},{7,3},{8,12},{12,8},{9,1... | collective-permute-start | bytes 589832 | tf_op jit(solution)/shard_map/ppermute | solution.py:309
  84.2 2.8 %collective-permute-start.12 = (bf16[768,128]{1,0:T(8,128)(2,1)S(1)}, bf16[768,128]{1,0:T(8,128)(2,1)S(1)}, u32[]{:S(2)}, u32[]{:S(2)}) collective-permute-start(bf16[768,128]{1,0:T(8,128)(2,1)S(1)} %collective-permute-done.8.refs_1_), channel_id=1, source_target_pairs={{0,4},{4,0},{1,5},{5,1},{2,6},{6,2},{3,7},{7,3},{8,12},{12,8},{9,1... | collective-permute-start | bytes 589832 | tf_op jit(solution)/shard_map/ppermute | solution.py:309
  88.1 13.2 %collective-permute-start.15 = (bf16[1808,128]{1,0:T(8,128)(2,1)S(1)}, bf16[1808,128]{1,0:T(8,128)(2,1)S(1)}, u32[]{:S(2)}, u32[]{:S(2)}) collective-permute-start(bf16[1808,128]{1,0:T(8,128)(2,1)S(1)} %get-tuple-element.22.refs_3_), channel_id=1, source_target_pairs={{0,1},{1,2},{2,3},{3,0},{4,5},{5,6},{6,7},{7,4},{8,9},{9,10},{10,1... | collective-permute-start | bytes 1388552 | tf_op jit(solution)/shard_map/ppermute | solution.py:309
  88.2 13.2 %collective-permute-start.16 = (bf16[1808,128]{1,0:T(8,128)(2,1)S(1)}, bf16[1808,128]{1,0:T(8,128)(2,1)S(1)}, u32[]{:S(2)}, u32[]{:S(2)}) collective-permute-start(bf16[1808,128]{1,0:T(8,128)(2,1)S(1)} %get-tuple-element.22.refs_3_), channel_id=1, source_target_pairs={{0,3},{1,0},{2,1},{3,2},{4,7},{5,4},{6,5},{7,6},{8,11},{9,8},{10,9... | collective-permute-start | bytes 1388552 | tf_op jit(solution)/shard_map/ppermute | solution.py:309
  101.3 7.6 %collective-permute-start.17 = (bf16[960,128]{1,0:T(8,128)(2,1)S(1)}, bf16[960,128]{1,0:T(8,128)(2,1)S(1)}, u32[]{:S(2)}, u32[]{:S(2)}) collective-permute-start(bf16[960,128]{1,0:T(8,128)(2,1)S(1)} %slice.18), channel_id=1, source_target_pairs={{0,1},{1,2},{2,3},{3,0},{4,5},{5,6},{6,7},{7,4},{8,9},{9,10},{10,1... | collective-permute-start | bytes 737288 | tf_op jit(solution)/shard_map/ppermute | solution.py:309
  101.4 5.9 %collective-permute-start.18 = (bf16[848,128]{1,0:T(8,128)(2,1)S(1)}, bf16[848,128]{1,0:T(8,128)(2,1)S(1)}, u32[]{:S(2)}, u32[]{:S(2)}) collective-permute-start(bf16[848,128]{1,0:T(8,128)(2,1)S(1)} %slice.19), channel_id=1, source_target_pairs={{0,3},{1,0},{2,1},{3,2},{4,7},{5,4},{6,5},{7,6},{8,11},{9,8},{10,9... | collective-permute-start | bytes 651272 | tf_op jit(solution)/shard_map/ppermute | solution.py:309

commit v3 on v2

v3 whole, which is shorter than its diff:
```python
import functools
import math

import jax
import jax.numpy as jnp
from jax import lax
from jax.experimental import pallas as pl
from jax.experimental.pallas import tpu as pltpu
from jax.sharding import Mesh, PartitionSpec as P

coef_a = 3.4445
coef_b = -4.775
coef_c = 2.0315

bf16 = jnp.bfloat16
f32 = jnp.float32

QR, QC = 384, 384
DR, DC = 144, 112
UR, UC = 128, 512
NX, NY, NZ = 4, 4, 8
NP = 2 * NY

X1 = 2 * QR + DR
XROWS = X1 + QR + UR * (UC // 128)

QH, UH, DU = QR // 2, UR // 2, 80
DL = DR - DU

D, P_, C, S = 0, 192, 288, 384
PG = 480
SHARD = 64
SENT = SHARD * NZ
HELD = (("D", 192), ("P", 96), ("S", 96), ("LP", 96), ("LC", 96), ("RC", 96), ("RS", 96))
PIECE = 768
BASE = {"D": 0, "P": 1536, "S": 2304, "LP": 3072, "LC": 3840, "RC": 4608, "RS": 5376}
GROWS = 6144


def vmem(n):
    return [pl.BlockSpec(memory_space=pltpu.VMEM)] * n


def call(kernel, outs, flops=0, scratch=(), hbm=(), after=(), limit=40):
    def run(*args):
        n = len(args)
        args = (*args, *after)
        outs_t = tuple(jax.ShapeDtypeStruct(s, d) for s, d in outs)
        moved = sum(a.size * a.dtype.itemsize for a in args) + sum(
            s.size * s.dtype.itemsize for s in outs_t
        )
        return pl.pallas_call(
            skip(kernel, n, len(after)),
            out_shape=outs_t,
            in_specs=[
                pl.BlockSpec(memory_space=pl.ANY if i in hbm or i >= n else pltpu.VMEM)
                for i in range(len(args))
            ],
            out_specs=tuple(vmem(len(outs))),
            scratch_shapes=list(scratch),
            cost_estimate=pl.CostEstimate(flops=flops, bytes_accessed=moved, transcendentals=0),
            compiler_params=pltpu.CompilerParams(vmem_limit_bytes=limit << 20),
        )(*args)

    return run


def skip(kernel, n, extra):
    return lambda *refs: kernel(*refs[:n], *refs[n + extra :])


def dot_t(a, b):
    return lax.dot_general(a, b, (((1,), (1,)), ((), ())), preferred_element_type=f32)


def dot(a, b):
    return jnp.dot(a, b, preferred_element_type=f32)


def lanes(parts):
    return jnp.concatenate(parts, axis=1)


def rows(parts):
    return jnp.concatenate(parts, axis=0)


def rows_of(block, lo, n):
    cut, parts = block
    if lo < cut:
        return parts[0][lo : lo + n, :]
    return parts[1][lo - cut : lo - cut + n, :]


def x_q(p):
    return lanes([rows_of(p, at, QR) for at in (0, QR, X1)])


def x_d(p):
    return rows_of(p, 2 * QR, DR)


def x_u(p):
    return lanes([rows_of(p, X1 + QR + UR * k, UR) for k in range(4)])


def dot_l(a, b):
    return lax.dot_general(a, b, (((0,), (0,)), ((), ())), preferred_element_type=f32)


def blocks_of(refs, cut):
    out = [(XROWS, (r,)) for r in refs[0:3]]
    return out + ([(cut, tuple(refs[3:5]))] if len(refs) == 5 else [])


def padded(v, to):
    return rows([v, jnp.zeros((to - v.shape[0], v.shape[1]), v.dtype)])


def pack_kernel(q, d, u, o, held, sems):
    moves = [(d, held)]
    for k in range(2):
        moves.append((q.at[:, 128 * k : 128 * (k + 1)], o.at[QR * k : QR * (k + 1), :]))
    moves.append((q.at[:, 256:384], o.at[X1 : X1 + QR, :]))
    for k in range(4):
        at = slice(X1 + QR + UR * k, X1 + QR + UR * (k + 1))
        moves.append((u.at[:, 128 * k : 128 * (k + 1)], o.at[at, :]))
    copies = [pltpu.make_async_copy(a, b, sems.at[i]) for i, (a, b) in enumerate(moves)]
    for copy in copies:
        copy.start()
    copies[0].wait()
    o[2 * QR : X1, :] = jnp.zeros((DR, 128), bf16)
    o[2 * QR : X1, 0:DC] = held[...]
    for copy in copies[1:]:
        copy.wait()


def half_products(a, b, upper):
    g = dot_t(x_q(a)[0:QH] if upper else x_q(a)[QH:QR], x_q(b))
    out = [(QH * k, g[:, 128 * k : 128 * (k + 1)]) for k in range(3)]
    at = 3 * QH
    out.append((at, dot_t(x_u(a)[0:UH] if upper else x_u(a)[UH:UR], x_u(b))))
    at += UH
    mine = x_d(a)[0:DU] if upper else x_d(a)[DU:DR]
    out.append((at, dot_t(mine, x_d(b)[0:128])))
    at += mine.shape[0]
    out.append((at, dot_t(x_d(b)[128:DR], padded(mine, 128))))
    at += DR - 128
    out.append((at, jnp.zeros((96 * NP - at, 128), f32)))
    return out


def gram_kernel(*refs):
    own, left, right = blocks_of(refs[0:3], 0)
    keep, send = refs[3:5]

    def put(low, high, size, base, at, value):
        value = value.astype(bf16)
        done, n = 0, value.shape[0]
        while done < n:
            piece, off = divmod(at + done, size)
            m = min(n - done, size - off)
            ref = low if piece < NY else high
            to = (piece % NY) * PG + base + off
            ref[to : to + m, :] = value[done : done + m, :]
            done += m

    def emit(low, high):
        g = dot_t(x_q(own), x_q(own))
        for k in range(3):
            put(low, high, 192, D, QR * k, g[:, 128 * k : 128 * (k + 1)])
        put(low, high, 192, D, 3 * QR, dot_t(x_u(own), x_u(own)))
        g = dot_t(x_d(own), padded(x_d(own), 256))
        at = 3 * QR + UR
        put(low, high, 192, D, at, g[:, 0:128])
        put(low, high, 192, D, at + DR, g[128:DR, 128:256])
        at += DR + DR - 128
        put(low, high, 192, D, at, jnp.zeros((192 * NP - at, 128), f32))
        for at, value in half_products(own, right, True):
            put(low, high, 96, P_, at, value)
        for at, value in half_products(left, own, False):
            put(low, high, 96, S, at, value)

    def emit_cross(low, high, a, b, upper):
        for at, value in half_products(a, b, upper):
            put(low, high, 96, C, at, value)

    core = lax.axis_index("c")
    first_two = lax.axis_index("x") < 2
    for mine, low, high in ((0, keep, send), (1, send, keep)):

        @pl.when(core == mine)
        def _():
            emit(low, high)

        @pl.when(jnp.logical_and(core == mine, first_two))
        def _():
            emit_cross(low, high, left, right, True)

        @pl.when(jnp.logical_and(core == mine, jnp.logical_not(first_two)))
        def _():
            emit_cross(low, high, right, left, False)


def core_sum_kernel(keep, got, *outs):
    y = lax.axis_index("y")
    n = outs[0].shape[0]
    for i, o in enumerate(outs):
        at = pl.ds(pl.multiple_of(lax.rem(y + i, NY) * n, 16), n)
        o[...] = (keep[at, :].astype(f32) + got[at, :].astype(f32)).astype(bf16)


def y_sum_kernel(a, b, c, d, o):
    o[0:PG, :] = (
        (a[...].astype(f32) + b[...].astype(f32)) + (c[...].astype(f32) + d[...].astype(f32))
    ).astype(bf16)
    o[PG:SENT, :] = jnp.zeros((SENT - PG, 128), bf16)


def z_sum_kernel(a, o):
    total = a[0:SHARD, :].astype(f32)
    for i in range(1, NZ):
        total = total + a[SHARD * i : SHARD * (i + 1), :].astype(f32)
    total = total.astype(bf16)
    for i in range(NZ):
        o[SHARD * i : SHARD * (i + 1), :] = total


def join_kernel(own, left, right, o):
    o[0:288, :] = own[0:288, :]
    o[288:384, :] = own[S : S + 96, :]
    o[384:576, :] = left[...]
    o[576:768, :] = right[...]


def unpack_gram(gram, mine, other):
    y, core = lax.axis_index("y"), lax.axis_index("c")
    for group, which in ((mine, core), (other, 1 - core)):
        for i, piece in enumerate(group):
            p = which * NY + lax.rem(y + NY - i, NY)
            at = 0
            for name, size in HELD:
                to = pl.multiple_of(BASE[name] + p * size, 16)
                gram[pl.ds(to, size), :] = piece[at : at + size, :]
                at += size


def half_q(gram, name):
    return lanes([gram[BASE[name] + QH * k : BASE[name] + QH * (k + 1), :] for k in range(3)])


def half_u(gram, name):
    at = BASE[name] + 3 * QH
    return gram[at : at + UH, :]


def half_d(gram, name, n):
    at = BASE[name] + 3 * QH + UH
    return gram[at : at + n, :], gram[at + n : at + n + DR - 128, :]


def straight(gram, upper, lower, b):
    q = dot(rows([half_q(gram, upper), half_q(gram, lower)]), x_q(b))
    u = dot(rows([half_u(gram, upper), half_u(gram, lower)]), x_u(b))
    main, rest = x_d(b)[0:128], x_d(b)[128:DR]
    parts = []
    for name, n in ((upper, DU), (lower, DL)):
        lead, last = half_d(gram, name, n)
        parts.append(dot(lead, main) + dot_l(last, rest)[0:n])
    return q, rows(parts), u


def turned(gram, upper, lower, b):
    q = dot_l(rows([half_q(gram, upper), half_q(gram, lower)]), x_q(b))
    u = dot_l(rows([half_u(gram, upper), half_u(gram, lower)]), x_u(b))
    d = None
    for name, n, v in ((upper, DU, x_d(b)[0:DU]), (lower, DL, x_d(b)[DU:DR])):
        lead, last = half_d(gram, name, n)
        term = rows([dot_l(lead, v), dot(last, padded(v, 128))])
        d = term if d is None else d + term
    return q, d, u


def own_product(gram, b):
    q = dot(lanes([gram[QR * k : QR * (k + 1), :] for k in range(3)]), x_q(b))
    at = 3 * QR
    u = dot(gram[at : at + UR, :], x_u(b))
    at += UR
    lead, last = gram[at : at + DR, :], gram[at + DR : at + DR + DR - 128, :]
    main, rest = x_d(b)[0:128], x_d(b)[128:DR]
    side = rows([dot_l(lead[128:DR], rest), dot(last, padded(rest, 128))])
    return q, dot(lead, main) + side, u


def added(*terms):
    out = terms[0]
    for t in terms[1:]:
        out = tuple(a + b for a, b in zip(out, t))
    return out


def near_product(gram, own, left, right):
    return added(
        own_product(gram, own),
        straight(gram, "P", "RS", right),
        turned(gram, "LP", "S", left),
    )


def far_product(gram, block, use):
    x = lax.axis_index("x")
    outer = jnp.logical_or(x == 0, x == 3)

    @pl.when(outer)
    def _():
        use(straight(gram, "RC", "LC", block))

    @pl.when(jnp.logical_not(outer))
    def _():
        use(turned(gram, "LC", "RC", block))


def packed_parts(value):
    q, d, u = value
    out = [(at, q[:, 128 * k : 128 * (k + 1)]) for k, at in enumerate((0, QR, X1))]
    out.append((2 * QR, d))
    return out + [(X1 + QR + UR * k, u[:, 128 * k : 128 * (k + 1)]) for k in range(4)]


def first_kernel(*refs):
    own, left, right, far = blocks_of(refs[8:13], X1)
    gram, first_b, acc = refs[13:16]
    unpack_gram(gram, refs[0:4], refs[4:8])
    near = near_product(gram, own, left, right)

    def use(value):
        for at, v in packed_parts(added(near, value)):
            to = slice(at, at + v.shape[0])
            first_b[to, :] = v.astype(bf16)
            acc[to, :] = coef_a * refs[8][to, :].astype(f32) + coef_b * v

    far_product(gram, far, use)


def second_near_kernel(gram, acc, own, left, right, total):
    for at, v in packed_parts(near_product(gram, *blocks_of((own, left, right), 0))):
        to = slice(at, at + v.shape[0])
        total[to, :] = acc[to, :] + coef_c * v


def second_far_kernel(factors, gram, total, o1, o2, step_q, step_d, step_u):
    fq, fd, fu = factors

    def use(value):
        parts = packed_parts(value)
        done = [total[at : at + v.shape[0], :] + coef_c * v for at, v in parts]
        for k in range(3):
            step_q[:, 128 * k : 128 * (k + 1)] = (fq * done[k]).astype(bf16)
        step_d[...] = (fd * done[3]).astype(bf16)[:, 0:DC]
        for k in range(4):
            step_u[:, 128 * k : 128 * (k + 1)] = (fu * done[4 + k]).astype(bf16)

    far_product(gram, (X1, (o1, o2)), use)


def shift(value, axis, size, by):
    return lax.ppermute(value, axis, [(i, (i + by) % size) for i in range(size)])


def ring(own):
    left, right = shift(own, "x", NX, 1), shift(own, "x", NX, -1)
    return [own, left, right, shift(left[0:X1], "x", NX, 1), shift(right[X1:], "x", NX, -1)]


def sum_y(keep, send):
    got = shift(send, "c", 2, 1)
    pieces = call(core_sum_kernel, [((PG, 128), bf16)] * NY)(keep, got)
    got = {i: shift(pieces[i], "y", NY, i) for i in (2, 1, 3)}
    return [pieces[0], got[1], got[2], got[3]]


def gather_y(part):
    got = {i: shift(part, "y", NY, i) for i in (2, 1, 3)}
    mine = [part, got[1], got[2], got[3]]
    return mine + [shift(m, "c", 2, 1) for m in mine]


def shards(grad_q_up, grad_kv_down, grad_kv_up):
    columns = NP * NZ
    factors = tuple(math.sqrt(g.shape[1] * columns) for g in (grad_q_up, grad_kv_down, grad_kv_up))
    flops = 2 * 4 * (QR * QR * QC + UR * UR * UC + DR * DR * 128)
    (packed,) = call(
        pack_kernel,
        [((XROWS, 128), bf16)],
        scratch=[pltpu.VMEM((DR, DC), bf16), pltpu.SemaphoreType.DMA((8,))],
        hbm=(0, 1, 2),
        limit=60,
    )(grad_q_up, grad_kv_down, grad_kv_up)
    x = ring(packed)
    keep, send = call(gram_kernel, [((NY * PG, 128), bf16)] * 2, flops)(*x[0:3])
    (total,) = call(y_sum_kernel, [((SENT, 128), bf16)])(*sum_y(keep, send))
    total = lax.all_to_all(total, "z", 0, 0, tiled=True)
    (total,) = call(z_sum_kernel, [((SENT, 128), bf16)])(total)
    total = lax.all_to_all(total, "z", 0, 0, tiled=True)
    left = shift(total[P_:S], "x", NX, 1)
    right = shift(total[C:PG], "x", NX, -1)
    (piece,) = call(join_kernel, [((PIECE, 128), bf16)])(total, left, right)
    gram, first_b, acc = call(
        first_kernel,
        [((GROWS, 128), bf16), ((XROWS, 128), bf16), ((XROWS, 128), f32)],
        flops,
    )(*gather_y(piece), *x)
    f = ring(first_b)
    (total,) = call(second_near_kernel, [((XROWS, 128), f32)], 3 * flops // 4)(gram, acc, *f[0:3])
    return tuple(
        call(
            functools.partial(second_far_kernel, factors),
            [((QR, QC), bf16), ((DR, DC), bf16), ((UR, UC), bf16)],
            flops // 4,
        )(gram, total, *f[3:5])
    )


def solution(mesh):
    fine = Mesh(mesh.devices.reshape(NY, NZ, 2, NX), ("y", "z", "c", "x"))
    placed = P("x", ("y", "z", "c"))
    return jax.shard_map(
        shards,
        mesh=fine,
        in_specs=(placed, placed, placed),
        out_specs=(placed, placed, placed),
        check_vma=False,
    )
```

time: 111 us -> 107 us (0.964)
  starting transfers between devices: 37.8 us -> 34 us
  waiting for transfers between devices: 38.2 us -> 36.8 us
  blocking collectives: 27.6 us -> 26.4 us
    ppermute x19 -> x21, starting transfers between devices: 37.8 us -> 34 us  [shift(): lax.ppermute(value, axis, [(i, (i + by) % size) for i in range(size)])]
    ppermute x19 -> x21, waiting for transfers between devices: 38.2 us -> 36.8 us  [shift(): lax.ppermute(value, axis, [(i, (i + by) % size) for i in range(size)])]
    all_to_all x2, blocking collectives: 27.6 us -> 26.4 us  [shards(): total = lax.all_to_all(total, 'z', 0, 0, tiled=True)]
    pallas_call x7 -> x9, Pallas kernels: 6.25 us -> 6.79 us  [run(): pl.pallas_call(skip(kernel, n, len(after)), out_shape=outs_t, in_specs=[p...]
  transfers between devices with their start and end apart: 19 -> 21, of which waited for: 10 -> 11; matrix products, arithmetic and copies ran while one was open for 0% -> 0% of each run, Pallas kernels for 0% -> 1%
where the time goes in v3:
time: 107 us; the launch traced here: 106 us
  waiting for transfers between devices  36.8 us (34%)
  starting transfers between devices  34 us (32%)
  blocking collectives  26.4 us (25%)
  Pallas kernels  6.79 us (6%)
  local copies, waits for them, and re-layouts  1.1 us (1%)
    ppermute x21, waiting for transfers between devices, shift(): lax.ppermute(value, axis, [(i, (i + by) % size) for i in range(size)])  36.8 us
    ppermute x21, starting transfers between devices, shift(): lax.ppermute(value, axis, [(i, (i + by) % size) for i in range(size)])  34 us
    all_to_all x2, blocking collectives, shards(): total = lax.all_to_all(total, 'z', 0, 0, tiled=True)  26.4 us
    pallas_call x9, Pallas kernels, run(): pl.pallas_call(skip(kernel, n, len(after)), out_shape=outs_t, in_specs=[p...  6.79 us
  transfers between devices with their start and end apart: 21, of which 11 were waited for; matrix products, arithmetic and copies ran while one was open for 0% of the time, Pallas kernels for 1%

profile of v3, /device:TPU:1, one launch (start us, length us, event | category | flops | bytes accessed | tf_op | source)
XLA Modules:
  0.0 106.0 jit_solution(1330829889306987926)
XLA Ops:
  0.6 1.9 %shard_map.58.refs_0_.refs_8_ = bf16[1808,128]{1,0:T(8,128)(2,1)} custom-call(bf16[384,384]{1,0:T(8,128)(2,1)} %refs_0_.1, bf16[144,112]{1,0:T(8,128)(2,1)} %refs_1_.1, bf16[128,512]{1,0:T(8,128)(2,1)} %refs_2_.1), custom_call_target="tpu_custom_call" | custom-call | bytes 921088 | tf_op jit(solution)/shard_map/pallas_call | solution.py:52
  2.5 3.4 %collective-permute-start.1 = (bf16[1808,128]{1,0:T(8,128)(2,1)}, bf16[1808,128]{1,0:T(8,128)(2,1)S(1)}, u32[]{:S(2)}, u32[]{:S(2)}) collective-permute-start(bf16[1808,128]{1,0:T(8,128)(2,1)} %shard_map.58.refs_0_.refs_8_), channel_id=1, source_target_pairs={{0,3},{1,0},{2,1},{3,2},{4,7},{5,4},{6,5},{7,6},{8,11},{9,8},{10,9... | collective-permute-start | bytes 1388552 | tf_op jit(solution)/shard_map/ppermute | solution.py:367
  5.9 9.6 %collective-permute-done.1.refs_2_.refs_10_ = bf16[1808,128]{1,0:T(8,128)(2,1)S(1)} collective-permute-done((bf16[1808,128]{1,0:T(8,128)(2,1)}, bf16[1808,128]{1,0:T(8,128)(2,1)S(1)}, u32[]{:S(2)}, u32[]{:S(2)}) %collective-permute-start.1) | collective-permute-done | bytes 462880 | tf_op jit(solution)/shard_map/ppermute | solution.py:367
  15.5 3.0 %collective-permute-done.refs_1_.refs_9_ = bf16[1808,128]{1,0:T(8,128)(2,1)S(1)} collective-permute-done((bf16[1808,128]{1,0:T(8,128)(2,1)}, bf16[1808,128]{1,0:T(8,128)(2,1)S(1)}, u32[]{:S(2)}, u32[]{:S(2)}) %collective-permute-start) | collective-permute-done | bytes 462880 | tf_op jit(solution)/shard_map/ppermute | solution.py:367
  18.5 1.0 copy-done
  19.5 1.0 shard_map.59
  20.5 2.0 %collective-permute-start.2 = (bf16[1920,128]{1,0:T(8,128)(2,1)S(1)}, bf16[1920,128]{1,0:T(8,128)(2,1)S(1)}, u32[]{:S(2)}, u32[]{:S(2)}) collective-permute-start(bf16[1920,128]{1,0:T(8,128)(2,1)S(1)} %get-tuple-element.13), channel_id=1, source_target_pairs={{0,4},{4,0},{1,5},{5,1},{2,6},{6,2},{3,7},{7,3},{8,12},{12,8},{9,1... | collective-permute-start | bytes 1474568 | tf_op jit(solution)/shard_map/ppermute | solution.py:367
  22.5 1.5 %collective-permute-done.2.refs_1_ = bf16[1920,128]{1,0:T(8,128)(2,1)S(1)} collective-permute-done((bf16[1920,128]{1,0:T(8,128)(2,1)S(1)}, bf16[1920,128]{1,0:T(8,128)(2,1)S(1)}, u32[]{:S(2)}, u32[]{:S(2)}) %collective-permute-start.2) | collective-permute-done | bytes 491552 | tf_op jit(solution)/shard_map/ppermute | solution.py:367
  24.1 1.4 %collective-permute-start.3 = (bf16[480,128]{1,0:T(8,128)(2,1)S(1)}, bf16[480,128]{1,0:T(8,128)(2,1)S(1)}, u32[]{:S(2)}, u32[]{:S(2)}) collective-permute-start(bf16[480,128]{1,0:T(8,128)(2,1)S(1)} %get-tuple-element.15), channel_id=1, source_target_pairs={{0,64},{64,128},{128,192},{192,0},{1,65},{65,129},{129,193},{193,1... | collective-permute-start | bytes 368648 | tf_op jit(solution)/shard_map/ppermute | solution.py:367
  25.5 2.6 %collective-permute-start.4 = (bf16[480,128]{1,0:T(8,128)(2,1)S(1)}, bf16[480,128]{1,0:T(8,128)(2,1)S(1)}, u32[]{:S(2)}, u32[]{:S(2)}) collective-permute-start(bf16[480,128]{1,0:T(8,128)(2,1)S(1)} %get-tuple-element.16), channel_id=1, source_target_pairs={{0,128},{64,192},{128,0},{192,64},{1,129},{65,193},{129,1},{193,65... | collective-permute-start | bytes 368648 | tf_op jit(solution)/shard_map/ppermute | solution.py:367
  28.1 1.1 %collective-permute-start.5 = (bf16[480,128]{1,0:T(8,128)(2,1)S(1)}, bf16[480,128]{1,0:T(8,128)(2,1)S(1)}, u32[]{:S(2)}, u32[]{:S(2)}) collective-permute-start(bf16[480,128]{1,0:T(8,128)(2,1)S(1)} %get-tuple-element.17), channel_id=1, source_target_pairs={{0,192},{64,0},{128,64},{192,128},{1,193},{65,1},{129,65},{193,129... | collective-permute-start | bytes 368648 | tf_op jit(solution)/shard_map/ppermute | solution.py:367
  29.2 0.9 collective-permute-done.3.refs_1_
  30.1 3.7 %collective-permute-done.4.refs_2_ = bf16[480,128]{1,0:T(8,128)(2,1)S(1)} collective-permute-done((bf16[480,128]{1,0:T(8,128)(2,1)S(1)}, bf16[480,128]{1,0:T(8,128)(2,1)S(1)}, u32[]{:S(2)}, u32[]{:S(2)}) %collective-permute-start.4) | collective-permute-done | bytes 122912 | tf_op jit(solution)/shard_map/ppermute | solution.py:367
  33.9 16.0 %all_to_all.22 = bf16[8,64,128]{2,1,0:T(8,128)(2,1)S(1)} all-to-all(bf16[8,64,128]{2,1,0:T(8,128)(2,1)S(1)} %bitcast.7), channel_id=1, replica_groups=mesh['y'=4,'z'=8,'c'=2,'x'=4] {'z'}, dimensions={0} | all-to-all | bytes 262144 | tf_op jit(solution)/shard_map/all_to_all | solution.py:402
  49.9 10.4 %all_to_all.23 = bf16[8,64,128]{2,1,0:T(8,128)(2,1)S(1)} all-to-all(bf16[8,64,128]{2,1,0:T(8,128)(2,1)S(1)} %bitcast.9), channel_id=1, replica_groups=mesh['y'=4,'z'=8,'c'=2,'x'=4] {'z'}, dimensions={0} | all-to-all | bytes 262144 | tf_op jit(solution)/shard_map/all_to_all | solution.py:404
  60.5 2.7 %collective-permute-start.7 = (bf16[192,128]{1,0:T(8,128)(2,1)S(1)}, bf16[192,128]{1,0:T(8,128)(2,1)S(1)}, u32[]{:S(2)}, u32[]{:S(2)}) collective-permute-start(bf16[192,128]{1,0:T(8,128)(2,1)S(1)} %slice.29), channel_id=1, source_target_pairs={{0,3},{1,0},{2,1},{3,2},{4,7},{5,4},{6,5},{7,6},{8,11},{9,8},{10,9... | collective-permute-start | bytes 147464 | tf_op jit(solution)/shard_map/ppermute | solution.py:367
  63.2 1.4 %collective-permute-done.6.refs_1_ = bf16[192,128]{1,0:T(8,128)(2,1)S(1)} collective-permute-done((bf16[192,128]{1,0:T(8,128)(2,1)S(1)}, bf16[192,128]{1,0:T(8,128)(2,1)S(1)}, u32[]{:S(2)}, u32[]{:S(2)}) %collective-permute-start.6) | collective-permute-done | bytes 49184 | tf_op jit(solution)/shard_map/ppermute | solution.py:367
  64.6 2.1 %collective-permute-start.10 = (bf16[768,128]{1,0:T(8,128)(2,1)S(1)}, bf16[768,128]{1,0:T(8,128)(2,1)S(1)}, u32[]{:S(2)}, u32[]{:S(2)}) collective-permute-start(bf16[768,128]{1,0:T(8,128)(2,1)S(1)} %shard_map.63.refs_0_), channel_id=1, source_target_pairs={{0,192},{64,0},{128,64},{192,128},{1,193},{65,1},{129,65},{193,129... | collective-permute-start | bytes 589832 | tf_op jit(solution)/shard_map/ppermute | solution.py:367
  67.6 1.3 %collective-permute-done.16.refs_12_ = bf16[896,128]{1,0:T(8,128)(2,1)S(1)} collective-permute-done((bf16[896,128]{1,0:T(8,128)(2,1)S(1)}, bf16[896,128]{1,0:T(8,128)(2,1)S(1)}, u32[]{:S(2)}, u32[]{:S(2)}) %collective-permute-start.16) | collective-permute-done | bytes 229408 | tf_op jit(solution)/shard_map/ppermute | solution.py:367
  68.9 4.9 %collective-permute-start.11 = (bf16[768,128]{1,0:T(8,128)(2,1)S(1)}, bf16[768,128]{1,0:T(8,128)(2,1)S(1)}, u32[]{:S(2)}, u32[]{:S(2)}) collective-permute-start(bf16[768,128]{1,0:T(8,128)(2,1)S(1)} %shard_map.63.refs_0_), channel_id=1, source_target_pairs={{0,4},{4,0},{1,5},{5,1},{2,6},{6,2},{3,7},{7,3},{8,12},{12,8},{9,1... | collective-permute-start | bytes 589832 | tf_op jit(solution)/shard_map/ppermute | solution.py:367
  73.8 3.1 %collective-permute-start.14 = (bf16[768,128]{1,0:T(8,128)(2,1)S(1)}, bf16[768,128]{1,0:T(8,128)(2,1)S(1)}, u32[]{:S(2)}, u32[]{:S(2)}) collective-permute-start(bf16[768,128]{1,0:T(8,128)(2,1)S(1)} %collective-permute-done.10.refs_3_), channel_id=1, source_target_pairs={{0,4},{4,0},{1,5},{5,1},{2,6},{6,2},{3,7},{7,3},{8,12},{12,8},{9,1... | collective-permute-start | bytes 589832 | tf_op jit(solution)/shard_map/ppermute | solution.py:367
  76.9 1.9 %collective-permute-start.13 = (bf16[768,128]{1,0:T(8,128)(2,1)S(1)}, bf16[768,128]{1,0:T(8,128)(2,1)S(1)}, u32[]{:S(2)}, u32[]{:S(2)}) collective-permute-start(bf16[768,128]{1,0:T(8,128)(2,1)S(1)} %collective-permute-done.9.refs_2_), channel_id=1, source_target_pairs={{0,4},{4,0},{1,5},{5,1},{2,6},{6,2},{3,7},{7,3},{8,12},{12,8},{9,1... | collective-permute-start | bytes 589832 | tf_op jit(solution)/shard_map/ppermute | solution.py:367
  78.9 2.0 %collective-permute-start.12 = (bf16[768,128]{1,0:T(8,128)(2,1)S(1)}, bf16[768,128]{1,0:T(8,128)(2,1)S(1)}, u32[]{:S(2)}, u32[]{:S(2)}) collective-permute-start(bf16[768,128]{1,0:T(8,128)(2,1)S(1)} %collective-permute-done.8.refs_1_), channel_id=1, source_target_pairs={{0,4},{4,0},{1,5},{5,1},{2,6},{6,2},{3,7},{7,3},{8,12},{12,8},{9,1... | collective-permute-start | bytes 589832 | tf_op jit(solution)/shard_map/ppermute | solution.py:367
  80.9 1.0 collective-permute-done.12.refs_5_
  81.9 1.5 %shard_map.64 = (bf16[6144,128]{1,0:T(8,128)(2,1)S(1)}, bf16[1808,128]{1,0:T(8,128)(2,1)S(1)}, f32[1808,128]{1,0:T(8,128)S(1)}) custom-call(bf16[768,128]{1,0:T(8,128)(2,1)S(1)} %shard_map.63.refs_0_, bf16[768,128]{1,0:T(8,128)(2,1)S(1)} %collective-permute-done.8.refs_1_, bf16[768,128]{1,0:T(8,128)(2,1)S(1)} %collective-permute-done.9.refs_2_, ...), custom_call_target="tpu_custom_call" | custom-call | flops 541327360 | bytes 6385664 | tf_op jit(solution)/shard_map/pallas_call | solution.py:52
  83.5 3.0 %collective-permute-start.18 = (bf16[1808,128]{1,0:T(8,128)(2,1)S(1)}, bf16[1808,128]{1,0:T(8,128)(2,1)S(1)}, u32[]{:S(2)}, u32[]{:S(2)}) collective-permute-start(bf16[1808,128]{1,0:T(8,128)(2,1)S(1)} %get-tuple-element.20.refs_2_), channel_id=1, source_target_pairs={{0,3},{1,0},{2,1},{3,2},{4,7},{5,4},{6,5},{7,6},{8,11},{9,8},{10,9... | collective-permute-start | bytes 1388552 | tf_op jit(solution)/shard_map/ppermute | solution.py:367
  86.6 10.6 %collective-permute-done.17.refs_3_ = bf16[1808,128]{1,0:T(8,128)(2,1)S(1)} collective-permute-done((bf16[1808,128]{1,0:T(8,128)(2,1)S(1)}, bf16[1808,128]{1,0:T(8,128)(2,1)S(1)}, u32[]{:S(2)}, u32[]{:S(2)}) %collective-permute-start.17) | collective-permute-done | bytes 462880 | tf_op jit(solution)/shard_map/ppermute | solution.py:367
  97.3 2.7 %collective-permute-start.20 = (bf16[896,128]{1,0:T(8,128)(2,1)S(1)}, bf16[896,128]{1,0:T(8,128)(2,1)S(1)}, u32[]{:S(2)}, u32[]{:S(2)}) collective-permute-start(bf16[896,128]{1,0:T(8,128)(2,1)S(1)} %slice.33), channel_id=1, source_target_pairs={{0,3},{1,0},{2,1},{3,2},{4,7},{5,4},{6,5},{7,6},{8,11},{9,8},{10,9... | collective-permute-start | bytes 688136 | tf_op jit(solution)/shard_map/ppermute | solution.py:367
  100.0 1.0 shard_map.65.refs_1_
  101.0 2.8 %collective-permute-done.20.refs_3_ = bf16[896,128]{1,0:T(8,128)(2,1)S(1)} collective-permute-done((bf16[896,128]{1,0:T(8,128)(2,1)S(1)}, bf16[896,128]{1,0:T(8,128)(2,1)S(1)}, u32[]{:S(2)}, u32[]{:S(2)}) %collective-permute-start.20) | collective-permute-done | bytes 229408 | tf_op jit(solution)/shard_map/ppermute | solution.py:367
  103.8 1.0 collective-permute-done.19.refs_2_
  104.8 1.2 %shard_map.66 = (bf16[384,384]{1,0:T(8,128)(2,1)}, bf16[144,112]{1,0:T(8,128)(2,1)}, bf16[128,512]{1,0:T(8,128)(2,1)}) custom-call(bf16[6144,128]{1,0:T(8,128)(2,1)S(1)} %get-tuple-element.18.refs_0_, f32[1808,128]{1,0:T(8,128)S(1)} %shard_map.65.refs_1_, bf16[912,128]{1,0:T(8,128)(2,1)S(1)} %collective-permute-done.19.refs_2_, ...), custom_call_target="tpu_custom_call" | custom-call | flops 135331840 | bytes 3419648 | tf_op jit(solution)/shard_map/pallas_call | solution.py:52
  (31 shorter events, 1.5 us)
Async XLA Ops:
  2.5 13.0 %collective-permute-start.1 = (bf16[1808,128]{1,0:T(8,128)(2,1)}, bf16[1808,128]{1,0:T(8,128)(2,1)S(1)}, u32[]{:S(2)}, u32[]{:S(2)}) collective-permute-start(bf16[1808,128]{1,0:T(8,128)(2,1)} %shard_map.58.refs_0_.refs_8_), channel_id=1, source_target_pairs={{0,3},{1,0},{2,1},{3,2},{4,7},{5,4},{6,5},{7,6},{8,11},{9,8},{10,9... | collective-permute-start | bytes 1388552 | tf_op jit(solution)/shard_map/ppermute | solution.py:367
  5.9 12.6 %collective-permute-start = (bf16[1808,128]{1,0:T(8,128)(2,1)}, bf16[1808,128]{1,0:T(8,128)(2,1)S(1)}, u32[]{:S(2)}, u32[]{:S(2)}) collective-permute-start(bf16[1808,128]{1,0:T(8,128)(2,1)} %shard_map.58.refs_0_.refs_8_), channel_id=1, source_target_pairs={{0,1},{1,2},{2,3},{3,0},{4,5},{5,6},{6,7},{7,4},{8,9},{9,10},{10,1... | collective-permute-start | bytes 1388552 | tf_op jit(solution)/shard_map/ppermute | solution.py:367
  18.5 1.0 copy-start
  20.5 3.5 %collective-permute-start.2 = (bf16[1920,128]{1,0:T(8,128)(2,1)S(1)}, bf16[1920,128]{1,0:T(8,128)(2,1)S(1)}, u32[]{:S(2)}, u32[]{:S(2)}) collective-permute-start(bf16[1920,128]{1,0:T(8,128)(2,1)S(1)} %get-tuple-element.13), channel_id=1, source_target_pairs={{0,4},{4,0},{1,5},{5,1},{2,6},{6,2},{3,7},{7,3},{8,12},{12,8},{9,1... | collective-permute-start | bytes 1474568 | tf_op jit(solution)/shard_map/ppermute | solution.py:367
  24.1 57.8 %copy-start.1 = (bf16[1808,128]{1,0:T(8,128)(2,1)S(1)}, bf16[1808,128]{1,0:T(8,128)(2,1)}, u32[]{:S(2)}) copy-start(bf16[1808,128]{1,0:T(8,128)(2,1)} %shard_map.58.refs_0_.refs_8_) | copy-start | bytes 1388548
  24.1 5.9 %collective-permute-start.3 = (bf16[480,128]{1,0:T(8,128)(2,1)S(1)}, bf16[480,128]{1,0:T(8,128)(2,1)S(1)}, u32[]{:S(2)}, u32[]{:S(2)}) collective-permute-start(bf16[480,128]{1,0:T(8,128)(2,1)S(1)} %get-tuple-element.15), channel_id=1, source_target_pairs={{0,64},{64,128},{128,192},{192,0},{1,65},{65,129},{129,193},{193,1... | collective-permute-start | bytes 368648 | tf_op jit(solution)/shard_map/ppermute | solution.py:367
  25.5 8.3 %collective-permute-start.4 = (bf16[480,128]{1,0:T(8,128)(2,1)S(1)}, bf16[480,128]{1,0:T(8,128)(2,1)S(1)}, u32[]{:S(2)}, u32[]{:S(2)}) collective-permute-start(bf16[480,128]{1,0:T(8,128)(2,1)S(1)} %get-tuple-element.16), channel_id=1, source_target_pairs={{0,128},{64,192},{128,0},{192,64},{1,129},{65,193},{129,1},{193,65... | collective-permute-start | bytes 368648 | tf_op jit(solution)/shard_map/ppermute | solution.py:367
  28.1 5.7 %collective-permute-start.5 = (bf16[480,128]{1,0:T(8,128)(2,1)S(1)}, bf16[480,128]{1,0:T(8,128)(2,1)S(1)}, u32[]{:S(2)}, u32[]{:S(2)}) collective-permute-start(bf16[480,128]{1,0:T(8,128)(2,1)S(1)} %get-tuple-element.17), channel_id=1, source_target_pairs={{0,192},{64,0},{128,64},{192,128},{1,193},{65,1},{129,65},{193,129... | collective-permute-start | bytes 368648 | tf_op jit(solution)/shard_map/ppermute | solution.py:367
  60.4 4.2 %collective-permute-start.6 = (bf16[192,128]{1,0:T(8,128)(2,1)S(1)}, bf16[192,128]{1,0:T(8,128)(2,1)S(1)}, u32[]{:S(2)}, u32[]{:S(2)}) collective-permute-start(bf16[192,128]{1,0:T(8,128)(2,1)S(1)} %bitcast.10), channel_id=1, source_target_pairs={{0,1},{1,2},{2,3},{3,0},{4,5},{5,6},{6,7},{7,4},{8,9},{9,10},{10,1... | collective-permute-start | bytes 147464 | tf_op jit(solution)/shard_map/ppermute | solution.py:367
  60.5 4.1 %collective-permute-start.7 = (bf16[192,128]{1,0:T(8,128)(2,1)S(1)}, bf16[192,128]{1,0:T(8,128)(2,1)S(1)}, u32[]{:S(2)}, u32[]{:S(2)}) collective-permute-start(bf16[192,128]{1,0:T(8,128)(2,1)S(1)} %slice.29), channel_id=1, source_target_pairs={{0,3},{1,0},{2,1},{3,2},{4,7},{5,4},{6,5},{7,6},{8,11},{9,8},{10,9... | collective-permute-start | bytes 147464 | tf_op jit(solution)/shard_map/ppermute | solution.py:367
  63.1 5.8 %collective-permute-start.16 = (bf16[896,128]{1,0:T(8,128)(2,1)S(1)}, bf16[896,128]{1,0:T(8,128)(2,1)S(1)}, u32[]{:S(2)}, u32[]{:S(2)}) collective-permute-start(bf16[896,128]{1,0:T(8,128)(2,1)S(1)} %slice.31), channel_id=1, source_target_pairs={{0,3},{1,0},{2,1},{3,2},{4,7},{5,4},{6,5},{7,6},{8,11},{9,8},{10,9... | collective-permute-start | bytes 688136 | tf_op jit(solution)/shard_map/ppermute | solution.py:367
  64.6 9.2 %collective-permute-start.10 = (bf16[768,128]{1,0:T(8,128)(2,1)S(1)}, bf16[768,128]{1,0:T(8,128)(2,1)S(1)}, u32[]{:S(2)}, u32[]{:S(2)}) collective-permute-start(bf16[768,128]{1,0:T(8,128)(2,1)S(1)} %shard_map.63.refs_0_), channel_id=1, source_target_pairs={{0,192},{64,0},{128,64},{192,128},{1,193},{65,1},{129,65},{193,129... | collective-permute-start | bytes 589832 | tf_op jit(solution)/shard_map/ppermute | solution.py:367
  66.7 10.2 %collective-permute-start.9 = (bf16[768,128]{1,0:T(8,128)(2,1)S(1)}, bf16[768,128]{1,0:T(8,128)(2,1)S(1)}, u32[]{:S(2)}, u32[]{:S(2)}) collective-permute-start(bf16[768,128]{1,0:T(8,128)(2,1)S(1)} %shard_map.63.refs_0_), channel_id=1, source_target_pairs={{0,128},{64,192},{128,0},{192,64},{1,129},{65,193},{129,1},{193,65... | collective-permute-start | bytes 589832 | tf_op jit(solution)/shard_map/ppermute | solution.py:367
  67.3 11.6 %collective-permute-start.8 = (bf16[768,128]{1,0:T(8,128)(2,1)S(1)}, bf16[768,128]{1,0:T(8,128)(2,1)S(1)}, u32[]{:S(2)}, u32[]{:S(2)}) collective-permute-start(bf16[768,128]{1,0:T(8,128)(2,1)S(1)} %shard_map.63.refs_0_), channel_id=1, source_target_pairs={{0,64},{64,128},{128,192},{192,0},{1,65},{65,129},{129,193},{193,1... | collective-permute-start | bytes 589832 | tf_op jit(solution)/shard_map/ppermute | solution.py:367
  67.4 13.5 %collective-permute-start.15 = (bf16[912,128]{1,0:T(8,128)(2,1)S(1)}, bf16[912,128]{1,0:T(8,128)(2,1)S(1)}, u32[]{:S(2)}, u32[]{:S(2)}) collective-permute-start(bf16[912,128]{1,0:T(8,128)(2,1)S(1)} %slice.30), channel_id=1, source_target_pairs={{0,1},{1,2},{2,3},{3,0},{4,5},{5,6},{6,7},{7,4},{8,9},{9,10},{10,1... | collective-permute-start | bytes 700424 | tf_op jit(solution)/shard_map/ppermute | solution.py:367
  68.9 12.0 %collective-permute-start.11 = (bf16[768,128]{1,0:T(8,128)(2,1)S(1)}, bf16[768,128]{1,0:T(8,128)(2,1)S(1)}, u32[]{:S(2)}, u32[]{:S(2)}) collective-permute-start(bf16[768,128]{1,0:T(8,128)(2,1)S(1)} %shard_map.63.refs_0_), channel_id=1, source_target_pairs={{0,4},{4,0},{1,5},{5,1},{2,6},{6,2},{3,7},{7,3},{8,12},{12,8},{9,1... | collective-permute-start | bytes 589832 | tf_op jit(solution)/shard_map/ppermute | solution.py:367
  73.8 7.1 %collective-permute-start.14 = (bf16[768,128]{1,0:T(8,128)(2,1)S(1)}, bf16[768,128]{1,0:T(8,128)(2,1)S(1)}, u32[]{:S(2)}, u32[]{:S(2)}) collective-permute-start(bf16[768,128]{1,0:T(8,128)(2,1)S(1)} %collective-permute-done.10.refs_3_), channel_id=1, source_target_pairs={{0,4},{4,0},{1,5},{5,1},{2,6},{6,2},{3,7},{7,3},{8,12},{12,8},{9,1... | collective-permute-start | bytes 589832 | tf_op jit(solution)/shard_map/ppermute | solution.py:367
  76.9 4.0 %collective-permute-start.13 = (bf16[768,128]{1,0:T(8,128)(2,1)S(1)}, bf16[768,128]{1,0:T(8,128)(2,1)S(1)}, u32[]{:S(2)}, u32[]{:S(2)}) collective-permute-start(bf16[768,128]{1,0:T(8,128)(2,1)S(1)} %collective-permute-done.9.refs_2_), channel_id=1, source_target_pairs={{0,4},{4,0},{1,5},{5,1},{2,6},{6,2},{3,7},{7,3},{8,12},{12,8},{9,1... | collective-permute-start | bytes 589832 | tf_op jit(solution)/shard_map/ppermute | solution.py:367
  78.9 3.1 %collective-permute-start.12 = (bf16[768,128]{1,0:T(8,128)(2,1)S(1)}, bf16[768,128]{1,0:T(8,128)(2,1)S(1)}, u32[]{:S(2)}, u32[]{:S(2)}) collective-permute-start(bf16[768,128]{1,0:T(8,128)(2,1)S(1)} %collective-permute-done.8.refs_1_), channel_id=1, source_target_pairs={{0,4},{4,0},{1,5},{5,1},{2,6},{6,2},{3,7},{7,3},{8,12},{12,8},{9,1... | collective-permute-start | bytes 589832 | tf_op jit(solution)/shard_map/ppermute | solution.py:367
  83.5 13.7 %collective-permute-start.17 = (bf16[1808,128]{1,0:T(8,128)(2,1)S(1)}, bf16[1808,128]{1,0:T(8,128)(2,1)S(1)}, u32[]{:S(2)}, u32[]{:S(2)}) collective-permute-start(bf16[1808,128]{1,0:T(8,128)(2,1)S(1)} %get-tuple-element.20.refs_2_), channel_id=1, source_target_pairs={{0,1},{1,2},{2,3},{3,0},{4,5},{5,6},{6,7},{7,4},{8,9},{9,10},{10,1... | collective-permute-start | bytes 1388552 | tf_op jit(solution)/shard_map/ppermute | solution.py:367
  83.5 13.7 %collective-permute-start.18 = (bf16[1808,128]{1,0:T(8,128)(2,1)S(1)}, bf16[1808,128]{1,0:T(8,128)(2,1)S(1)}, u32[]{:S(2)}, u32[]{:S(2)}) collective-permute-start(bf16[1808,128]{1,0:T(8,128)(2,1)S(1)} %get-tuple-element.20.refs_2_), channel_id=1, source_target_pairs={{0,3},{1,0},{2,1},{3,2},{4,7},{5,4},{6,5},{7,6},{8,11},{9,8},{10,9... | collective-permute-start | bytes 1388552 | tf_op jit(solution)/shard_map/ppermute | solution.py:367
  97.2 7.6 %collective-permute-start.19 = (bf16[912,128]{1,0:T(8,128)(2,1)S(1)}, bf16[912,128]{1,0:T(8,128)(2,1)S(1)}, u32[]{:S(2)}, u32[]{:S(2)}) collective-permute-start(bf16[912,128]{1,0:T(8,128)(2,1)S(1)} %slice.32), channel_id=1, source_target_pairs={{0,1},{1,2},{2,3},{3,0},{4,5},{5,6},{6,7},{7,4},{8,9},{9,10},{10,1... | collective-permute-start | bytes 700424 | tf_op jit(solution)/shard_map/ppermute | solution.py:367
  97.3 6.5 %collective-permute-start.20 = (bf16[896,128]{1,0:T(8,128)(2,1)S(1)}, bf16[896,128]{1,0:T(8,128)(2,1)S(1)}, u32[]{:S(2)}, u32[]{:S(2)}) collective-permute-start(bf16[896,128]{1,0:T(8,128)(2,1)S(1)} %slice.33), channel_id=1, source_target_pairs={{0,3},{1,0},{2,1},{3,2},{4,7},{5,4},{6,5},{7,6},{8,11},{9,8},{10,9... | collective-permute-start | bytes 688136 | tf_op jit(solution)/shard_map/ppermute | solution.py:367

commit v4 on v3

--- a/solution.py
+++ b/solution.py
@@ -27,21 +27,23 @@
 QH, UH, DU = QR // 2, UR // 2, 80
 DL = DR - DU
 
-D, P_, C, S = 0, 192, 288, 384
-PG = 480
+DN = 144
+D, P_, C, S = 0, DN, DN + 96, DN + 192
+PG = DN + 288
 SHARD = 64
 SENT = SHARD * NZ
-HELD = (("D", 192), ("P", 96), ("S", 96), ("LP", 96), ("LC", 96), ("RC", 96), ("RS", 96))
-PIECE = 768
-BASE = {"D": 0, "P": 1536, "S": 2304, "LP": 3072, "LC": 3840, "RC": 4608, "RS": 5376}
-GROWS = 6144
+HELD = (("D", DN), ("P", 96), ("S", 96), ("LP", 96), ("LC", 96), ("RC", 96), ("RS", 96))
+PIECE = DN + 576
+BASE = {name: NP * (DN * (i > 0) + 96 * max(i - 1, 0)) for i, (name, _) in enumerate(HELD)}
+GROWS = NP * PIECE
+DQ = (0, QR, 2 * QR - 128, 2 * QR)
 
 
 def vmem(n):
     return [pl.BlockSpec(memory_space=pltpu.VMEM)] * n
 
 
-def call(kernel, outs, flops=0, scratch=(), hbm=(), after=(), limit=40):
+def call(kernel, outs, flops=0, scratch=(), hbm=(), after=()):
     def run(*args):
         n = len(args)
         args = (*args, *after)
@@ -53,13 +55,13 @@
             skip(kernel, n, len(after)),
             out_shape=outs_t,
             in_specs=[
-                pl.BlockSpec(memory_space=pl.ANY if i in hbm or i >= n else pltpu.VMEM)
+                pl.BlockSpec(memory_space=pltpu.HBM if i in hbm else pl.ANY if i >= n else pltpu.VMEM)
                 for i in range(len(args))
             ],
             out_specs=tuple(vmem(len(outs))),
             scratch_shapes=list(scratch),
             cost_estimate=pl.CostEstimate(flops=flops, bytes_accessed=moved, transcendentals=0),
-            compiler_params=pltpu.CompilerParams(vmem_limit_bytes=limit << 20),
+            compiler_params=pltpu.CompilerParams(vmem_limit_bytes=40 << 20),
         )(*args)
 
     return run
@@ -150,9 +152,11 @@
     return out
 
 
-def gram_kernel(*refs):
-    own, left, right = blocks_of(refs[0:3], 0)
-    keep, send = refs[3:5]
+def gram_kernel(near, *refs):
+    own = (XROWS, (refs[0],))
+    left, right = ((XROWS, (r,)) for r in refs[1:3]) if near else (None, None)
+    keep, send = refs[-2:]
+    total = PG - DN if near else DN
 
     def put(low, high, size, base, at, value):
         value = value.astype(bf16)
@@ -161,29 +165,35 @@
             piece, off = divmod(at + done, size)
             m = min(n - done, size - off)
             ref = low if piece < NY else high
-            to = (piece % NY) * PG + base + off
+            to = (piece % NY) * total + base + off
             ref[to : to + m, :] = value[done : done + m, :]
             done += m
 
+    def emit_own(low, high):
+        g = dot_t(x_q(own), x_q(own))
+        for k, at in enumerate(DQ):
+            put(low, high, DN, D, at, g[128 * k : QR, 128 * k : 128 * (k + 1)])
+        at = DQ[3]
+        put(low, high, DN, D, at, dot_t(x_u(own), x_u(own)))
+        g = dot_t(x_d(own), padded(x_d(own), 256))
+        at += UR
+        put(low, high, DN, D, at, g[:, 0:128])
+        put(low, high, DN, D, at + DR, g[128:DR, 128:256])
+        at += DR + DR - 128
+        put(low, high, DN, D, at, jnp.zeros((DN * NP - at, 128), f32))
+
     def emit(low, high):
-        g = dot_t(x_q(own), x_q(own))
-        for k in range(3):
-            put(low, high, 192, D, QR * k, g[:, 128 * k : 128 * (k + 1)])
-        put(low, high, 192, D, 3 * QR, dot_t(x_u(own), x_u(own)))
-        g = dot_t(x_d(own), padded(x_d(own), 256))
-        at = 3 * QR + UR
-        put(low, high, 192, D, at, g[:, 0:128])
-        put(low, high, 192, D, at + DR, g[128:DR, 128:256])
-        at += DR + DR - 128
-        put(low, high, 192, D, at, jnp.zeros((192 * NP - at, 128), f32))
+        if not near:
+            emit_own(low, high)
+            return
         for at, value in half_products(own, right, True):
-            put(low, high, 96, P_, at, value)
+            put(low, high, 96, P_ - DN, at, value)
         for at, value in half_products(left, own, False):
-            put(low, high, 96, S, at, value)
+            put(low, high, 96, S - DN, at, value)
 
     def emit_cross(low, high, a, b, upper):
         for at, value in half_products(a, b, upper):
-            put(low, high, 96, C, at, value)
+            put(low, high, 96, C - DN, at, value)
 
     core = lax.axis_index("c")
     first_two = lax.axis_index("x") < 2
@@ -192,6 +202,9 @@
         @pl.when(core == mine)
         def _():
             emit(low, high)
+
+        if not near:
+            continue
 
         @pl.when(jnp.logical_and(core == mine, first_two))
         def _():
@@ -210,10 +223,19 @@
         o[...] = (keep[at, :].astype(f32) + got[at, :].astype(f32)).astype(bf16)
 
 
-def y_sum_kernel(a, b, c, d, o):
-    o[0:PG, :] = (
+def total_of(a, b, c, d):
+    return (
         (a[...].astype(f32) + b[...].astype(f32)) + (c[...].astype(f32) + d[...].astype(f32))
     ).astype(bf16)
+
+
+def own_sum_kernel(a, b, c, d, o):
+    o[...] = total_of(a, b, c, d)
+
+
+def y_sum_kernel(own, a, b, c, d, o):
+    o[0:DN, :] = own[...]
+    o[DN:PG, :] = total_of(a, b, c, d)
     o[PG:SENT, :] = jnp.zeros((SENT - PG, 128), bf16)
 
 
@@ -227,10 +249,10 @@
 
 
 def join_kernel(own, left, right, o):
-    o[0:288, :] = own[0:288, :]
-    o[288:384, :] = own[S : S + 96, :]
-    o[384:576, :] = left[...]
-    o[576:768, :] = right[...]
+    o[0:C, :] = own[0:C, :]
+    o[C:S, :] = own[S:PG, :]
+    o[S : S + 192, :] = left[...]
+    o[S + 192 : PIECE, :] = right[...]
 
 
 def unpack_gram(gram, mine, other):
@@ -282,8 +304,17 @@
 
 
 def own_product(gram, b):
-    q = dot(lanes([gram[QR * k : QR * (k + 1), :] for k in range(3)]), x_q(b))
-    at = 3 * QR
+    x = x_q(b)
+    g0, g1, g2 = (gram[DQ[k] : DQ[k + 1], :] for k in range(3))
+    q0, q1, q2 = (dot(g, x[128 * k : 128 * (k + 1)]) for k, g in enumerate((g0, g1, g2)))
+    q = rows(
+        [
+            q0[0:128] + dot_l(g0[128:384], x[128:384]),
+            q0[128:256] + q1[0:128] + dot_l(g1[128:256], x[256:384]),
+            q0[256:384] + q1[128:256] + q2,
+        ]
+    )
+    at = DQ[3]
     u = dot(gram[at : at + UR, :], x_u(b))
     at += UR
     lead, last = gram[at : at + DR, :], gram[at + DR : at + DR + DR - 128, :]
@@ -372,9 +403,9 @@
     return [own, left, right, shift(left[0:X1], "x", NX, 1), shift(right[X1:], "x", NX, -1)]
 
 
-def sum_y(keep, send):
+def sum_y(keep, send, n):
     got = shift(send, "c", 2, 1)
-    pieces = call(core_sum_kernel, [((PG, 128), bf16)] * NY)(keep, got)
+    pieces = call(core_sum_kernel, [((n, 128), bf16)] * NY)(keep, got)
     got = {i: shift(pieces[i], "y", NY, i) for i in (2, 1, 3)}
     return [pieces[0], got[1], got[2], got[3]]
 
@@ -394,11 +425,17 @@
         [((XROWS, 128), bf16)],
         scratch=[pltpu.VMEM((DR, DC), bf16), pltpu.SemaphoreType.DMA((8,))],
         hbm=(0, 1, 2),
-        limit=60,
     )(grad_q_up, grad_kv_down, grad_kv_up)
     x = ring(packed)
-    keep, send = call(gram_kernel, [((NY * PG, 128), bf16)] * 2, flops)(*x[0:3])
-    (total,) = call(y_sum_kernel, [((SENT, 128), bf16)])(*sum_y(keep, send))
+    keep, send = call(
+        functools.partial(gram_kernel, False), [((NY * DN, 128), bf16)] * 2, flops // 4
+    )(x[0])
+    (own,) = call(own_sum_kernel, [((DN, 128), bf16)])(*sum_y(keep, send, DN))
+    n = PG - DN
+    keep, send = call(
+        functools.partial(gram_kernel, True), [((NY * n, 128), bf16)] * 2, flops // 2, after=(own,)
+    )(*x[0:3])
+    (total,) = call(y_sum_kernel, [((SENT, 128), bf16)])(own, *sum_y(keep, send, n))
     total = lax.all_to_all(total, "z", 0, 0, tiled=True)
     (total,) = call(z_sum_kernel, [((SENT, 128), bf16)])(total)
     total = lax.all_to_all(total, "z", 0, 0, tiled=True)

time: 107 us -> 104 us (0.972)
  waiting for transfers between devices: 36.8 us -> 25.5 us
  starting transfers between devices: 34 us -> 42.3 us
  local copies, waits for them, and re-layouts: 1.1 us -> 2.7 us
  Pallas kernels: 6.79 us -> 5.23 us
    ppermute x21 -> x25, waiting for transfers between devices: 36.8 us -> 25.5 us  [shift(): lax.ppermute(value, axis, [(i, (i + by) % size) for i in range(size)])]
    ppermute x21 -> x25, starting transfers between devices: 34 us -> 42.3 us  [shift(): lax.ppermute(value, axis, [(i, (i + by) % size) for i in range(size)])]
    unnamed x4 -> x6, local copies, waits for them, and re-layouts: 1.02 us -> 2.63 us
    pallas_call x9 -> x12, Pallas kernels: 6.79 us -> 5.23 us  [run(): pl.pallas_call(skip(kernel, n, len(after)), out_shape=outs_t, in_specs=[p...]
  transfers between devices with their start and end apart: 21 -> 25, of which waited for: 11 -> 14; matrix products, arithmetic and copies ran while one was open for 0% -> 0% of each run, Pallas kernels for 1% -> 1%
where the time goes in v4:
time: 104 us; the launch traced here: 103 us
  starting transfers between devices  42.3 us (41%)
  blocking collectives  26.4 us (25%)
  waiting for transfers between devices  25.5 us (25%)
  Pallas kernels  5.23 us (5%)
  local copies, waits for them, and re-layouts  2.7 us (3%)
    ppermute x25, starting transfers between devices, shift(): lax.ppermute(value, axis, [(i, (i + by) % size) for i in range(size)])  42.3 us
    all_to_all x2, blocking collectives, shards(): total = lax.all_to_all(total, 'z', 0, 0, tiled=True)  26.4 us
    ppermute x25, waiting for transfers between devices, shift(): lax.ppermute(value, axis, [(i, (i + by) % size) for i in range(size)])  25.5 us
    pallas_call x12, Pallas kernels, run(): pl.pallas_call(skip(kernel, n, len(after)), out_shape=outs_t, in_specs=[p...  5.23 us
    unnamed x6, local copies, waits for them, and re-layouts  2.63 us
  transfers between devices with their start and end apart: 25, of which 14 were waited for; matrix products, arithmetic and copies ran while one was open for 0% of the time, Pallas kernels for 1%

profile of v4, /device:TPU:1, one launch (start us, length us, event | category | flops | bytes accessed | tf_op | source)
XLA Modules:
  0.0 102.9 jit_solution(13829474554232331633)
XLA Ops:
  0.6 1.0 copy-done
  3.5 3.4 %collective-permute-start.5 = (bf16[1808,128]{1,0:T(8,128)(2,1)S(1)}, bf16[1808,128]{1,0:T(8,128)(2,1)S(1)}, u32[]{:S(2)}, u32[]{:S(2)}) collective-permute-start(bf16[1808,128]{1,0:T(8,128)(2,1)S(1)} %shard_map.58.refs_0_.refs_8_), channel_id=1, source_target_pairs={{0,3},{1,0},{2,1},{3,2},{4,7},{5,4},{6,5},{7,6},{8,11},{9,8},{10,9... | collective-permute-start | bytes 1388552 | tf_op jit(solution)/shard_map/ppermute | solution.py:398
  7.3 2.0 %collective-permute-start = (bf16[576,128]{1,0:T(8,128)(2,1)S(1)}, bf16[576,128]{1,0:T(8,128)(2,1)S(1)}, u32[]{:S(2)}, u32[]{:S(2)}) collective-permute-start(bf16[576,128]{1,0:T(8,128)(2,1)S(1)} %get-tuple-element.19), channel_id=1, source_target_pairs={{0,4},{4,0},{1,5},{5,1},{2,6},{6,2},{3,7},{7,3},{8,12},{12,8},{9,1... | collective-permute-start | bytes 442376 | tf_op jit(solution)/shard_map/ppermute | solution.py:398
  9.3 1.0 collective-permute-done.refs_1_
  10.7 2.6 %collective-permute-start.2 = (bf16[144,128]{1,0:T(8,128)(2,1)S(1)}, bf16[144,128]{1,0:T(8,128)(2,1)S(1)}, u32[]{:S(2)}, u32[]{:S(2)}) collective-permute-start(bf16[144,128]{1,0:T(8,128)(2,1)S(1)} %get-tuple-element.22), channel_id=1, source_target_pairs={{0,128},{64,192},{128,0},{192,64},{1,129},{65,193},{129,1},{193,65... | collective-permute-start | bytes 110600 | tf_op jit(solution)/shard_map/ppermute | solution.py:398
  13.3 1.1 %collective-permute-start.3 = (bf16[144,128]{1,0:T(8,128)(2,1)S(1)}, bf16[144,128]{1,0:T(8,128)(2,1)S(1)}, u32[]{:S(2)}, u32[]{:S(2)}) collective-permute-start(bf16[144,128]{1,0:T(8,128)(2,1)S(1)} %get-tuple-element.23), channel_id=1, source_target_pairs={{0,192},{64,0},{128,64},{192,128},{1,193},{65,1},{129,65},{193,129... | collective-permute-start | bytes 110600 | tf_op jit(solution)/shard_map/ppermute | solution.py:398
  15.1 1.7 %collective-permute-done.3.refs_3_ = bf16[144,128]{1,0:T(8,128)(2,1)S(1)} collective-permute-done((bf16[144,128]{1,0:T(8,128)(2,1)S(1)}, bf16[144,128]{1,0:T(8,128)(2,1)S(1)}, u32[]{:S(2)}, u32[]{:S(2)}) %collective-permute-start.3) | collective-permute-done | bytes 36896 | tf_op jit(solution)/shard_map/ppermute | solution.py:398
  16.9 2.4 %collective-permute-done.4.refs_1_.refs_9_ = bf16[1808,128]{1,0:T(8,128)(2,1)S(1)} collective-permute-done((bf16[1808,128]{1,0:T(8,128)(2,1)S(1)}, bf16[1808,128]{1,0:T(8,128)(2,1)S(1)}, u32[]{:S(2)}, u32[]{:S(2)}) %collective-permute-start.4) | collective-permute-done | bytes 462880 | tf_op jit(solution)/shard_map/ppermute | solution.py:398
  20.0 2.0 %collective-permute-start.6 = (bf16[1152,128]{1,0:T(8,128)(2,1)S(1)}, bf16[1152,128]{1,0:T(8,128)(2,1)S(1)}, u32[]{:S(2)}, u32[]{:S(2)}) collective-permute-start(bf16[1152,128]{1,0:T(8,128)(2,1)S(1)} %get-tuple-element.25), channel_id=1, source_target_pairs={{0,4},{4,0},{1,5},{5,1},{2,6},{6,2},{3,7},{7,3},{8,12},{12,8},{9,1... | collective-permute-start | bytes 884744 | tf_op jit(solution)/shard_map/ppermute | solution.py:398
  22.0 1.2 %collective-permute-done.6.refs_1_ = bf16[1152,128]{1,0:T(8,128)(2,1)S(1)} collective-permute-done((bf16[1152,128]{1,0:T(8,128)(2,1)S(1)}, bf16[1152,128]{1,0:T(8,128)(2,1)S(1)}, u32[]{:S(2)}, u32[]{:S(2)}) %collective-permute-start.6) | collective-permute-done | bytes 294944 | tf_op jit(solution)/shard_map/ppermute | solution.py:398
  23.3 1.4 %collective-permute-start.7 = (bf16[288,128]{1,0:T(8,128)(2,1)S(1)}, bf16[288,128]{1,0:T(8,128)(2,1)S(1)}, u32[]{:S(2)}, u32[]{:S(2)}) collective-permute-start(bf16[288,128]{1,0:T(8,128)(2,1)S(1)} %get-tuple-element.27), channel_id=1, source_target_pairs={{0,64},{64,128},{128,192},{192,0},{1,65},{65,129},{129,193},{193,1... | collective-permute-start | bytes 221192 | tf_op jit(solution)/shard_map/ppermute | solution.py:398
  24.7 2.6 %collective-permute-start.8 = (bf16[288,128]{1,0:T(8,128)(2,1)S(1)}, bf16[288,128]{1,0:T(8,128)(2,1)S(1)}, u32[]{:S(2)}, u32[]{:S(2)}) collective-permute-start(bf16[288,128]{1,0:T(8,128)(2,1)S(1)} %get-tuple-element.28), channel_id=1, source_target_pairs={{0,128},{64,192},{128,0},{192,64},{1,129},{65,193},{129,1},{193,65... | collective-permute-start | bytes 221192 | tf_op jit(solution)/shard_map/ppermute | solution.py:398
  27.3 1.1 %collective-permute-start.9 = (bf16[288,128]{1,0:T(8,128)(2,1)S(1)}, bf16[288,128]{1,0:T(8,128)(2,1)S(1)}, u32[]{:S(2)}, u32[]{:S(2)}) collective-permute-start(bf16[288,128]{1,0:T(8,128)(2,1)S(1)} %get-tuple-element.29), channel_id=1, source_target_pairs={{0,192},{64,0},{128,64},{192,128},{1,193},{65,1},{129,65},{193,129... | collective-permute-start | bytes 221192 | tf_op jit(solution)/shard_map/ppermute | solution.py:398
  28.3 2.2 %collective-permute-done.8.refs_3_ = bf16[288,128]{1,0:T(8,128)(2,1)S(1)} collective-permute-done((bf16[288,128]{1,0:T(8,128)(2,1)S(1)}, bf16[288,128]{1,0:T(8,128)(2,1)S(1)}, u32[]{:S(2)}, u32[]{:S(2)}) %collective-permute-start.8) | collective-permute-done | bytes 73760 | tf_op jit(solution)/shard_map/ppermute | solution.py:398
  30.8 16.0 %all_to_all.22 = bf16[8,64,128]{2,1,0:T(8,128)(2,1)S(1)} all-to-all(bf16[8,64,128]{2,1,0:T(8,128)(2,1)S(1)} %bitcast.6), channel_id=1, replica_groups=mesh['y'=4,'z'=8,'c'=2,'x'=4] {'z'}, dimensions={0} | all-to-all | bytes 262144 | tf_op jit(solution)/shard_map/all_to_all | solution.py:439
  46.9 10.4 %all_to_all.23 = bf16[8,64,128]{2,1,0:T(8,128)(2,1)S(1)} all-to-all(bf16[8,64,128]{2,1,0:T(8,128)(2,1)S(1)} %bitcast.8), channel_id=1, replica_groups=mesh['y'=4,'z'=8,'c'=2,'x'=4] {'z'}, dimensions={0} | all-to-all | bytes 262144 | tf_op jit(solution)/shard_map/all_to_all | solution.py:441
  57.4 1.5 %collective-permute-start.10 = (bf16[192,128]{1,0:T(8,128)(2,1)S(1)}, bf16[192,128]{1,0:T(8,128)(2,1)S(1)}, u32[]{:S(2)}, u32[]{:S(2)}) collective-permute-start(bf16[192,128]{1,0:T(8,128)(2,1)S(1)} %get-tuple-element.34), channel_id=1, source_target_pairs={{0,1},{1,2},{2,3},{3,0},{4,5},{5,6},{6,7},{7,4},{8,9},{9,10},{10,1... | collective-permute-start | bytes 147464 | tf_op jit(solution)/shard_map/ppermute | solution.py:398
  58.9 1.6 %collective-permute-start.20 = (bf16[896,128]{1,0:T(8,128)(2,1)S(1)}, bf16[896,128]{1,0:T(8,128)(2,1)S(1)}, u32[]{:S(2)}, u32[]{:S(2)}) collective-permute-start(bf16[896,128]{1,0:T(8,128)(2,1)S(1)} %slice.27), channel_id=1, source_target_pairs={{0,3},{1,0},{2,1},{3,2},{4,7},{5,4},{6,5},{7,6},{8,11},{9,8},{10,9... | collective-permute-start | bytes 688136 | tf_op jit(solution)/shard_map/ppermute | solution.py:398
  60.6 1.0 collective-permute-done.10.refs_1_
  61.6 2.1 %collective-permute-start.14 = (bf16[720,128]{1,0:T(8,128)(2,1)S(1)}, bf16[720,128]{1,0:T(8,128)(2,1)S(1)}, u32[]{:S(2)}, u32[]{:S(2)}) collective-permute-start(bf16[720,128]{1,0:T(8,128)(2,1)S(1)} %shard_map.66.refs_0_), channel_id=1, source_target_pairs={{0,192},{64,0},{128,64},{192,128},{1,193},{65,1},{129,65},{193,129... | collective-permute-start | bytes 552968 | tf_op jit(solution)/shard_map/ppermute | solution.py:398
  64.7 6.7 %collective-permute-start.15 = (bf16[720,128]{1,0:T(8,128)(2,1)S(1)}, bf16[720,128]{1,0:T(8,128)(2,1)S(1)}, u32[]{:S(2)}, u32[]{:S(2)}) collective-permute-start(bf16[720,128]{1,0:T(8,128)(2,1)S(1)} %shard_map.66.refs_0_), channel_id=1, source_target_pairs={{0,4},{4,0},{1,5},{5,1},{2,6},{6,2},{3,7},{7,3},{8,12},{12,8},{9,1... | collective-permute-start | bytes 552968 | tf_op jit(solution)/shard_map/ppermute | solution.py:398
  71.4 3.5 %collective-permute-start.18 = (bf16[720,128]{1,0:T(8,128)(2,1)S(1)}, bf16[720,128]{1,0:T(8,128)(2,1)S(1)}, u32[]{:S(2)}, u32[]{:S(2)}) collective-permute-start(bf16[720,128]{1,0:T(8,128)(2,1)S(1)} %collective-permute-done.14.refs_3_), channel_id=1, source_target_pairs={{0,4},{4,0},{1,5},{5,1},{2,6},{6,2},{3,7},{7,3},{8,12},{12,8},{9,1... | collective-permute-start | bytes 552968 | tf_op jit(solution)/shard_map/ppermute | solution.py:398
  74.8 2.1 %collective-permute-start.17 = (bf16[720,128]{1,0:T(8,128)(2,1)S(1)}, bf16[720,128]{1,0:T(8,128)(2,1)S(1)}, u32[]{:S(2)}, u32[]{:S(2)}) collective-permute-start(bf16[720,128]{1,0:T(8,128)(2,1)S(1)} %collective-permute-done.13.refs_2_), channel_id=1, source_target_pairs={{0,4},{4,0},{1,5},{5,1},{2,6},{6,2},{3,7},{7,3},{8,12},{12,8},{9,1... | collective-permute-start | bytes 552968 | tf_op jit(solution)/shard_map/ppermute | solution.py:398
  76.9 1.8 %collective-permute-start.16 = (bf16[720,128]{1,0:T(8,128)(2,1)S(1)}, bf16[720,128]{1,0:T(8,128)(2,1)S(1)}, u32[]{:S(2)}, u32[]{:S(2)}) collective-permute-start(bf16[720,128]{1,0:T(8,128)(2,1)S(1)} %collective-permute-done.12.refs_1_), channel_id=1, source_target_pairs={{0,4},{4,0},{1,5},{5,1},{2,6},{6,2},{3,7},{7,3},{8,12},{12,8},{9,1... | collective-permute-start | bytes 552968 | tf_op jit(solution)/shard_map/ppermute | solution.py:398
  78.8 1.0 %collective-permute-done.16.refs_5_ = bf16[720,128]{1,0:T(8,128)(2,1)S(1)} collective-permute-done((bf16[720,128]{1,0:T(8,128)(2,1)S(1)}, bf16[720,128]{1,0:T(8,128)(2,1)S(1)}, u32[]{:S(2)}, u32[]{:S(2)}) %collective-permute-start.16) | collective-permute-done | bytes 184352 | tf_op jit(solution)/shard_map/ppermute | solution.py:398
  79.8 1.5 %shard_map.67 = (bf16[5760,128]{1,0:T(8,128)(2,1)S(1)}, bf16[1808,128]{1,0:T(8,128)(2,1)S(1)}, f32[1808,128]{1,0:T(8,128)S(1)}) custom-call(bf16[720,128]{1,0:T(8,128)(2,1)S(1)} %shard_map.66.refs_0_, bf16[720,128]{1,0:T(8,128)(2,1)S(1)} %collective-permute-done.12.refs_1_, bf16[720,128]{1,0:T(8,128)(2,1)S(1)} %collective-permute-done.13.refs_2_, ...), custom_call_target="tpu_custom_call" | custom-call | flops 541327360 | bytes 6189056 | tf_op jit(solution)/shard_map/pallas_call | solution.py:54
  81.6 2.4 %collective-permute-start.22 = (bf16[1808,128]{1,0:T(8,128)(2,1)S(1)}, bf16[1808,128]{1,0:T(8,128)(2,1)S(1)}, u32[]{:S(2)}, u32[]{:S(2)}) collective-permute-start(bf16[1808,128]{1,0:T(8,128)(2,1)S(1)} %get-tuple-element.32.refs_2_), channel_id=1, source_target_pairs={{0,3},{1,0},{2,1},{3,2},{4,7},{5,4},{6,5},{7,6},{8,11},{9,8},{10,9... | collective-permute-start | bytes 1388552 | tf_op jit(solution)/shard_map/ppermute | solution.py:398
  84.0 10.4 %collective-permute-done.21.refs_3_ = bf16[1808,128]{1,0:T(8,128)(2,1)S(1)} collective-permute-done((bf16[1808,128]{1,0:T(8,128)(2,1)S(1)}, bf16[1808,128]{1,0:T(8,128)(2,1)S(1)}, u32[]{:S(2)}, u32[]{:S(2)}) %collective-permute-start.21) | collective-permute-done | bytes 462880 | tf_op jit(solution)/shard_map/ppermute | solution.py:398
  94.5 2.7 %collective-permute-start.24 = (bf16[896,128]{1,0:T(8,128)(2,1)S(1)}, bf16[896,128]{1,0:T(8,128)(2,1)S(1)}, u32[]{:S(2)}, u32[]{:S(2)}) collective-permute-start(bf16[896,128]{1,0:T(8,128)(2,1)S(1)} %slice.29), channel_id=1, source_target_pairs={{0,3},{1,0},{2,1},{3,2},{4,7},{5,4},{6,5},{7,6},{8,11},{9,8},{10,9... | collective-permute-start | bytes 688136 | tf_op jit(solution)/shard_map/ppermute | solution.py:398
  98.2 2.5 %collective-permute-done.24.refs_3_ = bf16[896,128]{1,0:T(8,128)(2,1)S(1)} collective-permute-done((bf16[896,128]{1,0:T(8,128)(2,1)S(1)}, bf16[896,128]{1,0:T(8,128)(2,1)S(1)}, u32[]{:S(2)}, u32[]{:S(2)}) %collective-permute-start.24) | collective-permute-done | bytes 229408 | tf_op jit(solution)/shard_map/ppermute | solution.py:398
  100.7 1.0 collective-permute-done.23.refs_2_
  101.7 1.2 %shard_map.69 = (bf16[384,384]{1,0:T(8,128)(2,1)}, bf16[144,112]{1,0:T(8,128)(2,1)}, bf16[128,512]{1,0:T(8,128)(2,1)}) custom-call(bf16[5760,128]{1,0:T(8,128)(2,1)S(1)} %get-tuple-element.30.refs_0_, f32[1808,128]{1,0:T(8,128)S(1)} %shard_map.68.refs_1_, bf16[912,128]{1,0:T(8,128)(2,1)S(1)} %collective-permute-done.23.refs_2_, ...), custom_call_target="tpu_custom_call" | custom-call | flops 135331840 | bytes 3321344 | tf_op jit(solution)/shard_map/pallas_call | solution.py:54
  (43 shorter events, 7.3 us)
Async XLA Ops:
  0.6 1.0 copy-start
  1.6 0.9 copy-start.1
  2.5 0.8 copy-start.2
  3.5 13.4 %collective-permute-start.5 = (bf16[1808,128]{1,0:T(8,128)(2,1)S(1)}, bf16[1808,128]{1,0:T(8,128)(2,1)S(1)}, u32[]{:S(2)}, u32[]{:S(2)}) collective-permute-start(bf16[1808,128]{1,0:T(8,128)(2,1)S(1)} %shard_map.58.refs_0_.refs_8_), channel_id=1, source_target_pairs={{0,3},{1,0},{2,1},{3,2},{4,7},{5,4},{6,5},{7,6},{8,11},{9,8},{10,9... | collective-permute-start | bytes 1388552 | tf_op jit(solution)/shard_map/ppermute | solution.py:398
  6.8 12.4 %collective-permute-start.4 = (bf16[1808,128]{1,0:T(8,128)(2,1)S(1)}, bf16[1808,128]{1,0:T(8,128)(2,1)S(1)}, u32[]{:S(2)}, u32[]{:S(2)}) collective-permute-start(bf16[1808,128]{1,0:T(8,128)(2,1)S(1)} %shard_map.58.refs_0_.refs_8_), channel_id=1, source_target_pairs={{0,1},{1,2},{2,3},{3,0},{4,5},{5,6},{6,7},{7,4},{8,9},{9,10},{10,1... | collective-permute-start | bytes 1388552 | tf_op jit(solution)/shard_map/ppermute | solution.py:398
  7.3 3.1 %collective-permute-start = (bf16[576,128]{1,0:T(8,128)(2,1)S(1)}, bf16[576,128]{1,0:T(8,128)(2,1)S(1)}, u32[]{:S(2)}, u32[]{:S(2)}) collective-permute-start(bf16[576,128]{1,0:T(8,128)(2,1)S(1)} %get-tuple-element.19), channel_id=1, source_target_pairs={{0,4},{4,0},{1,5},{5,1},{2,6},{6,2},{3,7},{7,3},{8,12},{12,8},{9,1... | collective-permute-start | bytes 442376 | tf_op jit(solution)/shard_map/ppermute | solution.py:398
  10.3 4.4 %collective-permute-start.1 = (bf16[144,128]{1,0:T(8,128)(2,1)S(1)}, bf16[144,128]{1,0:T(8,128)(2,1)S(1)}, u32[]{:S(2)}, u32[]{:S(2)}) collective-permute-start(bf16[144,128]{1,0:T(8,128)(2,1)S(1)} %get-tuple-element.21), channel_id=1, source_target_pairs={{0,64},{64,128},{128,192},{192,0},{1,65},{65,129},{129,193},{193,1... | collective-permute-start | bytes 110600 | tf_op jit(solution)/shard_map/ppermute | solution.py:398
  10.7 4.4 %collective-permute-start.2 = (bf16[144,128]{1,0:T(8,128)(2,1)S(1)}, bf16[144,128]{1,0:T(8,128)(2,1)S(1)}, u32[]{:S(2)}, u32[]{:S(2)}) collective-permute-start(bf16[144,128]{1,0:T(8,128)(2,1)S(1)} %get-tuple-element.22), channel_id=1, source_target_pairs={{0,128},{64,192},{128,0},{192,64},{1,129},{65,193},{129,1},{193,65... | collective-permute-start | bytes 110600 | tf_op jit(solution)/shard_map/ppermute | solution.py:398
  13.3 3.5 %collective-permute-start.3 = (bf16[144,128]{1,0:T(8,128)(2,1)S(1)}, bf16[144,128]{1,0:T(8,128)(2,1)S(1)}, u32[]{:S(2)}, u32[]{:S(2)}) collective-permute-start(bf16[144,128]{1,0:T(8,128)(2,1)S(1)} %get-tuple-element.23), channel_id=1, source_target_pairs={{0,192},{64,0},{128,64},{192,128},{1,193},{65,1},{129,65},{193,129... | collective-permute-start | bytes 110600 | tf_op jit(solution)/shard_map/ppermute | solution.py:398
  20.0 3.2 %collective-permute-start.6 = (bf16[1152,128]{1,0:T(8,128)(2,1)S(1)}, bf16[1152,128]{1,0:T(8,128)(2,1)S(1)}, u32[]{:S(2)}, u32[]{:S(2)}) collective-permute-start(bf16[1152,128]{1,0:T(8,128)(2,1)S(1)} %get-tuple-element.25), channel_id=1, source_target_pairs={{0,4},{4,0},{1,5},{5,1},{2,6},{6,2},{3,7},{7,3},{8,12},{12,8},{9,1... | collective-permute-start | bytes 884744 | tf_op jit(solution)/shard_map/ppermute | solution.py:398
  23.3 5.1 %collective-permute-start.7 = (bf16[288,128]{1,0:T(8,128)(2,1)S(1)}, bf16[288,128]{1,0:T(8,128)(2,1)S(1)}, u32[]{:S(2)}, u32[]{:S(2)}) collective-permute-start(bf16[288,128]{1,0:T(8,128)(2,1)S(1)} %get-tuple-element.27), channel_id=1, source_target_pairs={{0,64},{64,128},{128,192},{192,0},{1,65},{65,129},{129,193},{193,1... | collective-permute-start | bytes 221192 | tf_op jit(solution)/shard_map/ppermute | solution.py:398
  24.7 5.9 %collective-permute-start.8 = (bf16[288,128]{1,0:T(8,128)(2,1)S(1)}, bf16[288,128]{1,0:T(8,128)(2,1)S(1)}, u32[]{:S(2)}, u32[]{:S(2)}) collective-permute-start(bf16[288,128]{1,0:T(8,128)(2,1)S(1)} %get-tuple-element.28), channel_id=1, source_target_pairs={{0,128},{64,192},{128,0},{192,64},{1,129},{65,193},{129,1},{193,65... | collective-permute-start | bytes 221192 | tf_op jit(solution)/shard_map/ppermute | solution.py:398
  27.3 3.5 %collective-permute-start.9 = (bf16[288,128]{1,0:T(8,128)(2,1)S(1)}, bf16[288,128]{1,0:T(8,128)(2,1)S(1)}, u32[]{:S(2)}, u32[]{:S(2)}) collective-permute-start(bf16[288,128]{1,0:T(8,128)(2,1)S(1)} %get-tuple-element.29), channel_id=1, source_target_pairs={{0,192},{64,0},{128,64},{192,128},{1,193},{65,1},{129,65},{193,129... | collective-permute-start | bytes 221192 | tf_op jit(solution)/shard_map/ppermute | solution.py:398
  57.3 3.3 %collective-permute-start.11 = (bf16[192,128]{1,0:T(8,128)(2,1)S(1)}, bf16[192,128]{1,0:T(8,128)(2,1)S(1)}, u32[]{:S(2)}, u32[]{:S(2)}) collective-permute-start(bf16[192,128]{1,0:T(8,128)(2,1)S(1)} %get-tuple-element.33), channel_id=1, source_target_pairs={{0,3},{1,0},{2,1},{3,2},{4,7},{5,4},{6,5},{7,6},{8,11},{9,8},{10,9... | collective-permute-start | bytes 147464 | tf_op jit(solution)/shard_map/ppermute | solution.py:398
  57.4 4.2 %collective-permute-start.10 = (bf16[192,128]{1,0:T(8,128)(2,1)S(1)}, bf16[192,128]{1,0:T(8,128)(2,1)S(1)}, u32[]{:S(2)}, u32[]{:S(2)}) collective-permute-start(bf16[192,128]{1,0:T(8,128)(2,1)S(1)} %get-tuple-element.34), channel_id=1, source_target_pairs={{0,1},{1,2},{2,3},{3,0},{4,5},{5,6},{6,7},{7,4},{8,9},{9,10},{10,1... | collective-permute-start | bytes 147464 | tf_op jit(solution)/shard_map/ppermute | solution.py:398
  58.9 5.8 %collective-permute-start.20 = (bf16[896,128]{1,0:T(8,128)(2,1)S(1)}, bf16[896,128]{1,0:T(8,128)(2,1)S(1)}, u32[]{:S(2)}, u32[]{:S(2)}) collective-permute-start(bf16[896,128]{1,0:T(8,128)(2,1)S(1)} %slice.27), channel_id=1, source_target_pairs={{0,3},{1,0},{2,1},{3,2},{4,7},{5,4},{6,5},{7,6},{8,11},{9,8},{10,9... | collective-permute-start | bytes 688136 | tf_op jit(solution)/shard_map/ppermute | solution.py:398
  61.6 9.7 %collective-permute-start.14 = (bf16[720,128]{1,0:T(8,128)(2,1)S(1)}, bf16[720,128]{1,0:T(8,128)(2,1)S(1)}, u32[]{:S(2)}, u32[]{:S(2)}) collective-permute-start(bf16[720,128]{1,0:T(8,128)(2,1)S(1)} %shard_map.66.refs_0_), channel_id=1, source_target_pairs={{0,192},{64,0},{128,64},{192,128},{1,193},{65,1},{129,65},{193,129... | collective-permute-start | bytes 552968 | tf_op jit(solution)/shard_map/ppermute | solution.py:398
  63.7 11.1 %collective-permute-start.13 = (bf16[720,128]{1,0:T(8,128)(2,1)S(1)}, bf16[720,128]{1,0:T(8,128)(2,1)S(1)}, u32[]{:S(2)}, u32[]{:S(2)}) collective-permute-start(bf16[720,128]{1,0:T(8,128)(2,1)S(1)} %shard_map.66.refs_0_), channel_id=1, source_target_pairs={{0,128},{64,192},{128,0},{192,64},{1,129},{65,193},{129,1},{193,65... | collective-permute-start | bytes 552968 | tf_op jit(solution)/shard_map/ppermute | solution.py:398
  63.7 13.2 %collective-permute-start.12 = (bf16[720,128]{1,0:T(8,128)(2,1)S(1)}, bf16[720,128]{1,0:T(8,128)(2,1)S(1)}, u32[]{:S(2)}, u32[]{:S(2)}) collective-permute-start(bf16[720,128]{1,0:T(8,128)(2,1)S(1)} %shard_map.66.refs_0_), channel_id=1, source_target_pairs={{0,64},{64,128},{128,192},{192,0},{1,65},{65,129},{129,193},{193,1... | collective-permute-start | bytes 552968 | tf_op jit(solution)/shard_map/ppermute | solution.py:398
  64.4 14.3 %collective-permute-start.19 = (bf16[912,128]{1,0:T(8,128)(2,1)S(1)}, bf16[912,128]{1,0:T(8,128)(2,1)S(1)}, u32[]{:S(2)}, u32[]{:S(2)}) collective-permute-start(bf16[912,128]{1,0:T(8,128)(2,1)S(1)} %slice.26), channel_id=1, source_target_pairs={{0,1},{1,2},{2,3},{3,0},{4,5},{5,6},{6,7},{7,4},{8,9},{9,10},{10,1... | collective-permute-start | bytes 700424 | tf_op jit(solution)/shard_map/ppermute | solution.py:398
  64.7 14.1 %collective-permute-start.15 = (bf16[720,128]{1,0:T(8,128)(2,1)S(1)}, bf16[720,128]{1,0:T(8,128)(2,1)S(1)}, u32[]{:S(2)}, u32[]{:S(2)}) collective-permute-start(bf16[720,128]{1,0:T(8,128)(2,1)S(1)} %shard_map.66.refs_0_), channel_id=1, source_target_pairs={{0,4},{4,0},{1,5},{5,1},{2,6},{6,2},{3,7},{7,3},{8,12},{12,8},{9,1... | collective-permute-start | bytes 552968 | tf_op jit(solution)/shard_map/ppermute | solution.py:398
  71.4 7.4 %collective-permute-start.18 = (bf16[720,128]{1,0:T(8,128)(2,1)S(1)}, bf16[720,128]{1,0:T(8,128)(2,1)S(1)}, u32[]{:S(2)}, u32[]{:S(2)}) collective-permute-start(bf16[720,128]{1,0:T(8,128)(2,1)S(1)} %collective-permute-done.14.refs_3_), channel_id=1, source_target_pairs={{0,4},{4,0},{1,5},{5,1},{2,6},{6,2},{3,7},{7,3},{8,12},{12,8},{9,1... | collective-permute-start | bytes 552968 | tf_op jit(solution)/shard_map/ppermute | solution.py:398
  74.8 3.9 %collective-permute-start.17 = (bf16[720,128]{1,0:T(8,128)(2,1)S(1)}, bf16[720,128]{1,0:T(8,128)(2,1)S(1)}, u32[]{:S(2)}, u32[]{:S(2)}) collective-permute-start(bf16[720,128]{1,0:T(8,128)(2,1)S(1)} %collective-permute-done.13.refs_2_), channel_id=1, source_target_pairs={{0,4},{4,0},{1,5},{5,1},{2,6},{6,2},{3,7},{7,3},{8,12},{12,8},{9,1... | collective-permute-start | bytes 552968 | tf_op jit(solution)/shard_map/ppermute | solution.py:398
  76.9 2.9 %collective-permute-start.16 = (bf16[720,128]{1,0:T(8,128)(2,1)S(1)}, bf16[720,128]{1,0:T(8,128)(2,1)S(1)}, u32[]{:S(2)}, u32[]{:S(2)}) collective-permute-start(bf16[720,128]{1,0:T(8,128)(2,1)S(1)} %collective-permute-done.12.refs_1_), channel_id=1, source_target_pairs={{0,4},{4,0},{1,5},{5,1},{2,6},{6,2},{3,7},{7,3},{8,12},{12,8},{9,1... | collective-permute-start | bytes 552968 | tf_op jit(solution)/shard_map/ppermute | solution.py:398
  81.3 13.1 %collective-permute-start.21 = (bf16[1808,128]{1,0:T(8,128)(2,1)S(1)}, bf16[1808,128]{1,0:T(8,128)(2,1)S(1)}, u32[]{:S(2)}, u32[]{:S(2)}) collective-permute-start(bf16[1808,128]{1,0:T(8,128)(2,1)S(1)} %get-tuple-element.32.refs_2_), channel_id=1, source_target_pairs={{0,1},{1,2},{2,3},{3,0},{4,5},{5,6},{6,7},{7,4},{8,9},{9,10},{10,1... | collective-permute-start | bytes 1388552 | tf_op jit(solution)/shard_map/ppermute | solution.py:398
  81.6 12.9 %collective-permute-start.22 = (bf16[1808,128]{1,0:T(8,128)(2,1)S(1)}, bf16[1808,128]{1,0:T(8,128)(2,1)S(1)}, u32[]{:S(2)}, u32[]{:S(2)}) collective-permute-start(bf16[1808,128]{1,0:T(8,128)(2,1)S(1)} %get-tuple-element.32.refs_2_), channel_id=1, source_target_pairs={{0,3},{1,0},{2,1},{3,2},{4,7},{5,4},{6,5},{7,6},{8,11},{9,8},{10,9... | collective-permute-start | bytes 1388552 | tf_op jit(solution)/shard_map/ppermute | solution.py:398
  94.4 7.3 %collective-permute-start.23 = (bf16[912,128]{1,0:T(8,128)(2,1)S(1)}, bf16[912,128]{1,0:T(8,128)(2,1)S(1)}, u32[]{:S(2)}, u32[]{:S(2)}) collective-permute-start(bf16[912,128]{1,0:T(8,128)(2,1)S(1)} %slice.28), channel_id=1, source_target_pairs={{0,1},{1,2},{2,3},{3,0},{4,5},{5,6},{6,7},{7,4},{8,9},{9,10},{10,1... | collective-permute-start | bytes 700424 | tf_op jit(solution)/shard_map/ppermute | solution.py:398
  94.5 6.2 %collective-permute-start.24 = (bf16[896,128]{1,0:T(8,128)(2,1)S(1)}, bf16[896,128]{1,0:T(8,128)(2,1)S(1)}, u32[]{:S(2)}, u32[]{:S(2)}) collective-permute-start(bf16[896,128]{1,0:T(8,128)(2,1)S(1)} %slice.29), channel_id=1, source_target_pairs={{0,3},{1,0},{2,1},{3,2},{4,7},{5,4},{6,5},{7,6},{8,11},{9,8},{10,9... | collective-permute-start | bytes 688136 | tf_op jit(solution)/shard_map/ppermute | solution.py:398

commit v5 on v4

--- a/solution.py
+++ b/solution.py
@@ -43,7 +43,7 @@
     return [pl.BlockSpec(memory_space=pltpu.VMEM)] * n
 
 
-def call(kernel, outs, flops=0, scratch=(), hbm=(), after=()):
+def call(kernel, outs, flops=0, scratch=(), hbm=(), after=(), limit=40):
     def run(*args):
         n = len(args)
         args = (*args, *after)
@@ -61,7 +61,7 @@
             out_specs=tuple(vmem(len(outs))),
             scratch_shapes=list(scratch),
             cost_estimate=pl.CostEstimate(flops=flops, bytes_accessed=moved, transcendentals=0),
-            compiler_params=pltpu.CompilerParams(vmem_limit_bytes=40 << 20),
+            compiler_params=pltpu.CompilerParams(vmem_limit_bytes=limit << 20),
         )(*args)
 
     return run
@@ -155,7 +155,11 @@
 def gram_kernel(near, *refs):
     own = (XROWS, (refs[0],))
     left, right = ((XROWS, (r,)) for r in refs[1:3]) if near else (None, None)
-    keep, send = refs[-2:]
+    if near:
+        keep, send = refs[-2:]
+    else:
+        keep, send, held = refs[-3:]
+        held[...] = refs[0][...]
     total = PG - DN if near else DN
 
     def put(low, high, size, base, at, value):
@@ -425,11 +429,15 @@
         [((XROWS, 128), bf16)],
         scratch=[pltpu.VMEM((DR, DC), bf16), pltpu.SemaphoreType.DMA((8,))],
         hbm=(0, 1, 2),
+        limit=60,
     )(grad_q_up, grad_kv_down, grad_kv_up)
     x = ring(packed)
-    keep, send = call(
-        functools.partial(gram_kernel, False), [((NY * DN, 128), bf16)] * 2, flops // 4
+    keep, send, held = call(
+        functools.partial(gram_kernel, False),
+        [((NY * DN, 128), bf16)] * 2 + [((XROWS, 128), bf16)],
+        flops // 4,
     )(x[0])
+    x = [held] + x[1:]
     (own,) = call(own_sum_kernel, [((DN, 128), bf16)])(*sum_y(keep, send, DN))
     n = PG - DN
     keep, send = call(

time: 104 us -> 104 us (level)
  Pallas kernels: 5.23 us -> 6.94 us
  local copies, waits for them, and re-layouts: 2.7 us -> 1.16 us
    pallas_call x12, Pallas kernels: 5.23 us -> 6.94 us  [run(): pl.pallas_call(skip(kernel, n, len(after)), out_shape=outs_t, in_specs=[p...]
    unnamed x6 -> x2, local copies, waits for them, and re-layouts: 2.63 us -> 1.09 us
  transfers between devices with their start and end apart: 25 -> 25, of which waited for: 14 -> 13; matrix products, arithmetic and copies ran while one was open for 0% -> 0% of each run, Pallas kernels for 1% -> 1%
where the time goes in v5:
time: 104 us; the launch traced here: 103 us
  starting transfers between devices  42.5 us (41%)
  blocking collectives  26.4 us (25%)
  waiting for transfers between devices  24.8 us (24%)
  Pallas kernels  6.94 us (7%)
  local copies, waits for them, and re-layouts  1.16 us (1%)
    ppermute x25, starting transfers between devices, shift(): lax.ppermute(value, axis, [(i, (i + by) % size) for i in range(size)])  42.5 us
    all_to_all x2, blocking collectives, shards(): total = lax.all_to_all(total, 'z', 0, 0, tiled=True)  26.4 us
    ppermute x25, waiting for transfers between devices, shift(): lax.ppermute(value, axis, [(i, (i + by) % size) for i in range(size)])  24.8 us
    pallas_call x12, Pallas kernels, run(): pl.pallas_call(skip(kernel, n, len(after)), out_shape=outs_t, in_specs=[p...  6.94 us
  transfers between devices with their start and end apart: 25, of which 13 were waited for; matrix products, arithmetic and copies ran while one was open for 0% of the time, Pallas kernels for 1%

profile of v5, /device:TPU:1, one launch (start us, length us, event | category | flops | bytes accessed | tf_op | source)
XLA Modules:
  0.0 102.5 jit_solution(15414607833695814003)
XLA Ops:
  0.6 1.9 %shard_map.58.refs_0_ = bf16[1808,128]{1,0:T(8,128)(2,1)} custom-call(bf16[384,384]{1,0:T(8,128)(2,1)} %refs_0_.1, bf16[144,112]{1,0:T(8,128)(2,1)} %refs_1_.1, bf16[128,512]{1,0:T(8,128)(2,1)} %refs_2_.1), custom_call_target="tpu_custom_call" | custom-call | bytes 921088 | tf_op jit(solution)/shard_map/pallas_call | solution.py:54
  2.5 3.4 %collective-permute-start.5 = (bf16[1808,128]{1,0:T(8,128)(2,1)}, bf16[1808,128]{1,0:T(8,128)(2,1)S(1)}, u32[]{:S(2)}, u32[]{:S(2)}) collective-permute-start(bf16[1808,128]{1,0:T(8,128)(2,1)} %shard_map.58.refs_0_), channel_id=1, source_target_pairs={{0,3},{1,0},{2,1},{3,2},{4,7},{5,4},{6,5},{7,6},{8,11},{9,8},{10,9... | collective-permute-start | bytes 1388552 | tf_op jit(solution)/shard_map/ppermute | solution.py:402
  5.9 1.1 %copy-done = bf16[1808,128]{1,0:T(8,128)(2,1)S(1)} copy-done((bf16[1808,128]{1,0:T(8,128)(2,1)S(1)}, bf16[1808,128]{1,0:T(8,128)(2,1)}, u32[]{:S(2)}) %copy-start) | copy-done | bytes 462872
  7.4 2.0 %collective-permute-start = (bf16[576,128]{1,0:T(8,128)(2,1)S(1)}, bf16[576,128]{1,0:T(8,128)(2,1)S(1)}, u32[]{:S(2)}, u32[]{:S(2)}) collective-permute-start(bf16[576,128]{1,0:T(8,128)(2,1)S(1)} %get-tuple-element.20), channel_id=1, source_target_pairs={{0,4},{4,0},{1,5},{5,1},{2,6},{6,2},{3,7},{7,3},{8,12},{12,8},{9,1... | collective-permute-start | bytes 442376 | tf_op jit(solution)/shard_map/ppermute | solution.py:402
  9.4 1.0 collective-permute-done.refs_1_
  10.9 2.6 %collective-permute-start.2 = (bf16[144,128]{1,0:T(8,128)(2,1)S(1)}, bf16[144,128]{1,0:T(8,128)(2,1)S(1)}, u32[]{:S(2)}, u32[]{:S(2)}) collective-permute-start(bf16[144,128]{1,0:T(8,128)(2,1)S(1)} %get-tuple-element.23), channel_id=1, source_target_pairs={{0,128},{64,192},{128,0},{192,64},{1,129},{65,193},{129,1},{193,65... | collective-permute-start | bytes 110600 | tf_op jit(solution)/shard_map/ppermute | solution.py:402
  13.5 1.1 %collective-permute-start.3 = (bf16[144,128]{1,0:T(8,128)(2,1)S(1)}, bf16[144,128]{1,0:T(8,128)(2,1)S(1)}, u32[]{:S(2)}, u32[]{:S(2)}) collective-permute-start(bf16[144,128]{1,0:T(8,128)(2,1)S(1)} %get-tuple-element.24), channel_id=1, source_target_pairs={{0,192},{64,0},{128,64},{192,128},{1,193},{65,1},{129,65},{193,129... | collective-permute-start | bytes 110600 | tf_op jit(solution)/shard_map/ppermute | solution.py:402
  15.3 1.7 %collective-permute-done.3.refs_3_ = bf16[144,128]{1,0:T(8,128)(2,1)S(1)} collective-permute-done((bf16[144,128]{1,0:T(8,128)(2,1)S(1)}, bf16[144,128]{1,0:T(8,128)(2,1)S(1)}, u32[]{:S(2)}, u32[]{:S(2)}) %collective-permute-start.3) | collective-permute-done | bytes 36896 | tf_op jit(solution)/shard_map/ppermute | solution.py:402
  17.0 1.5 %collective-permute-done.4.refs_1_.refs_9_ = bf16[1808,128]{1,0:T(8,128)(2,1)S(1)} collective-permute-done((bf16[1808,128]{1,0:T(8,128)(2,1)}, bf16[1808,128]{1,0:T(8,128)(2,1)S(1)}, u32[]{:S(2)}, u32[]{:S(2)}) %collective-permute-start.4) | collective-permute-done | bytes 462880 | tf_op jit(solution)/shard_map/ppermute | solution.py:402
  19.3 2.0 %collective-permute-start.6 = (bf16[1152,128]{1,0:T(8,128)(2,1)S(1)}, bf16[1152,128]{1,0:T(8,128)(2,1)S(1)}, u32[]{:S(2)}, u32[]{:S(2)}) collective-permute-start(bf16[1152,128]{1,0:T(8,128)(2,1)S(1)} %get-tuple-element.27), channel_id=1, source_target_pairs={{0,4},{4,0},{1,5},{5,1},{2,6},{6,2},{3,7},{7,3},{8,12},{12,8},{9,1... | collective-permute-start | bytes 884744 | tf_op jit(solution)/shard_map/ppermute | solution.py:402
  21.2 1.2 %collective-permute-done.6.refs_1_ = bf16[1152,128]{1,0:T(8,128)(2,1)S(1)} collective-permute-done((bf16[1152,128]{1,0:T(8,128)(2,1)S(1)}, bf16[1152,128]{1,0:T(8,128)(2,1)S(1)}, u32[]{:S(2)}, u32[]{:S(2)}) %collective-permute-start.6) | collective-permute-done | bytes 294944 | tf_op jit(solution)/shard_map/ppermute | solution.py:402
  22.5 1.4 %collective-permute-start.7 = (bf16[288,128]{1,0:T(8,128)(2,1)S(1)}, bf16[288,128]{1,0:T(8,128)(2,1)S(1)}, u32[]{:S(2)}, u32[]{:S(2)}) collective-permute-start(bf16[288,128]{1,0:T(8,128)(2,1)S(1)} %get-tuple-element.29), channel_id=1, source_target_pairs={{0,64},{64,128},{128,192},{192,0},{1,65},{65,129},{129,193},{193,1... | collective-permute-start | bytes 221192 | tf_op jit(solution)/shard_map/ppermute | solution.py:402
  23.9 2.6 %collective-permute-start.8 = (bf16[288,128]{1,0:T(8,128)(2,1)S(1)}, bf16[288,128]{1,0:T(8,128)(2,1)S(1)}, u32[]{:S(2)}, u32[]{:S(2)}) collective-permute-start(bf16[288,128]{1,0:T(8,128)(2,1)S(1)} %get-tuple-element.30), channel_id=1, source_target_pairs={{0,128},{64,192},{128,0},{192,64},{1,129},{65,193},{129,1},{193,65... | collective-permute-start | bytes 221192 | tf_op jit(solution)/shard_map/ppermute | solution.py:402
  26.5 1.1 %collective-permute-start.9 = (bf16[288,128]{1,0:T(8,128)(2,1)S(1)}, bf16[288,128]{1,0:T(8,128)(2,1)S(1)}, u32[]{:S(2)}, u32[]{:S(2)}) collective-permute-start(bf16[288,128]{1,0:T(8,128)(2,1)S(1)} %get-tuple-element.31), channel_id=1, source_target_pairs={{0,192},{64,0},{128,64},{192,128},{1,193},{65,1},{129,65},{193,129... | collective-permute-start | bytes 221192 | tf_op jit(solution)/shard_map/ppermute | solution.py:402
  27.6 2.2 %collective-permute-done.8.refs_3_ = bf16[288,128]{1,0:T(8,128)(2,1)S(1)} collective-permute-done((bf16[288,128]{1,0:T(8,128)(2,1)S(1)}, bf16[288,128]{1,0:T(8,128)(2,1)S(1)}, u32[]{:S(2)}, u32[]{:S(2)}) %collective-permute-start.8) | collective-permute-done | bytes 73760 | tf_op jit(solution)/shard_map/ppermute | solution.py:402
  30.1 16.0 %all_to_all.22 = bf16[8,64,128]{2,1,0:T(8,128)(2,1)S(1)} all-to-all(bf16[8,64,128]{2,1,0:T(8,128)(2,1)S(1)} %bitcast.6), channel_id=1, replica_groups=mesh['y'=4,'z'=8,'c'=2,'x'=4] {'z'}, dimensions={0} | all-to-all | bytes 262144 | tf_op jit(solution)/shard_map/all_to_all | solution.py:447
  46.1 10.4 %all_to_all.23 = bf16[8,64,128]{2,1,0:T(8,128)(2,1)S(1)} all-to-all(bf16[8,64,128]{2,1,0:T(8,128)(2,1)S(1)} %bitcast.8), channel_id=1, replica_groups=mesh['y'=4,'z'=8,'c'=2,'x'=4] {'z'}, dimensions={0} | all-to-all | bytes 262144 | tf_op jit(solution)/shard_map/all_to_all | solution.py:449
  58.1 1.9 %collective-permute-start.20 = (bf16[896,128]{1,0:T(8,128)(2,1)S(1)}, bf16[896,128]{1,0:T(8,128)(2,1)S(1)}, u32[]{:S(2)}, u32[]{:S(2)}) collective-permute-start(bf16[896,128]{1,0:T(8,128)(2,1)S(1)} %slice.27), channel_id=1, source_target_pairs={{0,3},{1,0},{2,1},{3,2},{4,7},{5,4},{6,5},{7,6},{8,11},{9,8},{10,9... | collective-permute-start | bytes 688136 | tf_op jit(solution)/shard_map/ppermute | solution.py:402
  60.0 1.4 %collective-permute-done.10.refs_1_ = bf16[192,128]{1,0:T(8,128)(2,1)S(1)} collective-permute-done((bf16[192,128]{1,0:T(8,128)(2,1)S(1)}, bf16[192,128]{1,0:T(8,128)(2,1)S(1)}, u32[]{:S(2)}, u32[]{:S(2)}) %collective-permute-start.10) | collective-permute-done | bytes 49184 | tf_op jit(solution)/shard_map/ppermute | solution.py:402
  61.4 2.8 %collective-permute-start.14 = (bf16[720,128]{1,0:T(8,128)(2,1)S(1)}, bf16[720,128]{1,0:T(8,128)(2,1)S(1)}, u32[]{:S(2)}, u32[]{:S(2)}) collective-permute-start(bf16[720,128]{1,0:T(8,128)(2,1)S(1)} %shard_map.66.refs_0_), channel_id=1, source_target_pairs={{0,192},{64,0},{128,64},{192,128},{1,193},{65,1},{129,65},{193,129... | collective-permute-start | bytes 552968 | tf_op jit(solution)/shard_map/ppermute | solution.py:402
  65.0 5.8 %collective-permute-start.15 = (bf16[720,128]{1,0:T(8,128)(2,1)S(1)}, bf16[720,128]{1,0:T(8,128)(2,1)S(1)}, u32[]{:S(2)}, u32[]{:S(2)}) collective-permute-start(bf16[720,128]{1,0:T(8,128)(2,1)S(1)} %shard_map.66.refs_0_), channel_id=1, source_target_pairs={{0,4},{4,0},{1,5},{5,1},{2,6},{6,2},{3,7},{7,3},{8,12},{12,8},{9,1... | collective-permute-start | bytes 552968 | tf_op jit(solution)/shard_map/ppermute | solution.py:402
  70.8 3.6 %collective-permute-start.18 = (bf16[720,128]{1,0:T(8,128)(2,1)S(1)}, bf16[720,128]{1,0:T(8,128)(2,1)S(1)}, u32[]{:S(2)}, u32[]{:S(2)}) collective-permute-start(bf16[720,128]{1,0:T(8,128)(2,1)S(1)} %collective-permute-done.14.refs_3_), channel_id=1, source_target_pairs={{0,4},{4,0},{1,5},{5,1},{2,6},{6,2},{3,7},{7,3},{8,12},{12,8},{9,1... | collective-permute-start | bytes 552968 | tf_op jit(solution)/shard_map/ppermute | solution.py:402
  74.4 2.1 %collective-permute-start.17 = (bf16[720,128]{1,0:T(8,128)(2,1)S(1)}, bf16[720,128]{1,0:T(8,128)(2,1)S(1)}, u32[]{:S(2)}, u32[]{:S(2)}) collective-permute-start(bf16[720,128]{1,0:T(8,128)(2,1)S(1)} %collective-permute-done.13.refs_2_), channel_id=1, source_target_pairs={{0,4},{4,0},{1,5},{5,1},{2,6},{6,2},{3,7},{7,3},{8,12},{12,8},{9,1... | collective-permute-start | bytes 552968 | tf_op jit(solution)/shard_map/ppermute | solution.py:402
  76.5 1.9 %collective-permute-start.16 = (bf16[720,128]{1,0:T(8,128)(2,1)S(1)}, bf16[720,128]{1,0:T(8,128)(2,1)S(1)}, u32[]{:S(2)}, u32[]{:S(2)}) collective-permute-start(bf16[720,128]{1,0:T(8,128)(2,1)S(1)} %collective-permute-done.12.refs_1_), channel_id=1, source_target_pairs={{0,4},{4,0},{1,5},{5,1},{2,6},{6,2},{3,7},{7,3},{8,12},{12,8},{9,1... | collective-permute-start | bytes 552968 | tf_op jit(solution)/shard_map/ppermute | solution.py:402
  78.4 1.0 %collective-permute-done.16.refs_5_ = bf16[720,128]{1,0:T(8,128)(2,1)S(1)} collective-permute-done((bf16[720,128]{1,0:T(8,128)(2,1)S(1)}, bf16[720,128]{1,0:T(8,128)(2,1)S(1)}, u32[]{:S(2)}, u32[]{:S(2)}) %collective-permute-start.16) | collective-permute-done | bytes 184352 | tf_op jit(solution)/shard_map/ppermute | solution.py:402
  79.4 1.5 %shard_map.67 = (bf16[5760,128]{1,0:T(8,128)(2,1)S(1)}, bf16[1808,128]{1,0:T(8,128)(2,1)S(1)}, f32[1808,128]{1,0:T(8,128)S(1)}) custom-call(bf16[720,128]{1,0:T(8,128)(2,1)S(1)} %shard_map.66.refs_0_, bf16[720,128]{1,0:T(8,128)(2,1)S(1)} %collective-permute-done.12.refs_1_, bf16[720,128]{1,0:T(8,128)(2,1)S(1)} %collective-permute-done.13.refs_2_, ...), custom_call_target="tpu_custom_call" | custom-call | flops 541327360 | bytes 6189056 | tf_op jit(solution)/shard_map/pallas_call | solution.py:54
  81.1 2.6 %collective-permute-start.22 = (bf16[1808,128]{1,0:T(8,128)(2,1)S(1)}, bf16[1808,128]{1,0:T(8,128)(2,1)S(1)}, u32[]{:S(2)}, u32[]{:S(2)}) collective-permute-start(bf16[1808,128]{1,0:T(8,128)(2,1)S(1)} %get-tuple-element.34.refs_2_), channel_id=1, source_target_pairs={{0,3},{1,0},{2,1},{3,2},{4,7},{5,4},{6,5},{7,6},{8,11},{9,8},{10,9... | collective-permute-start | bytes 1388552 | tf_op jit(solution)/shard_map/ppermute | solution.py:402
  83.7 10.4 %collective-permute-done.21.refs_3_ = bf16[1808,128]{1,0:T(8,128)(2,1)S(1)} collective-permute-done((bf16[1808,128]{1,0:T(8,128)(2,1)S(1)}, bf16[1808,128]{1,0:T(8,128)(2,1)S(1)}, u32[]{:S(2)}, u32[]{:S(2)}) %collective-permute-start.21) | collective-permute-done | bytes 462880 | tf_op jit(solution)/shard_map/ppermute | solution.py:402
  94.2 2.7 %collective-permute-start.24 = (bf16[896,128]{1,0:T(8,128)(2,1)S(1)}, bf16[896,128]{1,0:T(8,128)(2,1)S(1)}, u32[]{:S(2)}, u32[]{:S(2)}) collective-permute-start(bf16[896,128]{1,0:T(8,128)(2,1)S(1)} %slice.29), channel_id=1, source_target_pairs={{0,3},{1,0},{2,1},{3,2},{4,7},{5,4},{6,5},{7,6},{8,11},{9,8},{10,9... | collective-permute-start | bytes 688136 | tf_op jit(solution)/shard_map/ppermute | solution.py:402
  97.9 2.5 %collective-permute-done.24.refs_3_ = bf16[896,128]{1,0:T(8,128)(2,1)S(1)} collective-permute-done((bf16[896,128]{1,0:T(8,128)(2,1)S(1)}, bf16[896,128]{1,0:T(8,128)(2,1)S(1)}, u32[]{:S(2)}, u32[]{:S(2)}) %collective-permute-start.24) | collective-permute-done | bytes 229408 | tf_op jit(solution)/shard_map/ppermute | solution.py:402
  100.3 1.0 collective-permute-done.23.refs_2_
  101.3 1.2 %shard_map.69 = (bf16[384,384]{1,0:T(8,128)(2,1)}, bf16[144,112]{1,0:T(8,128)(2,1)}, bf16[128,512]{1,0:T(8,128)(2,1)}) custom-call(bf16[5760,128]{1,0:T(8,128)(2,1)S(1)} %get-tuple-element.32.refs_0_, f32[1808,128]{1,0:T(8,128)S(1)} %shard_map.68.refs_1_, bf16[912,128]{1,0:T(8,128)(2,1)S(1)} %collective-permute-done.23.refs_2_, ...), custom_call_target="tpu_custom_call" | custom-call | flops 135331840 | bytes 3321344 | tf_op jit(solution)/shard_map/pallas_call | solution.py:54
  (39 shorter events, 6.3 us)
Async XLA Ops:
  2.5 14.5 %collective-permute-start.5 = (bf16[1808,128]{1,0:T(8,128)(2,1)}, bf16[1808,128]{1,0:T(8,128)(2,1)S(1)}, u32[]{:S(2)}, u32[]{:S(2)}) collective-permute-start(bf16[1808,128]{1,0:T(8,128)(2,1)} %shard_map.58.refs_0_), channel_id=1, source_target_pairs={{0,3},{1,0},{2,1},{3,2},{4,7},{5,4},{6,5},{7,6},{8,11},{9,8},{10,9... | collective-permute-start | bytes 1388552 | tf_op jit(solution)/shard_map/ppermute | solution.py:402
  5.9 12.6 %collective-permute-start.4 = (bf16[1808,128]{1,0:T(8,128)(2,1)}, bf16[1808,128]{1,0:T(8,128)(2,1)S(1)}, u32[]{:S(2)}, u32[]{:S(2)}) collective-permute-start(bf16[1808,128]{1,0:T(8,128)(2,1)} %shard_map.58.refs_0_), channel_id=1, source_target_pairs={{0,1},{1,2},{2,3},{3,0},{4,5},{5,6},{6,7},{7,4},{8,9},{9,10},{10,1... | collective-permute-start | bytes 1388552 | tf_op jit(solution)/shard_map/ppermute | solution.py:402
  5.9 1.1 %copy-start = (bf16[1808,128]{1,0:T(8,128)(2,1)S(1)}, bf16[1808,128]{1,0:T(8,128)(2,1)}, u32[]{:S(2)}) copy-start(bf16[1808,128]{1,0:T(8,128)(2,1)} %shard_map.58.refs_0_) | copy-start | bytes 1388548
  7.4 3.0 %collective-permute-start = (bf16[576,128]{1,0:T(8,128)(2,1)S(1)}, bf16[576,128]{1,0:T(8,128)(2,1)S(1)}, u32[]{:S(2)}, u32[]{:S(2)}) collective-permute-start(bf16[576,128]{1,0:T(8,128)(2,1)S(1)} %get-tuple-element.20), channel_id=1, source_target_pairs={{0,4},{4,0},{1,5},{5,1},{2,6},{6,2},{3,7},{7,3},{8,12},{12,8},{9,1... | collective-permute-start | bytes 442376 | tf_op jit(solution)/shard_map/ppermute | solution.py:402
  10.5 4.4 %collective-permute-start.1 = (bf16[144,128]{1,0:T(8,128)(2,1)S(1)}, bf16[144,128]{1,0:T(8,128)(2,1)S(1)}, u32[]{:S(2)}, u32[]{:S(2)}) collective-permute-start(bf16[144,128]{1,0:T(8,128)(2,1)S(1)} %get-tuple-element.22), channel_id=1, source_target_pairs={{0,64},{64,128},{128,192},{192,0},{1,65},{65,129},{129,193},{193,1... | collective-permute-start | bytes 110600 | tf_op jit(solution)/shard_map/ppermute | solution.py:402
  10.9 4.4 %collective-permute-start.2 = (bf16[144,128]{1,0:T(8,128)(2,1)S(1)}, bf16[144,128]{1,0:T(8,128)(2,1)S(1)}, u32[]{:S(2)}, u32[]{:S(2)}) collective-permute-start(bf16[144,128]{1,0:T(8,128)(2,1)S(1)} %get-tuple-element.23), channel_id=1, source_target_pairs={{0,128},{64,192},{128,0},{192,64},{1,129},{65,193},{129,1},{193,65... | collective-permute-start | bytes 110600 | tf_op jit(solution)/shard_map/ppermute | solution.py:402
  13.5 3.4 %collective-permute-start.3 = (bf16[144,128]{1,0:T(8,128)(2,1)S(1)}, bf16[144,128]{1,0:T(8,128)(2,1)S(1)}, u32[]{:S(2)}, u32[]{:S(2)}) collective-permute-start(bf16[144,128]{1,0:T(8,128)(2,1)S(1)} %get-tuple-element.24), channel_id=1, source_target_pairs={{0,192},{64,0},{128,64},{192,128},{1,193},{65,1},{129,65},{193,129... | collective-permute-start | bytes 110600 | tf_op jit(solution)/shard_map/ppermute | solution.py:402
  19.3 3.2 %collective-permute-start.6 = (bf16[1152,128]{1,0:T(8,128)(2,1)S(1)}, bf16[1152,128]{1,0:T(8,128)(2,1)S(1)}, u32[]{:S(2)}, u32[]{:S(2)}) collective-permute-start(bf16[1152,128]{1,0:T(8,128)(2,1)S(1)} %get-tuple-element.27), channel_id=1, source_target_pairs={{0,4},{4,0},{1,5},{5,1},{2,6},{6,2},{3,7},{7,3},{8,12},{12,8},{9,1... | collective-permute-start | bytes 884744 | tf_op jit(solution)/shard_map/ppermute | solution.py:402
  22.5 5.1 %collective-permute-start.7 = (bf16[288,128]{1,0:T(8,128)(2,1)S(1)}, bf16[288,128]{1,0:T(8,128)(2,1)S(1)}, u32[]{:S(2)}, u32[]{:S(2)}) collective-permute-start(bf16[288,128]{1,0:T(8,128)(2,1)S(1)} %get-tuple-element.29), channel_id=1, source_target_pairs={{0,64},{64,128},{128,192},{192,0},{1,65},{65,129},{129,193},{193,1... | collective-permute-start | bytes 221192 | tf_op jit(solution)/shard_map/ppermute | solution.py:402
  23.9 5.9 %collective-permute-start.8 = (bf16[288,128]{1,0:T(8,128)(2,1)S(1)}, bf16[288,128]{1,0:T(8,128)(2,1)S(1)}, u32[]{:S(2)}, u32[]{:S(2)}) collective-permute-start(bf16[288,128]{1,0:T(8,128)(2,1)S(1)} %get-tuple-element.30), channel_id=1, source_target_pairs={{0,128},{64,192},{128,0},{192,64},{1,129},{65,193},{129,1},{193,65... | collective-permute-start | bytes 221192 | tf_op jit(solution)/shard_map/ppermute | solution.py:402
  26.5 3.5 %collective-permute-start.9 = (bf16[288,128]{1,0:T(8,128)(2,1)S(1)}, bf16[288,128]{1,0:T(8,128)(2,1)S(1)}, u32[]{:S(2)}, u32[]{:S(2)}) collective-permute-start(bf16[288,128]{1,0:T(8,128)(2,1)S(1)} %get-tuple-element.31), channel_id=1, source_target_pairs={{0,192},{64,0},{128,64},{192,128},{1,193},{65,1},{129,65},{193,129... | collective-permute-start | bytes 221192 | tf_op jit(solution)/shard_map/ppermute | solution.py:402
  56.5 3.5 %collective-permute-start.11 = (bf16[192,128]{1,0:T(8,128)(2,1)S(1)}, bf16[192,128]{1,0:T(8,128)(2,1)S(1)}, u32[]{:S(2)}, u32[]{:S(2)}) collective-permute-start(bf16[192,128]{1,0:T(8,128)(2,1)S(1)} %get-tuple-element.35), channel_id=1, source_target_pairs={{0,3},{1,0},{2,1},{3,2},{4,7},{5,4},{6,5},{7,6},{8,11},{9,8},{10,9... | collective-permute-start | bytes 147464 | tf_op jit(solution)/shard_map/ppermute | solution.py:402
  57.3 4.2 %collective-permute-start.10 = (bf16[192,128]{1,0:T(8,128)(2,1)S(1)}, bf16[192,128]{1,0:T(8,128)(2,1)S(1)}, u32[]{:S(2)}, u32[]{:S(2)}) collective-permute-start(bf16[192,128]{1,0:T(8,128)(2,1)S(1)} %get-tuple-element.36), channel_id=1, source_target_pairs={{0,1},{1,2},{2,3},{3,0},{4,5},{5,6},{6,7},{7,4},{8,9},{9,10},{10,1... | collective-permute-start | bytes 147464 | tf_op jit(solution)/shard_map/ppermute | solution.py:402
  58.1 6.9 %collective-permute-start.20 = (bf16[896,128]{1,0:T(8,128)(2,1)S(1)}, bf16[896,128]{1,0:T(8,128)(2,1)S(1)}, u32[]{:S(2)}, u32[]{:S(2)}) collective-permute-start(bf16[896,128]{1,0:T(8,128)(2,1)S(1)} %slice.27), channel_id=1, source_target_pairs={{0,3},{1,0},{2,1},{3,2},{4,7},{5,4},{6,5},{7,6},{8,11},{9,8},{10,9... | collective-permute-start | bytes 688136 | tf_op jit(solution)/shard_map/ppermute | solution.py:402
  61.4 9.4 %collective-permute-start.14 = (bf16[720,128]{1,0:T(8,128)(2,1)S(1)}, bf16[720,128]{1,0:T(8,128)(2,1)S(1)}, u32[]{:S(2)}, u32[]{:S(2)}) collective-permute-start(bf16[720,128]{1,0:T(8,128)(2,1)S(1)} %shard_map.66.refs_0_), channel_id=1, source_target_pairs={{0,192},{64,0},{128,64},{192,128},{1,193},{65,1},{129,65},{193,129... | collective-permute-start | bytes 552968 | tf_op jit(solution)/shard_map/ppermute | solution.py:402
  64.2 10.2 %collective-permute-start.13 = (bf16[720,128]{1,0:T(8,128)(2,1)S(1)}, bf16[720,128]{1,0:T(8,128)(2,1)S(1)}, u32[]{:S(2)}, u32[]{:S(2)}) collective-permute-start(bf16[720,128]{1,0:T(8,128)(2,1)S(1)} %shard_map.66.refs_0_), channel_id=1, source_target_pairs={{0,128},{64,192},{128,0},{192,64},{1,129},{65,193},{129,1},{193,65... | collective-permute-start | bytes 552968 | tf_op jit(solution)/shard_map/ppermute | solution.py:402
  64.7 11.8 %collective-permute-start.12 = (bf16[720,128]{1,0:T(8,128)(2,1)S(1)}, bf16[720,128]{1,0:T(8,128)(2,1)S(1)}, u32[]{:S(2)}, u32[]{:S(2)}) collective-permute-start(bf16[720,128]{1,0:T(8,128)(2,1)S(1)} %shard_map.66.refs_0_), channel_id=1, source_target_pairs={{0,64},{64,128},{128,192},{192,0},{1,65},{65,129},{129,193},{193,1... | collective-permute-start | bytes 552968 | tf_op jit(solution)/shard_map/ppermute | solution.py:402
  64.9 13.5 %collective-permute-start.19 = (bf16[912,128]{1,0:T(8,128)(2,1)S(1)}, bf16[912,128]{1,0:T(8,128)(2,1)S(1)}, u32[]{:S(2)}, u32[]{:S(2)}) collective-permute-start(bf16[912,128]{1,0:T(8,128)(2,1)S(1)} %slice.26), channel_id=1, source_target_pairs={{0,1},{1,2},{2,3},{3,0},{4,5},{5,6},{6,7},{7,4},{8,9},{9,10},{10,1... | collective-permute-start | bytes 700424 | tf_op jit(solution)/shard_map/ppermute | solution.py:402
  65.0 13.4 %collective-permute-start.15 = (bf16[720,128]{1,0:T(8,128)(2,1)S(1)}, bf16[720,128]{1,0:T(8,128)(2,1)S(1)}, u32[]{:S(2)}, u32[]{:S(2)}) collective-permute-start(bf16[720,128]{1,0:T(8,128)(2,1)S(1)} %shard_map.66.refs_0_), channel_id=1, source_target_pairs={{0,4},{4,0},{1,5},{5,1},{2,6},{6,2},{3,7},{7,3},{8,12},{12,8},{9,1... | collective-permute-start | bytes 552968 | tf_op jit(solution)/shard_map/ppermute | solution.py:402
  70.8 7.6 %collective-permute-start.18 = (bf16[720,128]{1,0:T(8,128)(2,1)S(1)}, bf16[720,128]{1,0:T(8,128)(2,1)S(1)}, u32[]{:S(2)}, u32[]{:S(2)}) collective-permute-start(bf16[720,128]{1,0:T(8,128)(2,1)S(1)} %collective-permute-done.14.refs_3_), channel_id=1, source_target_pairs={{0,4},{4,0},{1,5},{5,1},{2,6},{6,2},{3,7},{7,3},{8,12},{12,8},{9,1... | collective-permute-start | bytes 552968 | tf_op jit(solution)/shard_map/ppermute | solution.py:402
  74.4 4.0 %collective-permute-start.17 = (bf16[720,128]{1,0:T(8,128)(2,1)S(1)}, bf16[720,128]{1,0:T(8,128)(2,1)S(1)}, u32[]{:S(2)}, u32[]{:S(2)}) collective-permute-start(bf16[720,128]{1,0:T(8,128)(2,1)S(1)} %collective-permute-done.13.refs_2_), channel_id=1, source_target_pairs={{0,4},{4,0},{1,5},{5,1},{2,6},{6,2},{3,7},{7,3},{8,12},{12,8},{9,1... | collective-permute-start | bytes 552968 | tf_op jit(solution)/shard_map/ppermute | solution.py:402
  76.5 2.9 %collective-permute-start.16 = (bf16[720,128]{1,0:T(8,128)(2,1)S(1)}, bf16[720,128]{1,0:T(8,128)(2,1)S(1)}, u32[]{:S(2)}, u32[]{:S(2)}) collective-permute-start(bf16[720,128]{1,0:T(8,128)(2,1)S(1)} %collective-permute-done.12.refs_1_), channel_id=1, source_target_pairs={{0,4},{4,0},{1,5},{5,1},{2,6},{6,2},{3,7},{7,3},{8,12},{12,8},{9,1... | collective-permute-start | bytes 552968 | tf_op jit(solution)/shard_map/ppermute | solution.py:402
  80.9 13.1 %collective-permute-start.21 = (bf16[1808,128]{1,0:T(8,128)(2,1)S(1)}, bf16[1808,128]{1,0:T(8,128)(2,1)S(1)}, u32[]{:S(2)}, u32[]{:S(2)}) collective-permute-start(bf16[1808,128]{1,0:T(8,128)(2,1)S(1)} %get-tuple-element.34.refs_2_), channel_id=1, source_target_pairs={{0,1},{1,2},{2,3},{3,0},{4,5},{5,6},{6,7},{7,4},{8,9},{9,10},{10,1... | collective-permute-start | bytes 1388552 | tf_op jit(solution)/shard_map/ppermute | solution.py:402
  81.1 13.1 %collective-permute-start.22 = (bf16[1808,128]{1,0:T(8,128)(2,1)S(1)}, bf16[1808,128]{1,0:T(8,128)(2,1)S(1)}, u32[]{:S(2)}, u32[]{:S(2)}) collective-permute-start(bf16[1808,128]{1,0:T(8,128)(2,1)S(1)} %get-tuple-element.34.refs_2_), channel_id=1, source_target_pairs={{0,3},{1,0},{2,1},{3,2},{4,7},{5,4},{6,5},{7,6},{8,11},{9,8},{10,9... | collective-permute-start | bytes 1388552 | tf_op jit(solution)/shard_map/ppermute | solution.py:402
  94.1 7.3 %collective-permute-start.23 = (bf16[912,128]{1,0:T(8,128)(2,1)S(1)}, bf16[912,128]{1,0:T(8,128)(2,1)S(1)}, u32[]{:S(2)}, u32[]{:S(2)}) collective-permute-start(bf16[912,128]{1,0:T(8,128)(2,1)S(1)} %slice.28), channel_id=1, source_target_pairs={{0,1},{1,2},{2,3},{3,0},{4,5},{5,6},{6,7},{7,4},{8,9},{9,10},{10,1... | collective-permute-start | bytes 700424 | tf_op jit(solution)/shard_map/ppermute | solution.py:402
  94.2 6.2 %collective-permute-start.24 = (bf16[896,128]{1,0:T(8,128)(2,1)S(1)}, bf16[896,128]{1,0:T(8,128)(2,1)S(1)}, u32[]{:S(2)}, u32[]{:S(2)}) collective-permute-start(bf16[896,128]{1,0:T(8,128)(2,1)S(1)} %slice.29), channel_id=1, source_target_pairs={{0,3},{1,0},{2,1},{3,2},{4,7},{5,4},{6,5},{7,6},{8,11},{9,8},{10,9... | collective-permute-start | bytes 688136 | tf_op jit(solution)/shard_map/ppermute | solution.py:402

commit v6 on v5

--- a/solution.py
+++ b/solution.py
@@ -372,15 +372,15 @@
         for at, v in packed_parts(added(near, value)):
             to = slice(at, at + v.shape[0])
             first_b[to, :] = v.astype(bf16)
-            acc[to, :] = coef_a * refs[8][to, :].astype(f32) + coef_b * v
+            acc[to, :] = v
 
     far_product(gram, far, use)
 
 
-def second_near_kernel(gram, acc, own, left, right, total):
+def second_near_kernel(gram, acc, x, own, left, right, total):
     for at, v in packed_parts(near_product(gram, *blocks_of((own, left, right), 0))):
         to = slice(at, at + v.shape[0])
-        total[to, :] = acc[to, :] + coef_c * v
+        total[to, :] = (coef_a * x[to, :].astype(f32) + coef_b * acc[to, :]) + coef_c * v
 
 
 def second_far_kernel(factors, gram, total, o1, o2, step_q, step_d, step_u):
@@ -456,7 +456,9 @@
         flops,
     )(*gather_y(piece), *x)
     f = ring(first_b)
-    (total,) = call(second_near_kernel, [((XROWS, 128), f32)], 3 * flops // 4)(gram, acc, *f[0:3])
+    (total,) = call(second_near_kernel, [((XROWS, 128), f32)], 3 * flops // 4)(
+        gram, acc, x[0], *f[0:3]
+    )
     return tuple(
         call(
             functools.partial(second_far_kernel, factors),

time: 104 us -> 104 us (level)
  no operation moved by 1% of the time
where the time goes in v6:
time: 104 us; the launch traced here: 103 us
  starting transfers between devices  42.5 us (41%)
  blocking collectives  26.4 us (25%)
  waiting for transfers between devices  24.7 us (24%)
  Pallas kernels  6.94 us (7%)
  local copies, waits for them, and re-layouts  1.16 us (1%)
    ppermute x25, starting transfers between devices, shift(): lax.ppermute(value, axis, [(i, (i + by) % size) for i in range(size)])  42.5 us
    all_to_all x2, blocking collectives, shards(): total = lax.all_to_all(total, 'z', 0, 0, tiled=True)  26.4 us
    ppermute x25, waiting for transfers between devices, shift(): lax.ppermute(value, axis, [(i, (i + by) % size) for i in range(size)])  24.7 us
    pallas_call x12, Pallas kernels, run(): pl.pallas_call(skip(kernel, n, len(after)), out_shape=outs_t, in_specs=[p...  6.94 us
  transfers between devices with their start and end apart: 25, of which 13 were waited for; matrix products, arithmetic and copies ran while one was open for 0% of the time, Pallas kernels for 1%

profile of v6, /device:TPU:1, one launch (start us, length us, event | category | flops | bytes accessed | tf_op | source)
XLA Modules:
  0.0 102.5 jit_solution(280210197783840668)
XLA Ops:
  0.6 1.9 %shard_map.58.refs_0_ = bf16[1808,128]{1,0:T(8,128)(2,1)} custom-call(bf16[384,384]{1,0:T(8,128)(2,1)} %refs_0_.1, bf16[144,112]{1,0:T(8,128)(2,1)} %refs_1_.1, bf16[128,512]{1,0:T(8,128)(2,1)} %refs_2_.1), custom_call_target="tpu_custom_call" | custom-call | bytes 921088 | tf_op jit(solution)/shard_map/pallas_call | solution.py:54
  2.5 3.4 %collective-permute-start.5 = (bf16[1808,128]{1,0:T(8,128)(2,1)}, bf16[1808,128]{1,0:T(8,128)(2,1)S(1)}, u32[]{:S(2)}, u32[]{:S(2)}) collective-permute-start(bf16[1808,128]{1,0:T(8,128)(2,1)} %shard_map.58.refs_0_), channel_id=1, source_target_pairs={{0,3},{1,0},{2,1},{3,2},{4,7},{5,4},{6,5},{7,6},{8,11},{9,8},{10,9... | collective-permute-start | bytes 1388552 | tf_op jit(solution)/shard_map/ppermute | solution.py:402
  5.9 1.1 %copy-done = bf16[1808,128]{1,0:T(8,128)(2,1)S(1)} copy-done((bf16[1808,128]{1,0:T(8,128)(2,1)S(1)}, bf16[1808,128]{1,0:T(8,128)(2,1)}, u32[]{:S(2)}) %copy-start) | copy-done | bytes 462872
  7.4 2.0 %collective-permute-start = (bf16[576,128]{1,0:T(8,128)(2,1)S(1)}, bf16[576,128]{1,0:T(8,128)(2,1)S(1)}, u32[]{:S(2)}, u32[]{:S(2)}) collective-permute-start(bf16[576,128]{1,0:T(8,128)(2,1)S(1)} %get-tuple-element.20), channel_id=1, source_target_pairs={{0,4},{4,0},{1,5},{5,1},{2,6},{6,2},{3,7},{7,3},{8,12},{12,8},{9,1... | collective-permute-start | bytes 442376 | tf_op jit(solution)/shard_map/ppermute | solution.py:402
  9.4 1.0 collective-permute-done.refs_1_
  10.9 2.6 %collective-permute-start.2 = (bf16[144,128]{1,0:T(8,128)(2,1)S(1)}, bf16[144,128]{1,0:T(8,128)(2,1)S(1)}, u32[]{:S(2)}, u32[]{:S(2)}) collective-permute-start(bf16[144,128]{1,0:T(8,128)(2,1)S(1)} %get-tuple-element.23), channel_id=1, source_target_pairs={{0,128},{64,192},{128,0},{192,64},{1,129},{65,193},{129,1},{193,65... | collective-permute-start | bytes 110600 | tf_op jit(solution)/shard_map/ppermute | solution.py:402
  13.5 1.1 %collective-permute-start.3 = (bf16[144,128]{1,0:T(8,128)(2,1)S(1)}, bf16[144,128]{1,0:T(8,128)(2,1)S(1)}, u32[]{:S(2)}, u32[]{:S(2)}) collective-permute-start(bf16[144,128]{1,0:T(8,128)(2,1)S(1)} %get-tuple-element.24), channel_id=1, source_target_pairs={{0,192},{64,0},{128,64},{192,128},{1,193},{65,1},{129,65},{193,129... | collective-permute-start | bytes 110600 | tf_op jit(solution)/shard_map/ppermute | solution.py:402
  15.3 1.7 %collective-permute-done.3.refs_3_ = bf16[144,128]{1,0:T(8,128)(2,1)S(1)} collective-permute-done((bf16[144,128]{1,0:T(8,128)(2,1)S(1)}, bf16[144,128]{1,0:T(8,128)(2,1)S(1)}, u32[]{:S(2)}, u32[]{:S(2)}) %collective-permute-start.3) | collective-permute-done | bytes 36896 | tf_op jit(solution)/shard_map/ppermute | solution.py:402
  17.0 1.5 %collective-permute-done.4.refs_1_.refs_9_ = bf16[1808,128]{1,0:T(8,128)(2,1)S(1)} collective-permute-done((bf16[1808,128]{1,0:T(8,128)(2,1)}, bf16[1808,128]{1,0:T(8,128)(2,1)S(1)}, u32[]{:S(2)}, u32[]{:S(2)}) %collective-permute-start.4) | collective-permute-done | bytes 462880 | tf_op jit(solution)/shard_map/ppermute | solution.py:402
  19.3 2.0 %collective-permute-start.6 = (bf16[1152,128]{1,0:T(8,128)(2,1)S(1)}, bf16[1152,128]{1,0:T(8,128)(2,1)S(1)}, u32[]{:S(2)}, u32[]{:S(2)}) collective-permute-start(bf16[1152,128]{1,0:T(8,128)(2,1)S(1)} %get-tuple-element.27), channel_id=1, source_target_pairs={{0,4},{4,0},{1,5},{5,1},{2,6},{6,2},{3,7},{7,3},{8,12},{12,8},{9,1... | collective-permute-start | bytes 884744 | tf_op jit(solution)/shard_map/ppermute | solution.py:402
  21.2 1.2 %collective-permute-done.6.refs_1_ = bf16[1152,128]{1,0:T(8,128)(2,1)S(1)} collective-permute-done((bf16[1152,128]{1,0:T(8,128)(2,1)S(1)}, bf16[1152,128]{1,0:T(8,128)(2,1)S(1)}, u32[]{:S(2)}, u32[]{:S(2)}) %collective-permute-start.6) | collective-permute-done | bytes 294944 | tf_op jit(solution)/shard_map/ppermute | solution.py:402
  22.5 1.4 %collective-permute-start.7 = (bf16[288,128]{1,0:T(8,128)(2,1)S(1)}, bf16[288,128]{1,0:T(8,128)(2,1)S(1)}, u32[]{:S(2)}, u32[]{:S(2)}) collective-permute-start(bf16[288,128]{1,0:T(8,128)(2,1)S(1)} %get-tuple-element.29), channel_id=1, source_target_pairs={{0,64},{64,128},{128,192},{192,0},{1,65},{65,129},{129,193},{193,1... | collective-permute-start | bytes 221192 | tf_op jit(solution)/shard_map/ppermute | solution.py:402
  23.9 2.6 %collective-permute-start.8 = (bf16[288,128]{1,0:T(8,128)(2,1)S(1)}, bf16[288,128]{1,0:T(8,128)(2,1)S(1)}, u32[]{:S(2)}, u32[]{:S(2)}) collective-permute-start(bf16[288,128]{1,0:T(8,128)(2,1)S(1)} %get-tuple-element.30), channel_id=1, source_target_pairs={{0,128},{64,192},{128,0},{192,64},{1,129},{65,193},{129,1},{193,65... | collective-permute-start | bytes 221192 | tf_op jit(solution)/shard_map/ppermute | solution.py:402
  26.5 1.1 %collective-permute-start.9 = (bf16[288,128]{1,0:T(8,128)(2,1)S(1)}, bf16[288,128]{1,0:T(8,128)(2,1)S(1)}, u32[]{:S(2)}, u32[]{:S(2)}) collective-permute-start(bf16[288,128]{1,0:T(8,128)(2,1)S(1)} %get-tuple-element.31), channel_id=1, source_target_pairs={{0,192},{64,0},{128,64},{192,128},{1,193},{65,1},{129,65},{193,129... | collective-permute-start | bytes 221192 | tf_op jit(solution)/shard_map/ppermute | solution.py:402
  27.6 2.2 %collective-permute-done.8.refs_3_ = bf16[288,128]{1,0:T(8,128)(2,1)S(1)} collective-permute-done((bf16[288,128]{1,0:T(8,128)(2,1)S(1)}, bf16[288,128]{1,0:T(8,128)(2,1)S(1)}, u32[]{:S(2)}, u32[]{:S(2)}) %collective-permute-start.8) | collective-permute-done | bytes 73760 | tf_op jit(solution)/shard_map/ppermute | solution.py:402
  30.1 16.0 %all_to_all.22 = bf16[8,64,128]{2,1,0:T(8,128)(2,1)S(1)} all-to-all(bf16[8,64,128]{2,1,0:T(8,128)(2,1)S(1)} %bitcast.6), channel_id=1, replica_groups=mesh['y'=4,'z'=8,'c'=2,'x'=4] {'z'}, dimensions={0} | all-to-all | bytes 262144 | tf_op jit(solution)/shard_map/all_to_all | solution.py:447
  46.1 10.4 %all_to_all.23 = bf16[8,64,128]{2,1,0:T(8,128)(2,1)S(1)} all-to-all(bf16[8,64,128]{2,1,0:T(8,128)(2,1)S(1)} %bitcast.8), channel_id=1, replica_groups=mesh['y'=4,'z'=8,'c'=2,'x'=4] {'z'}, dimensions={0} | all-to-all | bytes 262144 | tf_op jit(solution)/shard_map/all_to_all | solution.py:449
  58.1 1.9 %collective-permute-start.20 = (bf16[896,128]{1,0:T(8,128)(2,1)S(1)}, bf16[896,128]{1,0:T(8,128)(2,1)S(1)}, u32[]{:S(2)}, u32[]{:S(2)}) collective-permute-start(bf16[896,128]{1,0:T(8,128)(2,1)S(1)} %slice.27), channel_id=1, source_target_pairs={{0,3},{1,0},{2,1},{3,2},{4,7},{5,4},{6,5},{7,6},{8,11},{9,8},{10,9... | collective-permute-start | bytes 688136 | tf_op jit(solution)/shard_map/ppermute | solution.py:402
  60.0 1.4 %collective-permute-done.10.refs_1_ = bf16[192,128]{1,0:T(8,128)(2,1)S(1)} collective-permute-done((bf16[192,128]{1,0:T(8,128)(2,1)S(1)}, bf16[192,128]{1,0:T(8,128)(2,1)S(1)}, u32[]{:S(2)}, u32[]{:S(2)}) %collective-permute-start.10) | collective-permute-done | bytes 49184 | tf_op jit(solution)/shard_map/ppermute | solution.py:402
  61.4 2.8 %collective-permute-start.14 = (bf16[720,128]{1,0:T(8,128)(2,1)S(1)}, bf16[720,128]{1,0:T(8,128)(2,1)S(1)}, u32[]{:S(2)}, u32[]{:S(2)}) collective-permute-start(bf16[720,128]{1,0:T(8,128)(2,1)S(1)} %shard_map.66.refs_0_), channel_id=1, source_target_pairs={{0,192},{64,0},{128,64},{192,128},{1,193},{65,1},{129,65},{193,129... | collective-permute-start | bytes 552968 | tf_op jit(solution)/shard_map/ppermute | solution.py:402
  65.0 5.8 %collective-permute-start.15 = (bf16[720,128]{1,0:T(8,128)(2,1)S(1)}, bf16[720,128]{1,0:T(8,128)(2,1)S(1)}, u32[]{:S(2)}, u32[]{:S(2)}) collective-permute-start(bf16[720,128]{1,0:T(8,128)(2,1)S(1)} %shard_map.66.refs_0_), channel_id=1, source_target_pairs={{0,4},{4,0},{1,5},{5,1},{2,6},{6,2},{3,7},{7,3},{8,12},{12,8},{9,1... | collective-permute-start | bytes 552968 | tf_op jit(solution)/shard_map/ppermute | solution.py:402
  70.8 3.6 %collective-permute-start.18 = (bf16[720,128]{1,0:T(8,128)(2,1)S(1)}, bf16[720,128]{1,0:T(8,128)(2,1)S(1)}, u32[]{:S(2)}, u32[]{:S(2)}) collective-permute-start(bf16[720,128]{1,0:T(8,128)(2,1)S(1)} %collective-permute-done.14.refs_3_), channel_id=1, source_target_pairs={{0,4},{4,0},{1,5},{5,1},{2,6},{6,2},{3,7},{7,3},{8,12},{12,8},{9,1... | collective-permute-start | bytes 552968 | tf_op jit(solution)/shard_map/ppermute | solution.py:402
  74.4 2.1 %collective-permute-start.17 = (bf16[720,128]{1,0:T(8,128)(2,1)S(1)}, bf16[720,128]{1,0:T(8,128)(2,1)S(1)}, u32[]{:S(2)}, u32[]{:S(2)}) collective-permute-start(bf16[720,128]{1,0:T(8,128)(2,1)S(1)} %collective-permute-done.13.refs_2_), channel_id=1, source_target_pairs={{0,4},{4,0},{1,5},{5,1},{2,6},{6,2},{3,7},{7,3},{8,12},{12,8},{9,1... | collective-permute-start | bytes 552968 | tf_op jit(solution)/shard_map/ppermute | solution.py:402
  76.5 1.9 %collective-permute-start.16 = (bf16[720,128]{1,0:T(8,128)(2,1)S(1)}, bf16[720,128]{1,0:T(8,128)(2,1)S(1)}, u32[]{:S(2)}, u32[]{:S(2)}) collective-permute-start(bf16[720,128]{1,0:T(8,128)(2,1)S(1)} %collective-permute-done.12.refs_1_), channel_id=1, source_target_pairs={{0,4},{4,0},{1,5},{5,1},{2,6},{6,2},{3,7},{7,3},{8,12},{12,8},{9,1... | collective-permute-start | bytes 552968 | tf_op jit(solution)/shard_map/ppermute | solution.py:402
  78.4 1.0 %collective-permute-done.16.refs_5_ = bf16[720,128]{1,0:T(8,128)(2,1)S(1)} collective-permute-done((bf16[720,128]{1,0:T(8,128)(2,1)S(1)}, bf16[720,128]{1,0:T(8,128)(2,1)S(1)}, u32[]{:S(2)}, u32[]{:S(2)}) %collective-permute-start.16) | collective-permute-done | bytes 184352 | tf_op jit(solution)/shard_map/ppermute | solution.py:402
  79.4 1.5 %shard_map.67 = (bf16[5760,128]{1,0:T(8,128)(2,1)S(1)}, bf16[1808,128]{1,0:T(8,128)(2,1)S(1)}, f32[1808,128]{1,0:T(8,128)S(1)}) custom-call(bf16[720,128]{1,0:T(8,128)(2,1)S(1)} %shard_map.66.refs_0_, bf16[720,128]{1,0:T(8,128)(2,1)S(1)} %collective-permute-done.12.refs_1_, bf16[720,128]{1,0:T(8,128)(2,1)S(1)} %collective-permute-done.13.refs_2_, ...), custom_call_target="tpu_custom_call" | custom-call | flops 541327360 | bytes 6189056 | tf_op jit(solution)/shard_map/pallas_call | solution.py:54
  81.0 2.6 %collective-permute-start.22 = (bf16[1808,128]{1,0:T(8,128)(2,1)S(1)}, bf16[1808,128]{1,0:T(8,128)(2,1)S(1)}, u32[]{:S(2)}, u32[]{:S(2)}) collective-permute-start(bf16[1808,128]{1,0:T(8,128)(2,1)S(1)} %get-tuple-element.34.refs_3_), channel_id=1, source_target_pairs={{0,3},{1,0},{2,1},{3,2},{4,7},{5,4},{6,5},{7,6},{8,11},{9,8},{10,9... | collective-permute-start | bytes 1388552 | tf_op jit(solution)/shard_map/ppermute | solution.py:402
  83.7 10.4 %collective-permute-done.21.refs_4_ = bf16[1808,128]{1,0:T(8,128)(2,1)S(1)} collective-permute-done((bf16[1808,128]{1,0:T(8,128)(2,1)S(1)}, bf16[1808,128]{1,0:T(8,128)(2,1)S(1)}, u32[]{:S(2)}, u32[]{:S(2)}) %collective-permute-start.21) | collective-permute-done | bytes 462880 | tf_op jit(solution)/shard_map/ppermute | solution.py:402
  94.2 2.7 %collective-permute-start.24 = (bf16[896,128]{1,0:T(8,128)(2,1)S(1)}, bf16[896,128]{1,0:T(8,128)(2,1)S(1)}, u32[]{:S(2)}, u32[]{:S(2)}) collective-permute-start(bf16[896,128]{1,0:T(8,128)(2,1)S(1)} %slice.29), channel_id=1, source_target_pairs={{0,3},{1,0},{2,1},{3,2},{4,7},{5,4},{6,5},{7,6},{8,11},{9,8},{10,9... | collective-permute-start | bytes 688136 | tf_op jit(solution)/shard_map/ppermute | solution.py:402
  97.9 2.4 %collective-permute-done.24.refs_3_ = bf16[896,128]{1,0:T(8,128)(2,1)S(1)} collective-permute-done((bf16[896,128]{1,0:T(8,128)(2,1)S(1)}, bf16[896,128]{1,0:T(8,128)(2,1)S(1)}, u32[]{:S(2)}, u32[]{:S(2)}) %collective-permute-start.24) | collective-permute-done | bytes 229408 | tf_op jit(solution)/shard_map/ppermute | solution.py:402
  100.3 1.0 collective-permute-done.23.refs_2_
  101.3 1.2 %shard_map.69 = (bf16[384,384]{1,0:T(8,128)(2,1)}, bf16[144,112]{1,0:T(8,128)(2,1)}, bf16[128,512]{1,0:T(8,128)(2,1)}) custom-call(bf16[5760,128]{1,0:T(8,128)(2,1)S(1)} %get-tuple-element.32.refs_0_, f32[1808,128]{1,0:T(8,128)S(1)} %shard_map.68.refs_1_, bf16[912,128]{1,0:T(8,128)(2,1)S(1)} %collective-permute-done.23.refs_2_, ...), custom_call_target="tpu_custom_call" | custom-call | flops 135331840 | bytes 3321344 | tf_op jit(solution)/shard_map/pallas_call | solution.py:54
  (39 shorter events, 6.4 us)
Async XLA Ops:
  2.5 14.5 %collective-permute-start.5 = (bf16[1808,128]{1,0:T(8,128)(2,1)}, bf16[1808,128]{1,0:T(8,128)(2,1)S(1)}, u32[]{:S(2)}, u32[]{:S(2)}) collective-permute-start(bf16[1808,128]{1,0:T(8,128)(2,1)} %shard_map.58.refs_0_), channel_id=1, source_target_pairs={{0,3},{1,0},{2,1},{3,2},{4,7},{5,4},{6,5},{7,6},{8,11},{9,8},{10,9... | collective-permute-start | bytes 1388552 | tf_op jit(solution)/shard_map/ppermute | solution.py:402
  5.9 12.6 %collective-permute-start.4 = (bf16[1808,128]{1,0:T(8,128)(2,1)}, bf16[1808,128]{1,0:T(8,128)(2,1)S(1)}, u32[]{:S(2)}, u32[]{:S(2)}) collective-permute-start(bf16[1808,128]{1,0:T(8,128)(2,1)} %shard_map.58.refs_0_), channel_id=1, source_target_pairs={{0,1},{1,2},{2,3},{3,0},{4,5},{5,6},{6,7},{7,4},{8,9},{9,10},{10,1... | collective-permute-start | bytes 1388552 | tf_op jit(solution)/shard_map/ppermute | solution.py:402
  5.9 1.1 %copy-start = (bf16[1808,128]{1,0:T(8,128)(2,1)S(1)}, bf16[1808,128]{1,0:T(8,128)(2,1)}, u32[]{:S(2)}) copy-start(bf16[1808,128]{1,0:T(8,128)(2,1)} %shard_map.58.refs_0_) | copy-start | bytes 1388548
  7.4 3.0 %collective-permute-start = (bf16[576,128]{1,0:T(8,128)(2,1)S(1)}, bf16[576,128]{1,0:T(8,128)(2,1)S(1)}, u32[]{:S(2)}, u32[]{:S(2)}) collective-permute-start(bf16[576,128]{1,0:T(8,128)(2,1)S(1)} %get-tuple-element.20), channel_id=1, source_target_pairs={{0,4},{4,0},{1,5},{5,1},{2,6},{6,2},{3,7},{7,3},{8,12},{12,8},{9,1... | collective-permute-start | bytes 442376 | tf_op jit(solution)/shard_map/ppermute | solution.py:402
  10.5 4.4 %collective-permute-start.1 = (bf16[144,128]{1,0:T(8,128)(2,1)S(1)}, bf16[144,128]{1,0:T(8,128)(2,1)S(1)}, u32[]{:S(2)}, u32[]{:S(2)}) collective-permute-start(bf16[144,128]{1,0:T(8,128)(2,1)S(1)} %get-tuple-element.22), channel_id=1, source_target_pairs={{0,64},{64,128},{128,192},{192,0},{1,65},{65,129},{129,193},{193,1... | collective-permute-start | bytes 110600 | tf_op jit(solution)/shard_map/ppermute | solution.py:402
  10.9 4.4 %collective-permute-start.2 = (bf16[144,128]{1,0:T(8,128)(2,1)S(1)}, bf16[144,128]{1,0:T(8,128)(2,1)S(1)}, u32[]{:S(2)}, u32[]{:S(2)}) collective-permute-start(bf16[144,128]{1,0:T(8,128)(2,1)S(1)} %get-tuple-element.23), channel_id=1, source_target_pairs={{0,128},{64,192},{128,0},{192,64},{1,129},{65,193},{129,1},{193,65... | collective-permute-start | bytes 110600 | tf_op jit(solution)/shard_map/ppermute | solution.py:402
  13.5 3.4 %collective-permute-start.3 = (bf16[144,128]{1,0:T(8,128)(2,1)S(1)}, bf16[144,128]{1,0:T(8,128)(2,1)S(1)}, u32[]{:S(2)}, u32[]{:S(2)}) collective-permute-start(bf16[144,128]{1,0:T(8,128)(2,1)S(1)} %get-tuple-element.24), channel_id=1, source_target_pairs={{0,192},{64,0},{128,64},{192,128},{1,193},{65,1},{129,65},{193,129... | collective-permute-start | bytes 110600 | tf_op jit(solution)/shard_map/ppermute | solution.py:402
  19.3 3.2 %collective-permute-start.6 = (bf16[1152,128]{1,0:T(8,128)(2,1)S(1)}, bf16[1152,128]{1,0:T(8,128)(2,1)S(1)}, u32[]{:S(2)}, u32[]{:S(2)}) collective-permute-start(bf16[1152,128]{1,0:T(8,128)(2,1)S(1)} %get-tuple-element.27), channel_id=1, source_target_pairs={{0,4},{4,0},{1,5},{5,1},{2,6},{6,2},{3,7},{7,3},{8,12},{12,8},{9,1... | collective-permute-start | bytes 884744 | tf_op jit(solution)/shard_map/ppermute | solution.py:402
  22.5 5.1 %collective-permute-start.7 = (bf16[288,128]{1,0:T(8,128)(2,1)S(1)}, bf16[288,128]{1,0:T(8,128)(2,1)S(1)}, u32[]{:S(2)}, u32[]{:S(2)}) collective-permute-start(bf16[288,128]{1,0:T(8,128)(2,1)S(1)} %get-tuple-element.29), channel_id=1, source_target_pairs={{0,64},{64,128},{128,192},{192,0},{1,65},{65,129},{129,193},{193,1... | collective-permute-start | bytes 221192 | tf_op jit(solution)/shard_map/ppermute | solution.py:402
  23.9 5.9 %collective-permute-start.8 = (bf16[288,128]{1,0:T(8,128)(2,1)S(1)}, bf16[288,128]{1,0:T(8,128)(2,1)S(1)}, u32[]{:S(2)}, u32[]{:S(2)}) collective-permute-start(bf16[288,128]{1,0:T(8,128)(2,1)S(1)} %get-tuple-element.30), channel_id=1, source_target_pairs={{0,128},{64,192},{128,0},{192,64},{1,129},{65,193},{129,1},{193,65... | collective-permute-start | bytes 221192 | tf_op jit(solution)/shard_map/ppermute | solution.py:402
  26.5 3.5 %collective-permute-start.9 = (bf16[288,128]{1,0:T(8,128)(2,1)S(1)}, bf16[288,128]{1,0:T(8,128)(2,1)S(1)}, u32[]{:S(2)}, u32[]{:S(2)}) collective-permute-start(bf16[288,128]{1,0:T(8,128)(2,1)S(1)} %get-tuple-element.31), channel_id=1, source_target_pairs={{0,192},{64,0},{128,64},{192,128},{1,193},{65,1},{129,65},{193,129... | collective-permute-start | bytes 221192 | tf_op jit(solution)/shard_map/ppermute | solution.py:402
  56.5 3.5 %collective-permute-start.11 = (bf16[192,128]{1,0:T(8,128)(2,1)S(1)}, bf16[192,128]{1,0:T(8,128)(2,1)S(1)}, u32[]{:S(2)}, u32[]{:S(2)}) collective-permute-start(bf16[192,128]{1,0:T(8,128)(2,1)S(1)} %get-tuple-element.35), channel_id=1, source_target_pairs={{0,3},{1,0},{2,1},{3,2},{4,7},{5,4},{6,5},{7,6},{8,11},{9,8},{10,9... | collective-permute-start | bytes 147464 | tf_op jit(solution)/shard_map/ppermute | solution.py:402
  57.3 4.2 %collective-permute-start.10 = (bf16[192,128]{1,0:T(8,128)(2,1)S(1)}, bf16[192,128]{1,0:T(8,128)(2,1)S(1)}, u32[]{:S(2)}, u32[]{:S(2)}) collective-permute-start(bf16[192,128]{1,0:T(8,128)(2,1)S(1)} %get-tuple-element.36), channel_id=1, source_target_pairs={{0,1},{1,2},{2,3},{3,0},{4,5},{5,6},{6,7},{7,4},{8,9},{9,10},{10,1... | collective-permute-start | bytes 147464 | tf_op jit(solution)/shard_map/ppermute | solution.py:402
  58.1 6.9 %collective-permute-start.20 = (bf16[896,128]{1,0:T(8,128)(2,1)S(1)}, bf16[896,128]{1,0:T(8,128)(2,1)S(1)}, u32[]{:S(2)}, u32[]{:S(2)}) collective-permute-start(bf16[896,128]{1,0:T(8,128)(2,1)S(1)} %slice.27), channel_id=1, source_target_pairs={{0,3},{1,0},{2,1},{3,2},{4,7},{5,4},{6,5},{7,6},{8,11},{9,8},{10,9... | collective-permute-start | bytes 688136 | tf_op jit(solution)/shard_map/ppermute | solution.py:402
  61.4 9.4 %collective-permute-start.14 = (bf16[720,128]{1,0:T(8,128)(2,1)S(1)}, bf16[720,128]{1,0:T(8,128)(2,1)S(1)}, u32[]{:S(2)}, u32[]{:S(2)}) collective-permute-start(bf16[720,128]{1,0:T(8,128)(2,1)S(1)} %shard_map.66.refs_0_), channel_id=1, source_target_pairs={{0,192},{64,0},{128,64},{192,128},{1,193},{65,1},{129,65},{193,129... | collective-permute-start | bytes 552968 | tf_op jit(solution)/shard_map/ppermute | solution.py:402
  64.2 10.2 %collective-permute-start.13 = (bf16[720,128]{1,0:T(8,128)(2,1)S(1)}, bf16[720,128]{1,0:T(8,128)(2,1)S(1)}, u32[]{:S(2)}, u32[]{:S(2)}) collective-permute-start(bf16[720,128]{1,0:T(8,128)(2,1)S(1)} %shard_map.66.refs_0_), channel_id=1, source_target_pairs={{0,128},{64,192},{128,0},{192,64},{1,129},{65,193},{129,1},{193,65... | collective-permute-start | bytes 552968 | tf_op jit(solution)/shard_map/ppermute | solution.py:402
  64.7 11.8 %collective-permute-start.12 = (bf16[720,128]{1,0:T(8,128)(2,1)S(1)}, bf16[720,128]{1,0:T(8,128)(2,1)S(1)}, u32[]{:S(2)}, u32[]{:S(2)}) collective-permute-start(bf16[720,128]{1,0:T(8,128)(2,1)S(1)} %shard_map.66.refs_0_), channel_id=1, source_target_pairs={{0,64},{64,128},{128,192},{192,0},{1,65},{65,129},{129,193},{193,1... | collective-permute-start | bytes 552968 | tf_op jit(solution)/shard_map/ppermute | solution.py:402
  64.9 13.5 %collective-permute-start.19 = (bf16[912,128]{1,0:T(8,128)(2,1)S(1)}, bf16[912,128]{1,0:T(8,128)(2,1)S(1)}, u32[]{:S(2)}, u32[]{:S(2)}) collective-permute-start(bf16[912,128]{1,0:T(8,128)(2,1)S(1)} %slice.26), channel_id=1, source_target_pairs={{0,1},{1,2},{2,3},{3,0},{4,5},{5,6},{6,7},{7,4},{8,9},{9,10},{10,1... | collective-permute-start | bytes 700424 | tf_op jit(solution)/shard_map/ppermute | solution.py:402
  65.0 13.4 %collective-permute-start.15 = (bf16[720,128]{1,0:T(8,128)(2,1)S(1)}, bf16[720,128]{1,0:T(8,128)(2,1)S(1)}, u32[]{:S(2)}, u32[]{:S(2)}) collective-permute-start(bf16[720,128]{1,0:T(8,128)(2,1)S(1)} %shard_map.66.refs_0_), channel_id=1, source_target_pairs={{0,4},{4,0},{1,5},{5,1},{2,6},{6,2},{3,7},{7,3},{8,12},{12,8},{9,1... | collective-permute-start | bytes 552968 | tf_op jit(solution)/shard_map/ppermute | solution.py:402
  70.8 7.6 %collective-permute-start.18 = (bf16[720,128]{1,0:T(8,128)(2,1)S(1)}, bf16[720,128]{1,0:T(8,128)(2,1)S(1)}, u32[]{:S(2)}, u32[]{:S(2)}) collective-permute-start(bf16[720,128]{1,0:T(8,128)(2,1)S(1)} %collective-permute-done.14.refs_3_), channel_id=1, source_target_pairs={{0,4},{4,0},{1,5},{5,1},{2,6},{6,2},{3,7},{7,3},{8,12},{12,8},{9,1... | collective-permute-start | bytes 552968 | tf_op jit(solution)/shard_map/ppermute | solution.py:402
  74.4 4.0 %collective-permute-start.17 = (bf16[720,128]{1,0:T(8,128)(2,1)S(1)}, bf16[720,128]{1,0:T(8,128)(2,1)S(1)}, u32[]{:S(2)}, u32[]{:S(2)}) collective-permute-start(bf16[720,128]{1,0:T(8,128)(2,1)S(1)} %collective-permute-done.13.refs_2_), channel_id=1, source_target_pairs={{0,4},{4,0},{1,5},{5,1},{2,6},{6,2},{3,7},{7,3},{8,12},{12,8},{9,1... | collective-permute-start | bytes 552968 | tf_op jit(solution)/shard_map/ppermute | solution.py:402
  76.5 2.9 %collective-permute-start.16 = (bf16[720,128]{1,0:T(8,128)(2,1)S(1)}, bf16[720,128]{1,0:T(8,128)(2,1)S(1)}, u32[]{:S(2)}, u32[]{:S(2)}) collective-permute-start(bf16[720,128]{1,0:T(8,128)(2,1)S(1)} %collective-permute-done.12.refs_1_), channel_id=1, source_target_pairs={{0,4},{4,0},{1,5},{5,1},{2,6},{6,2},{3,7},{7,3},{8,12},{12,8},{9,1... | collective-permute-start | bytes 552968 | tf_op jit(solution)/shard_map/ppermute | solution.py:402
  80.9 13.1 %collective-permute-start.21 = (bf16[1808,128]{1,0:T(8,128)(2,1)S(1)}, bf16[1808,128]{1,0:T(8,128)(2,1)S(1)}, u32[]{:S(2)}, u32[]{:S(2)}) collective-permute-start(bf16[1808,128]{1,0:T(8,128)(2,1)S(1)} %get-tuple-element.34.refs_3_), channel_id=1, source_target_pairs={{0,1},{1,2},{2,3},{3,0},{4,5},{5,6},{6,7},{7,4},{8,9},{9,10},{10,1... | collective-permute-start | bytes 1388552 | tf_op jit(solution)/shard_map/ppermute | solution.py:402
  81.0 13.1 %collective-permute-start.22 = (bf16[1808,128]{1,0:T(8,128)(2,1)S(1)}, bf16[1808,128]{1,0:T(8,128)(2,1)S(1)}, u32[]{:S(2)}, u32[]{:S(2)}) collective-permute-start(bf16[1808,128]{1,0:T(8,128)(2,1)S(1)} %get-tuple-element.34.refs_3_), channel_id=1, source_target_pairs={{0,3},{1,0},{2,1},{3,2},{4,7},{5,4},{6,5},{7,6},{8,11},{9,8},{10,9... | collective-permute-start | bytes 1388552 | tf_op jit(solution)/shard_map/ppermute | solution.py:402
  94.0 7.3 %collective-permute-start.23 = (bf16[912,128]{1,0:T(8,128)(2,1)S(1)}, bf16[912,128]{1,0:T(8,128)(2,1)S(1)}, u32[]{:S(2)}, u32[]{:S(2)}) collective-permute-start(bf16[912,128]{1,0:T(8,128)(2,1)S(1)} %slice.28), channel_id=1, source_target_pairs={{0,1},{1,2},{2,3},{3,0},{4,5},{5,6},{6,7},{7,4},{8,9},{9,10},{10,1... | collective-permute-start | bytes 700424 | tf_op jit(solution)/shard_map/ppermute | solution.py:402
  94.2 6.1 %collective-permute-start.24 = (bf16[896,128]{1,0:T(8,128)(2,1)S(1)}, bf16[896,128]{1,0:T(8,128)(2,1)S(1)}, u32[]{:S(2)}, u32[]{:S(2)}) collective-permute-start(bf16[896,128]{1,0:T(8,128)(2,1)S(1)} %slice.29), channel_id=1, source_target_pairs={{0,3},{1,0},{2,1},{3,2},{4,7},{5,4},{6,5},{7,6},{8,11},{9,8},{10,9... | collective-permute-start | bytes 688136 | tf_op jit(solution)/shard_map/ppermute | solution.py:402

commit v7 on v6

--- a/solution.py
+++ b/solution.py
@@ -43,7 +43,7 @@
     return [pl.BlockSpec(memory_space=pltpu.VMEM)] * n
 
 
-def call(kernel, outs, flops=0, scratch=(), hbm=(), after=(), limit=40):
+def call(kernel, outs, flops=0, scratch=(), hbm=(), after=(), limit=40, out_hbm=False):
     def run(*args):
         n = len(args)
         args = (*args, *after)
@@ -58,7 +58,9 @@
                 pl.BlockSpec(memory_space=pltpu.HBM if i in hbm else pl.ANY if i >= n else pltpu.VMEM)
                 for i in range(len(args))
             ],
-            out_specs=tuple(vmem(len(outs))),
+            out_specs=tuple(
+                [pl.BlockSpec(memory_space=pl.ANY)] * len(outs) if out_hbm else vmem(len(outs))
+            ),
             scratch_shapes=list(scratch),
             cost_estimate=pl.CostEstimate(flops=flops, bytes_accessed=moved, transcendentals=0),
             compiler_params=pltpu.CompilerParams(vmem_limit_bytes=limit << 20),
@@ -383,17 +385,26 @@
         total[to, :] = (coef_a * x[to, :].astype(f32) + coef_b * acc[to, :]) + coef_c * v
 
 
-def second_far_kernel(factors, gram, total, o1, o2, step_q, step_d, step_u):
+def second_far_kernel(factors, gram, total, o1, o2, out_q, out_d, out_u, *scratch):
     fq, fd, fu = factors
+    step_q, step_d, step_u, sems = scratch
+    moves = [(step_q.at[:, 128 * k : 128 * (k + 1)], out_q.at[:, 128 * k : 128 * (k + 1)]) for k in range(3)]
+    moves += [(step_d, out_d), (step_u, out_u)]
+    copies = [pltpu.make_async_copy(a, b, sems.at[i]) for i, (a, b) in enumerate(moves)]
 
     def use(value):
         parts = packed_parts(value)
         done = [total[at : at + v.shape[0], :] + coef_c * v for at, v in parts]
         for k in range(3):
             step_q[:, 128 * k : 128 * (k + 1)] = (fq * done[k]).astype(bf16)
+            copies[k].start()
         step_d[...] = (fd * done[3]).astype(bf16)[:, 0:DC]
+        copies[3].start()
         for k in range(4):
             step_u[:, 128 * k : 128 * (k + 1)] = (fu * done[4 + k]).astype(bf16)
+        copies[4].start()
+        for copy in copies:
+            copy.wait()
 
     far_product(gram, (X1, (o1, o2)), use)
 
@@ -464,6 +475,13 @@
             functools.partial(second_far_kernel, factors),
             [((QR, QC), bf16), ((DR, DC), bf16), ((UR, UC), bf16)],
             flops // 4,
+            scratch=[
+                pltpu.VMEM((QR, QC), bf16),
+                pltpu.VMEM((DR, DC), bf16),
+                pltpu.VMEM((UR, UC), bf16),
+                pltpu.SemaphoreType.DMA((5,)),
+            ],
+            out_hbm=True,
         )(gram, total, *f[3:5])
     )
 

time: 104 us -> 104 us (level)
  no operation moved by 1% of the time
where the time goes in v7:
time: 104 us; the launch traced here: 103 us
  starting transfers between devices  42.5 us (41%)
  blocking collectives  26.4 us (25%)
  waiting for transfers between devices  24.7 us (24%)
  Pallas kernels  6.95 us (7%)
  local copies, waits for them, and re-layouts  1.16 us (1%)
    ppermute x25, starting transfers between devices, shift(): lax.ppermute(value, axis, [(i, (i + by) % size) for i in range(size)])  42.5 us
    all_to_all x2, blocking collectives, shards(): total = lax.all_to_all(total, 'z', 0, 0, tiled=True)  26.4 us
    ppermute x25, waiting for transfers between devices, shift(): lax.ppermute(value, axis, [(i, (i + by) % size) for i in range(size)])  24.7 us
    pallas_call x12, Pallas kernels, run(): pl.pallas_call(skip(kernel, n, len(after)), out_shape=outs_t, in_specs=[p...  6.95 us
  transfers between devices with their start and end apart: 25, of which 13 were waited for; matrix products, arithmetic and copies ran while one was open for 0% of the time, Pallas kernels for 1%

profile of v7, /device:TPU:1, one launch (start us, length us, event | category | flops | bytes accessed | tf_op | source)
XLA Modules:
  0.0 102.7 jit_solution(6901151917350668408)
XLA Ops:
  0.6 1.9 %shard_map.58.refs_0_ = bf16[1808,128]{1,0:T(8,128)(2,1)} custom-call(bf16[384,384]{1,0:T(8,128)(2,1)} %refs_0_.1, bf16[144,112]{1,0:T(8,128)(2,1)} %refs_1_.1, bf16[128,512]{1,0:T(8,128)(2,1)} %refs_2_.1), custom_call_target="tpu_custom_call" | custom-call | bytes 921088 | tf_op jit(solution)/shard_map/pallas_call | solution.py:54
  2.5 3.4 %collective-permute-start.5 = (bf16[1808,128]{1,0:T(8,128)(2,1)}, bf16[1808,128]{1,0:T(8,128)(2,1)S(1)}, u32[]{:S(2)}, u32[]{:S(2)}) collective-permute-start(bf16[1808,128]{1,0:T(8,128)(2,1)} %shard_map.58.refs_0_), channel_id=1, source_target_pairs={{0,3},{1,0},{2,1},{3,2},{4,7},{5,4},{6,5},{7,6},{8,11},{9,8},{10,9... | collective-permute-start | bytes 1388552 | tf_op jit(solution)/shard_map/ppermute | solution.py:413
  5.9 1.1 %copy-done = bf16[1808,128]{1,0:T(8,128)(2,1)S(1)} copy-done((bf16[1808,128]{1,0:T(8,128)(2,1)S(1)}, bf16[1808,128]{1,0:T(8,128)(2,1)}, u32[]{:S(2)}) %copy-start) | copy-done | bytes 462872
  7.4 2.0 %collective-permute-start = (bf16[576,128]{1,0:T(8,128)(2,1)S(1)}, bf16[576,128]{1,0:T(8,128)(2,1)S(1)}, u32[]{:S(2)}, u32[]{:S(2)}) collective-permute-start(bf16[576,128]{1,0:T(8,128)(2,1)S(1)} %get-tuple-element.20), channel_id=1, source_target_pairs={{0,4},{4,0},{1,5},{5,1},{2,6},{6,2},{3,7},{7,3},{8,12},{12,8},{9,1... | collective-permute-start | bytes 442376 | tf_op jit(solution)/shard_map/ppermute | solution.py:413
  9.4 1.0 collective-permute-done.refs_1_
  10.9 2.6 %collective-permute-start.2 = (bf16[144,128]{1,0:T(8,128)(2,1)S(1)}, bf16[144,128]{1,0:T(8,128)(2,1)S(1)}, u32[]{:S(2)}, u32[]{:S(2)}) collective-permute-start(bf16[144,128]{1,0:T(8,128)(2,1)S(1)} %get-tuple-element.23), channel_id=1, source_target_pairs={{0,128},{64,192},{128,0},{192,64},{1,129},{65,193},{129,1},{193,65... | collective-permute-start | bytes 110600 | tf_op jit(solution)/shard_map/ppermute | solution.py:413
  13.5 1.1 %collective-permute-start.3 = (bf16[144,128]{1,0:T(8,128)(2,1)S(1)}, bf16[144,128]{1,0:T(8,128)(2,1)S(1)}, u32[]{:S(2)}, u32[]{:S(2)}) collective-permute-start(bf16[144,128]{1,0:T(8,128)(2,1)S(1)} %get-tuple-element.24), channel_id=1, source_target_pairs={{0,192},{64,0},{128,64},{192,128},{1,193},{65,1},{129,65},{193,129... | collective-permute-start | bytes 110600 | tf_op jit(solution)/shard_map/ppermute | solution.py:413
  15.3 1.7 %collective-permute-done.3.refs_3_ = bf16[144,128]{1,0:T(8,128)(2,1)S(1)} collective-permute-done((bf16[144,128]{1,0:T(8,128)(2,1)S(1)}, bf16[144,128]{1,0:T(8,128)(2,1)S(1)}, u32[]{:S(2)}, u32[]{:S(2)}) %collective-permute-start.3) | collective-permute-done | bytes 36896 | tf_op jit(solution)/shard_map/ppermute | solution.py:413
  17.0 1.5 %collective-permute-done.4.refs_1_.refs_9_ = bf16[1808,128]{1,0:T(8,128)(2,1)S(1)} collective-permute-done((bf16[1808,128]{1,0:T(8,128)(2,1)}, bf16[1808,128]{1,0:T(8,128)(2,1)S(1)}, u32[]{:S(2)}, u32[]{:S(2)}) %collective-permute-start.4) | collective-permute-done | bytes 462880 | tf_op jit(solution)/shard_map/ppermute | solution.py:413
  19.3 2.0 %collective-permute-start.6 = (bf16[1152,128]{1,0:T(8,128)(2,1)S(1)}, bf16[1152,128]{1,0:T(8,128)(2,1)S(1)}, u32[]{:S(2)}, u32[]{:S(2)}) collective-permute-start(bf16[1152,128]{1,0:T(8,128)(2,1)S(1)} %get-tuple-element.27), channel_id=1, source_target_pairs={{0,4},{4,0},{1,5},{5,1},{2,6},{6,2},{3,7},{7,3},{8,12},{12,8},{9,1... | collective-permute-start | bytes 884744 | tf_op jit(solution)/shard_map/ppermute | solution.py:413
  21.2 1.2 %collective-permute-done.6.refs_1_ = bf16[1152,128]{1,0:T(8,128)(2,1)S(1)} collective-permute-done((bf16[1152,128]{1,0:T(8,128)(2,1)S(1)}, bf16[1152,128]{1,0:T(8,128)(2,1)S(1)}, u32[]{:S(2)}, u32[]{:S(2)}) %collective-permute-start.6) | collective-permute-done | bytes 294944 | tf_op jit(solution)/shard_map/ppermute | solution.py:413
  22.5 1.4 %collective-permute-start.7 = (bf16[288,128]{1,0:T(8,128)(2,1)S(1)}, bf16[288,128]{1,0:T(8,128)(2,1)S(1)}, u32[]{:S(2)}, u32[]{:S(2)}) collective-permute-start(bf16[288,128]{1,0:T(8,128)(2,1)S(1)} %get-tuple-element.29), channel_id=1, source_target_pairs={{0,64},{64,128},{128,192},{192,0},{1,65},{65,129},{129,193},{193,1... | collective-permute-start | bytes 221192 | tf_op jit(solution)/shard_map/ppermute | solution.py:413
  23.9 2.6 %collective-permute-start.8 = (bf16[288,128]{1,0:T(8,128)(2,1)S(1)}, bf16[288,128]{1,0:T(8,128)(2,1)S(1)}, u32[]{:S(2)}, u32[]{:S(2)}) collective-permute-start(bf16[288,128]{1,0:T(8,128)(2,1)S(1)} %get-tuple-element.30), channel_id=1, source_target_pairs={{0,128},{64,192},{128,0},{192,64},{1,129},{65,193},{129,1},{193,65... | collective-permute-start | bytes 221192 | tf_op jit(solution)/shard_map/ppermute | solution.py:413
  26.5 1.1 %collective-permute-start.9 = (bf16[288,128]{1,0:T(8,128)(2,1)S(1)}, bf16[288,128]{1,0:T(8,128)(2,1)S(1)}, u32[]{:S(2)}, u32[]{:S(2)}) collective-permute-start(bf16[288,128]{1,0:T(8,128)(2,1)S(1)} %get-tuple-element.31), channel_id=1, source_target_pairs={{0,192},{64,0},{128,64},{192,128},{1,193},{65,1},{129,65},{193,129... | collective-permute-start | bytes 221192 | tf_op jit(solution)/shard_map/ppermute | solution.py:413
  27.6 2.2 %collective-permute-done.8.refs_3_ = bf16[288,128]{1,0:T(8,128)(2,1)S(1)} collective-permute-done((bf16[288,128]{1,0:T(8,128)(2,1)S(1)}, bf16[288,128]{1,0:T(8,128)(2,1)S(1)}, u32[]{:S(2)}, u32[]{:S(2)}) %collective-permute-start.8) | collective-permute-done | bytes 73760 | tf_op jit(solution)/shard_map/ppermute | solution.py:413
  30.1 16.0 %all_to_all.22 = bf16[8,64,128]{2,1,0:T(8,128)(2,1)S(1)} all-to-all(bf16[8,64,128]{2,1,0:T(8,128)(2,1)S(1)} %bitcast.6), channel_id=1, replica_groups=mesh['y'=4,'z'=8,'c'=2,'x'=4] {'z'}, dimensions={0} | all-to-all | bytes 262144 | tf_op jit(solution)/shard_map/all_to_all | solution.py:458
  46.1 10.4 %all_to_all.23 = bf16[8,64,128]{2,1,0:T(8,128)(2,1)S(1)} all-to-all(bf16[8,64,128]{2,1,0:T(8,128)(2,1)S(1)} %bitcast.8), channel_id=1, replica_groups=mesh['y'=4,'z'=8,'c'=2,'x'=4] {'z'}, dimensions={0} | all-to-all | bytes 262144 | tf_op jit(solution)/shard_map/all_to_all | solution.py:460
  58.1 1.9 %collective-permute-start.20 = (bf16[896,128]{1,0:T(8,128)(2,1)S(1)}, bf16[896,128]{1,0:T(8,128)(2,1)S(1)}, u32[]{:S(2)}, u32[]{:S(2)}) collective-permute-start(bf16[896,128]{1,0:T(8,128)(2,1)S(1)} %slice.27), channel_id=1, source_target_pairs={{0,3},{1,0},{2,1},{3,2},{4,7},{5,4},{6,5},{7,6},{8,11},{9,8},{10,9... | collective-permute-start | bytes 688136 | tf_op jit(solution)/shard_map/ppermute | solution.py:413
  60.0 1.4 %collective-permute-done.10.refs_1_ = bf16[192,128]{1,0:T(8,128)(2,1)S(1)} collective-permute-done((bf16[192,128]{1,0:T(8,128)(2,1)S(1)}, bf16[192,128]{1,0:T(8,128)(2,1)S(1)}, u32[]{:S(2)}, u32[]{:S(2)}) %collective-permute-start.10) | collective-permute-done | bytes 49184 | tf_op jit(solution)/shard_map/ppermute | solution.py:413
  61.4 2.8 %collective-permute-start.14 = (bf16[720,128]{1,0:T(8,128)(2,1)S(1)}, bf16[720,128]{1,0:T(8,128)(2,1)S(1)}, u32[]{:S(2)}, u32[]{:S(2)}) collective-permute-start(bf16[720,128]{1,0:T(8,128)(2,1)S(1)} %shard_map.66.refs_0_), channel_id=1, source_target_pairs={{0,192},{64,0},{128,64},{192,128},{1,193},{65,1},{129,65},{193,129... | collective-permute-start | bytes 552968 | tf_op jit(solution)/shard_map/ppermute | solution.py:413
  65.0 5.8 %collective-permute-start.15 = (bf16[720,128]{1,0:T(8,128)(2,1)S(1)}, bf16[720,128]{1,0:T(8,128)(2,1)S(1)}, u32[]{:S(2)}, u32[]{:S(2)}) collective-permute-start(bf16[720,128]{1,0:T(8,128)(2,1)S(1)} %shard_map.66.refs_0_), channel_id=1, source_target_pairs={{0,4},{4,0},{1,5},{5,1},{2,6},{6,2},{3,7},{7,3},{8,12},{12,8},{9,1... | collective-permute-start | bytes 552968 | tf_op jit(solution)/shard_map/ppermute | solution.py:413
  70.8 3.6 %collective-permute-start.18 = (bf16[720,128]{1,0:T(8,128)(2,1)S(1)}, bf16[720,128]{1,0:T(8,128)(2,1)S(1)}, u32[]{:S(2)}, u32[]{:S(2)}) collective-permute-start(bf16[720,128]{1,0:T(8,128)(2,1)S(1)} %collective-permute-done.14.refs_3_), channel_id=1, source_target_pairs={{0,4},{4,0},{1,5},{5,1},{2,6},{6,2},{3,7},{7,3},{8,12},{12,8},{9,1... | collective-permute-start | bytes 552968 | tf_op jit(solution)/shard_map/ppermute | solution.py:413
  74.4 2.1 %collective-permute-start.17 = (bf16[720,128]{1,0:T(8,128)(2,1)S(1)}, bf16[720,128]{1,0:T(8,128)(2,1)S(1)}, u32[]{:S(2)}, u32[]{:S(2)}) collective-permute-start(bf16[720,128]{1,0:T(8,128)(2,1)S(1)} %collective-permute-done.13.refs_2_), channel_id=1, source_target_pairs={{0,4},{4,0},{1,5},{5,1},{2,6},{6,2},{3,7},{7,3},{8,12},{12,8},{9,1... | collective-permute-start | bytes 552968 | tf_op jit(solution)/shard_map/ppermute | solution.py:413
  76.5 1.9 %collective-permute-start.16 = (bf16[720,128]{1,0:T(8,128)(2,1)S(1)}, bf16[720,128]{1,0:T(8,128)(2,1)S(1)}, u32[]{:S(2)}, u32[]{:S(2)}) collective-permute-start(bf16[720,128]{1,0:T(8,128)(2,1)S(1)} %collective-permute-done.12.refs_1_), channel_id=1, source_target_pairs={{0,4},{4,0},{1,5},{5,1},{2,6},{6,2},{3,7},{7,3},{8,12},{12,8},{9,1... | collective-permute-start | bytes 552968 | tf_op jit(solution)/shard_map/ppermute | solution.py:413
  78.4 1.0 %collective-permute-done.16.refs_5_ = bf16[720,128]{1,0:T(8,128)(2,1)S(1)} collective-permute-done((bf16[720,128]{1,0:T(8,128)(2,1)S(1)}, bf16[720,128]{1,0:T(8,128)(2,1)S(1)}, u32[]{:S(2)}, u32[]{:S(2)}) %collective-permute-start.16) | collective-permute-done | bytes 184352 | tf_op jit(solution)/shard_map/ppermute | solution.py:413
  79.4 1.5 %shard_map.67 = (bf16[5760,128]{1,0:T(8,128)(2,1)S(1)}, bf16[1808,128]{1,0:T(8,128)(2,1)S(1)}, f32[1808,128]{1,0:T(8,128)S(1)}) custom-call(bf16[720,128]{1,0:T(8,128)(2,1)S(1)} %shard_map.66.refs_0_, bf16[720,128]{1,0:T(8,128)(2,1)S(1)} %collective-permute-done.12.refs_1_, bf16[720,128]{1,0:T(8,128)(2,1)S(1)} %collective-permute-done.13.refs_2_, ...), custom_call_target="tpu_custom_call" | custom-call | flops 541327360 | bytes 6189056 | tf_op jit(solution)/shard_map/pallas_call | solution.py:54
  81.0 2.6 %collective-permute-start.22 = (bf16[1808,128]{1,0:T(8,128)(2,1)S(1)}, bf16[1808,128]{1,0:T(8,128)(2,1)S(1)}, u32[]{:S(2)}, u32[]{:S(2)}) collective-permute-start(bf16[1808,128]{1,0:T(8,128)(2,1)S(1)} %get-tuple-element.34.refs_3_), channel_id=1, source_target_pairs={{0,3},{1,0},{2,1},{3,2},{4,7},{5,4},{6,5},{7,6},{8,11},{9,8},{10,9... | collective-permute-start | bytes 1388552 | tf_op jit(solution)/shard_map/ppermute | solution.py:413
  83.7 10.4 %collective-permute-done.21.refs_4_ = bf16[1808,128]{1,0:T(8,128)(2,1)S(1)} collective-permute-done((bf16[1808,128]{1,0:T(8,128)(2,1)S(1)}, bf16[1808,128]{1,0:T(8,128)(2,1)S(1)}, u32[]{:S(2)}, u32[]{:S(2)}) %collective-permute-start.21) | collective-permute-done | bytes 462880 | tf_op jit(solution)/shard_map/ppermute | solution.py:413
  94.2 2.7 %collective-permute-start.24 = (bf16[896,128]{1,0:T(8,128)(2,1)S(1)}, bf16[896,128]{1,0:T(8,128)(2,1)S(1)}, u32[]{:S(2)}, u32[]{:S(2)}) collective-permute-start(bf16[896,128]{1,0:T(8,128)(2,1)S(1)} %slice.29), channel_id=1, source_target_pairs={{0,3},{1,0},{2,1},{3,2},{4,7},{5,4},{6,5},{7,6},{8,11},{9,8},{10,9... | collective-permute-start | bytes 688136 | tf_op jit(solution)/shard_map/ppermute | solution.py:413
  97.9 2.4 %collective-permute-done.24.refs_3_ = bf16[896,128]{1,0:T(8,128)(2,1)S(1)} collective-permute-done((bf16[896,128]{1,0:T(8,128)(2,1)S(1)}, bf16[896,128]{1,0:T(8,128)(2,1)S(1)}, u32[]{:S(2)}, u32[]{:S(2)}) %collective-permute-start.24) | collective-permute-done | bytes 229408 | tf_op jit(solution)/shard_map/ppermute | solution.py:413
  100.3 1.0 collective-permute-done.23.refs_2_
  101.3 1.2 %shard_map.69 = (bf16[384,384]{1,0:T(8,128)(2,1)}, bf16[144,112]{1,0:T(8,128)(2,1)}, bf16[128,512]{1,0:T(8,128)(2,1)}) custom-call(bf16[5760,128]{1,0:T(8,128)(2,1)S(1)} %get-tuple-element.32.refs_0_, f32[1808,128]{1,0:T(8,128)S(1)} %shard_map.68.refs_1_, bf16[912,128]{1,0:T(8,128)(2,1)S(1)} %collective-permute-done.23.refs_2_, ...), custom_call_target="tpu_custom_call" | custom-call | flops 135331840 | bytes 3321344 | tf_op jit(solution)/shard_map/pallas_call | solution.py:54
  (39 shorter events, 6.4 us)
Async XLA Ops:
  2.5 14.5 %collective-permute-start.5 = (bf16[1808,128]{1,0:T(8,128)(2,1)}, bf16[1808,128]{1,0:T(8,128)(2,1)S(1)}, u32[]{:S(2)}, u32[]{:S(2)}) collective-permute-start(bf16[1808,128]{1,0:T(8,128)(2,1)} %shard_map.58.refs_0_), channel_id=1, source_target_pairs={{0,3},{1,0},{2,1},{3,2},{4,7},{5,4},{6,5},{7,6},{8,11},{9,8},{10,9... | collective-permute-start | bytes 1388552 | tf_op jit(solution)/shard_map/ppermute | solution.py:413
  5.9 12.6 %collective-permute-start.4 = (bf16[1808,128]{1,0:T(8,128)(2,1)}, bf16[1808,128]{1,0:T(8,128)(2,1)S(1)}, u32[]{:S(2)}, u32[]{:S(2)}) collective-permute-start(bf16[1808,128]{1,0:T(8,128)(2,1)} %shard_map.58.refs_0_), channel_id=1, source_target_pairs={{0,1},{1,2},{2,3},{3,0},{4,5},{5,6},{6,7},{7,4},{8,9},{9,10},{10,1... | collective-permute-start | bytes 1388552 | tf_op jit(solution)/shard_map/ppermute | solution.py:413
  5.9 1.1 %copy-start = (bf16[1808,128]{1,0:T(8,128)(2,1)S(1)}, bf16[1808,128]{1,0:T(8,128)(2,1)}, u32[]{:S(2)}) copy-start(bf16[1808,128]{1,0:T(8,128)(2,1)} %shard_map.58.refs_0_) | copy-start | bytes 1388548
  7.4 3.0 %collective-permute-start = (bf16[576,128]{1,0:T(8,128)(2,1)S(1)}, bf16[576,128]{1,0:T(8,128)(2,1)S(1)}, u32[]{:S(2)}, u32[]{:S(2)}) collective-permute-start(bf16[576,128]{1,0:T(8,128)(2,1)S(1)} %get-tuple-element.20), channel_id=1, source_target_pairs={{0,4},{4,0},{1,5},{5,1},{2,6},{6,2},{3,7},{7,3},{8,12},{12,8},{9,1... | collective-permute-start | bytes 442376 | tf_op jit(solution)/shard_map/ppermute | solution.py:413
  10.5 4.4 %collective-permute-start.1 = (bf16[144,128]{1,0:T(8,128)(2,1)S(1)}, bf16[144,128]{1,0:T(8,128)(2,1)S(1)}, u32[]{:S(2)}, u32[]{:S(2)}) collective-permute-start(bf16[144,128]{1,0:T(8,128)(2,1)S(1)} %get-tuple-element.22), channel_id=1, source_target_pairs={{0,64},{64,128},{128,192},{192,0},{1,65},{65,129},{129,193},{193,1... | collective-permute-start | bytes 110600 | tf_op jit(solution)/shard_map/ppermute | solution.py:413
  10.9 4.4 %collective-permute-start.2 = (bf16[144,128]{1,0:T(8,128)(2,1)S(1)}, bf16[144,128]{1,0:T(8,128)(2,1)S(1)}, u32[]{:S(2)}, u32[]{:S(2)}) collective-permute-start(bf16[144,128]{1,0:T(8,128)(2,1)S(1)} %get-tuple-element.23), channel_id=1, source_target_pairs={{0,128},{64,192},{128,0},{192,64},{1,129},{65,193},{129,1},{193,65... | collective-permute-start | bytes 110600 | tf_op jit(solution)/shard_map/ppermute | solution.py:413
  13.5 3.4 %collective-permute-start.3 = (bf16[144,128]{1,0:T(8,128)(2,1)S(1)}, bf16[144,128]{1,0:T(8,128)(2,1)S(1)}, u32[]{:S(2)}, u32[]{:S(2)}) collective-permute-start(bf16[144,128]{1,0:T(8,128)(2,1)S(1)} %get-tuple-element.24), channel_id=1, source_target_pairs={{0,192},{64,0},{128,64},{192,128},{1,193},{65,1},{129,65},{193,129... | collective-permute-start | bytes 110600 | tf_op jit(solution)/shard_map/ppermute | solution.py:413
  19.3 3.2 %collective-permute-start.6 = (bf16[1152,128]{1,0:T(8,128)(2,1)S(1)}, bf16[1152,128]{1,0:T(8,128)(2,1)S(1)}, u32[]{:S(2)}, u32[]{:S(2)}) collective-permute-start(bf16[1152,128]{1,0:T(8,128)(2,1)S(1)} %get-tuple-element.27), channel_id=1, source_target_pairs={{0,4},{4,0},{1,5},{5,1},{2,6},{6,2},{3,7},{7,3},{8,12},{12,8},{9,1... | collective-permute-start | bytes 884744 | tf_op jit(solution)/shard_map/ppermute | solution.py:413
  22.5 5.1 %collective-permute-start.7 = (bf16[288,128]{1,0:T(8,128)(2,1)S(1)}, bf16[288,128]{1,0:T(8,128)(2,1)S(1)}, u32[]{:S(2)}, u32[]{:S(2)}) collective-permute-start(bf16[288,128]{1,0:T(8,128)(2,1)S(1)} %get-tuple-element.29), channel_id=1, source_target_pairs={{0,64},{64,128},{128,192},{192,0},{1,65},{65,129},{129,193},{193,1... | collective-permute-start | bytes 221192 | tf_op jit(solution)/shard_map/ppermute | solution.py:413
  23.9 5.9 %collective-permute-start.8 = (bf16[288,128]{1,0:T(8,128)(2,1)S(1)}, bf16[288,128]{1,0:T(8,128)(2,1)S(1)}, u32[]{:S(2)}, u32[]{:S(2)}) collective-permute-start(bf16[288,128]{1,0:T(8,128)(2,1)S(1)} %get-tuple-element.30), channel_id=1, source_target_pairs={{0,128},{64,192},{128,0},{192,64},{1,129},{65,193},{129,1},{193,65... | collective-permute-start | bytes 221192 | tf_op jit(solution)/shard_map/ppermute | solution.py:413
  26.5 3.5 %collective-permute-start.9 = (bf16[288,128]{1,0:T(8,128)(2,1)S(1)}, bf16[288,128]{1,0:T(8,128)(2,1)S(1)}, u32[]{:S(2)}, u32[]{:S(2)}) collective-permute-start(bf16[288,128]{1,0:T(8,128)(2,1)S(1)} %get-tuple-element.31), channel_id=1, source_target_pairs={{0,192},{64,0},{128,64},{192,128},{1,193},{65,1},{129,65},{193,129... | collective-permute-start | bytes 221192 | tf_op jit(solution)/shard_map/ppermute | solution.py:413
  56.5 3.5 %collective-permute-start.11 = (bf16[192,128]{1,0:T(8,128)(2,1)S(1)}, bf16[192,128]{1,0:T(8,128)(2,1)S(1)}, u32[]{:S(2)}, u32[]{:S(2)}) collective-permute-start(bf16[192,128]{1,0:T(8,128)(2,1)S(1)} %get-tuple-element.35), channel_id=1, source_target_pairs={{0,3},{1,0},{2,1},{3,2},{4,7},{5,4},{6,5},{7,6},{8,11},{9,8},{10,9... | collective-permute-start | bytes 147464 | tf_op jit(solution)/shard_map/ppermute | solution.py:413
  57.3 4.2 %collective-permute-start.10 = (bf16[192,128]{1,0:T(8,128)(2,1)S(1)}, bf16[192,128]{1,0:T(8,128)(2,1)S(1)}, u32[]{:S(2)}, u32[]{:S(2)}) collective-permute-start(bf16[192,128]{1,0:T(8,128)(2,1)S(1)} %get-tuple-element.36), channel_id=1, source_target_pairs={{0,1},{1,2},{2,3},{3,0},{4,5},{5,6},{6,7},{7,4},{8,9},{9,10},{10,1... | collective-permute-start | bytes 147464 | tf_op jit(solution)/shard_map/ppermute | solution.py:413
  58.1 6.9 %collective-permute-start.20 = (bf16[896,128]{1,0:T(8,128)(2,1)S(1)}, bf16[896,128]{1,0:T(8,128)(2,1)S(1)}, u32[]{:S(2)}, u32[]{:S(2)}) collective-permute-start(bf16[896,128]{1,0:T(8,128)(2,1)S(1)} %slice.27), channel_id=1, source_target_pairs={{0,3},{1,0},{2,1},{3,2},{4,7},{5,4},{6,5},{7,6},{8,11},{9,8},{10,9... | collective-permute-start | bytes 688136 | tf_op jit(solution)/shard_map/ppermute | solution.py:413
  61.4 9.4 %collective-permute-start.14 = (bf16[720,128]{1,0:T(8,128)(2,1)S(1)}, bf16[720,128]{1,0:T(8,128)(2,1)S(1)}, u32[]{:S(2)}, u32[]{:S(2)}) collective-permute-start(bf16[720,128]{1,0:T(8,128)(2,1)S(1)} %shard_map.66.refs_0_), channel_id=1, source_target_pairs={{0,192},{64,0},{128,64},{192,128},{1,193},{65,1},{129,65},{193,129... | collective-permute-start | bytes 552968 | tf_op jit(solution)/shard_map/ppermute | solution.py:413
  64.2 10.2 %collective-permute-start.13 = (bf16[720,128]{1,0:T(8,128)(2,1)S(1)}, bf16[720,128]{1,0:T(8,128)(2,1)S(1)}, u32[]{:S(2)}, u32[]{:S(2)}) collective-permute-start(bf16[720,128]{1,0:T(8,128)(2,1)S(1)} %shard_map.66.refs_0_), channel_id=1, source_target_pairs={{0,128},{64,192},{128,0},{192,64},{1,129},{65,193},{129,1},{193,65... | collective-permute-start | bytes 552968 | tf_op jit(solution)/shard_map/ppermute | solution.py:413
  64.7 11.8 %collective-permute-start.12 = (bf16[720,128]{1,0:T(8,128)(2,1)S(1)}, bf16[720,128]{1,0:T(8,128)(2,1)S(1)}, u32[]{:S(2)}, u32[]{:S(2)}) collective-permute-start(bf16[720,128]{1,0:T(8,128)(2,1)S(1)} %shard_map.66.refs_0_), channel_id=1, source_target_pairs={{0,64},{64,128},{128,192},{192,0},{1,65},{65,129},{129,193},{193,1... | collective-permute-start | bytes 552968 | tf_op jit(solution)/shard_map/ppermute | solution.py:413
  64.9 13.5 %collective-permute-start.19 = (bf16[912,128]{1,0:T(8,128)(2,1)S(1)}, bf16[912,128]{1,0:T(8,128)(2,1)S(1)}, u32[]{:S(2)}, u32[]{:S(2)}) collective-permute-start(bf16[912,128]{1,0:T(8,128)(2,1)S(1)} %slice.26), channel_id=1, source_target_pairs={{0,1},{1,2},{2,3},{3,0},{4,5},{5,6},{6,7},{7,4},{8,9},{9,10},{10,1... | collective-permute-start | bytes 700424 | tf_op jit(solution)/shard_map/ppermute | solution.py:413
  65.0 13.4 %collective-permute-start.15 = (bf16[720,128]{1,0:T(8,128)(2,1)S(1)}, bf16[720,128]{1,0:T(8,128)(2,1)S(1)}, u32[]{:S(2)}, u32[]{:S(2)}) collective-permute-start(bf16[720,128]{1,0:T(8,128)(2,1)S(1)} %shard_map.66.refs_0_), channel_id=1, source_target_pairs={{0,4},{4,0},{1,5},{5,1},{2,6},{6,2},{3,7},{7,3},{8,12},{12,8},{9,1... | collective-permute-start | bytes 552968 | tf_op jit(solution)/shard_map/ppermute | solution.py:413
  70.8 7.6 %collective-permute-start.18 = (bf16[720,128]{1,0:T(8,128)(2,1)S(1)}, bf16[720,128]{1,0:T(8,128)(2,1)S(1)}, u32[]{:S(2)}, u32[]{:S(2)}) collective-permute-start(bf16[720,128]{1,0:T(8,128)(2,1)S(1)} %collective-permute-done.14.refs_3_), channel_id=1, source_target_pairs={{0,4},{4,0},{1,5},{5,1},{2,6},{6,2},{3,7},{7,3},{8,12},{12,8},{9,1... | collective-permute-start | bytes 552968 | tf_op jit(solution)/shard_map/ppermute | solution.py:413
  74.4 4.0 %collective-permute-start.17 = (bf16[720,128]{1,0:T(8,128)(2,1)S(1)}, bf16[720,128]{1,0:T(8,128)(2,1)S(1)}, u32[]{:S(2)}, u32[]{:S(2)}) collective-permute-start(bf16[720,128]{1,0:T(8,128)(2,1)S(1)} %collective-permute-done.13.refs_2_), channel_id=1, source_target_pairs={{0,4},{4,0},{1,5},{5,1},{2,6},{6,2},{3,7},{7,3},{8,12},{12,8},{9,1... | collective-permute-start | bytes 552968 | tf_op jit(solution)/shard_map/ppermute | solution.py:413
  76.5 2.9 %collective-permute-start.16 = (bf16[720,128]{1,0:T(8,128)(2,1)S(1)}, bf16[720,128]{1,0:T(8,128)(2,1)S(1)}, u32[]{:S(2)}, u32[]{:S(2)}) collective-permute-start(bf16[720,128]{1,0:T(8,128)(2,1)S(1)} %collective-permute-done.12.refs_1_), channel_id=1, source_target_pairs={{0,4},{4,0},{1,5},{5,1},{2,6},{6,2},{3,7},{7,3},{8,12},{12,8},{9,1... | collective-permute-start | bytes 552968 | tf_op jit(solution)/shard_map/ppermute | solution.py:413
  80.9 13.1 %collective-permute-start.21 = (bf16[1808,128]{1,0:T(8,128)(2,1)S(1)}, bf16[1808,128]{1,0:T(8,128)(2,1)S(1)}, u32[]{:S(2)}, u32[]{:S(2)}) collective-permute-start(bf16[1808,128]{1,0:T(8,128)(2,1)S(1)} %get-tuple-element.34.refs_3_), channel_id=1, source_target_pairs={{0,1},{1,2},{2,3},{3,0},{4,5},{5,6},{6,7},{7,4},{8,9},{9,10},{10,1... | collective-permute-start | bytes 1388552 | tf_op jit(solution)/shard_map/ppermute | solution.py:413
  81.0 13.1 %collective-permute-start.22 = (bf16[1808,128]{1,0:T(8,128)(2,1)S(1)}, bf16[1808,128]{1,0:T(8,128)(2,1)S(1)}, u32[]{:S(2)}, u32[]{:S(2)}) collective-permute-start(bf16[1808,128]{1,0:T(8,128)(2,1)S(1)} %get-tuple-element.34.refs_3_), channel_id=1, source_target_pairs={{0,3},{1,0},{2,1},{3,2},{4,7},{5,4},{6,5},{7,6},{8,11},{9,8},{10,9... | collective-permute-start | bytes 1388552 | tf_op jit(solution)/shard_map/ppermute | solution.py:413
  94.0 7.3 %collective-permute-start.23 = (bf16[912,128]{1,0:T(8,128)(2,1)S(1)}, bf16[912,128]{1,0:T(8,128)(2,1)S(1)}, u32[]{:S(2)}, u32[]{:S(2)}) collective-permute-start(bf16[912,128]{1,0:T(8,128)(2,1)S(1)} %slice.28), channel_id=1, source_target_pairs={{0,1},{1,2},{2,3},{3,0},{4,5},{5,6},{6,7},{7,4},{8,9},{9,10},{10,1... | collective-permute-start | bytes 700424 | tf_op jit(solution)/shard_map/ppermute | solution.py:413
  94.2 6.1 %collective-permute-start.24 = (bf16[896,128]{1,0:T(8,128)(2,1)S(1)}, bf16[896,128]{1,0:T(8,128)(2,1)S(1)}, u32[]{:S(2)}, u32[]{:S(2)}) collective-permute-start(bf16[896,128]{1,0:T(8,128)(2,1)S(1)} %slice.29), channel_id=1, source_target_pairs={{0,3},{1,0},{2,1},{3,2},{4,7},{5,4},{6,5},{7,6},{8,11},{9,8},{10,9... | collective-permute-start | bytes 688136 | tf_op jit(solution)/shard_map/ppermute | solution.py:413
